TPU v7x, 32 devices: a whole 2x2x4 slice. The times are simulated.
32 devices in a mesh: blk: 8 (over y, x, core), head: 4 (over z).
Axes of the slice: x: 2, y: 2, z: 4, core: 2. Of those that a mesh axis runs over, the one named last changes fastest.
Arguments:
- tokens: bfloat16 [2, 2048, 1024], P(None, ('blk', 'head')), may hold values from -6 to 6
- w_query: bfloat16 [1024, 1024], P('blk', 'head'), may hold values from -0.1875 to 0.1875
- w_key: bfloat16 [1024, 1024], P('blk', 'head'), may hold values from -0.1875 to 0.1875
- w_value: bfloat16 [1024, 1024], P('blk', 'head'), may hold values from -0.1875 to 0.1875
- w_out: bfloat16 [1024, 1024], P('head', 'blk'), may hold values from -6 to 6
- b_query: bfloat16 [1024], P(('blk', 'head')), may hold values from -3 to 3
- b_value: bfloat16 [1024], P(('blk', 'head')), may hold values from -3 to 3
- b_out: bfloat16 [1024], P(('blk', 'head')), may hold values from -2 to 2
- norm1_gain: bfloat16 [1024], P(('blk', 'head')), may hold values from 0.5 to 1.5
- norm1_shift: bfloat16 [1024], P(('blk', 'head')), may hold values from -2 to 2
- w_in: bfloat16 [1024, 4096], P('blk', 'head'), may hold values from -0.1875 to 0.1875
- w_back: bfloat16 [1024, 4096], P('blk', 'head'), may hold values from -0.09375 to 0.09375
- b_in: bfloat16 [4096], P(('blk', 'head')), may hold values from -3 to 3
- b_back: bfloat16 [1024], P(('blk', 'head')), may hold values from -2 to 2
- norm2_gain: bfloat16 [1024], P(('blk', 'head')), may hold values from 0.5 to 1.5
- norm2_shift: bfloat16 [1024], P(('blk', 'head')), may hold values from -2 to 2
- cotangent: bfloat16 [2, 2048, 1024], P(None, ('blk', 'head')), may hold values from -6 to 6
Outputs:
- output: bfloat16 [2, 2048, 1024], P(None, ('blk', 'head'))
- grad_tokens: bfloat16 [2, 2048, 1024], P(None, ('blk', 'head'))
- grad_w_query: float32 [1024, 1024], P('blk', 'head')
- grad_w_key: float32 [1024, 1024], P('blk', 'head')
- grad_w_value: float32 [1024, 1024], P('blk', 'head')
- grad_w_out: float32 [1024, 1024], P('head', 'blk')
- grad_b_query: float32 [1024], P(('blk', 'head'))
- grad_b_value: float32 [1024], P(('blk', 'head'))
- grad_b_out: float32 [1024], P(('blk', 'head'))
- grad_norm1_gain: float32 [1024], P(('blk', 'head'))
- grad_norm1_shift: float32 [1024], P(('blk', 'head'))
- grad_w_in: float32 [1024, 4096], P('blk', 'head')
- grad_w_back: float32 [1024, 4096], P('blk', 'head')
- grad_b_in: float32 [4096], P(('blk', 'head'))
- grad_b_back: float32 [1024], P(('blk', 'head'))
- grad_norm2_gain: float32 [1024], P(('blk', 'head'))
- grad_norm2_shift: float32 [1024], P(('blk', 'head'))
All inputs are finite; a program needn't handle non-finite values.
Results may differ from a plain program's by a relative error of at most 0.02.
Values may be sent and summed in bfloat16 or wider, within the bound.
A program may use at most 704 MiB of HBM per device.

v0:
```python
import jax
import jax.numpy as jnp
from jax import lax
from jax.sharding import PartitionSpec as P

HEAD_DIM = 64


NORM_EPS = 1e-05


def layer_norm(summed, gain, shift):
    centre = jnp.mean(summed, axis=-1, keepdims=True)
    centred = summed - centre
    spread = jnp.mean(centred * centred, axis=-1, keepdims=True)
    return centred * lax.rsqrt(spread + NORM_EPS) * gain + shift


def gelu_exact(inputs):
    return jax.nn.gelu(inputs, approximate=False)


def split_heads(packed):
    return packed.reshape(packed.shape[0], packed.shape[1], -1, HEAD_DIM)


def contract_rows(left, right):
    return lax.dot_general(
        left, right, (((0,), (0,)), ((), ())), preferred_element_type=jnp.float32
    )


def contract_cols(left, right):
    return lax.dot_general(
        left, right, (((1,), (1,)), ((), ())), preferred_element_type=jnp.float32
    )


def score_block(queries4, keys4):
    return jnp.einsum(
        "sqge,skge->sqgk", queries4, keys4, preferred_element_type=jnp.float32
    ) * HEAD_DIM ** (-0.5)


def score_grads(queries4, keys4, values4, grads4, log_sums, deltas):
    probs = jnp.exp(score_block(queries4, keys4) - log_sums[..., None])
    d_probs = jnp.einsum("sqge,skge->sqgk", grads4, values4, preferred_element_type=jnp.float32)
    d_scores = (probs * (d_probs - deltas[..., None])).astype(jnp.bfloat16)
    return (probs.astype(jnp.bfloat16), d_scores)


def token_rows(local):
    return lax.all_gather(local, "head", axis=1, tiled=True)


def token_partials(terms):
    return lax.psum_scatter(
        terms.astype(jnp.bfloat16), "head", scatter_dimension=1, tiled=True
    ).astype(jnp.float32)


def place_part(part, full_len, start):
    return lax.dynamic_update_slice_in_dim(jnp.zeros((full_len,), jnp.float32), part, start, 0)


def per_device(
    tokens,
    w_query,
    w_key,
    w_value,
    w_out,
    b_query,
    b_value,
    b_out,
    norm1_gain,
    norm1_shift,
    w_in,
    w_back,
    b_in,
    b_back,
    norm2_gain,
    norm2_shift,
    cotangent,
):
    f32 = jnp.float32
    bf16 = jnp.bfloat16
    score_scale = HEAD_DIM ** (-0.5)
    bq_full, bv_full, bo_full, gain_one, shift_one, bin_full, bback_full, gain_two, shift_two = (
        lax.all_gather(b_query, ("blk", "head"), axis=0, tiled=True),
        lax.all_gather(b_value, ("blk", "head"), axis=0, tiled=True),
        lax.all_gather(b_out, ("blk", "head"), axis=0, tiled=True),
        lax.all_gather(norm1_gain, ("blk", "head"), axis=0, tiled=True),
        lax.all_gather(norm1_shift, ("blk", "head"), axis=0, tiled=True),
        lax.all_gather(b_in, ("blk", "head"), axis=0, tiled=True),
        lax.all_gather(b_back, ("blk", "head"), axis=0, tiled=True),
        lax.all_gather(norm2_gain, ("blk", "head"), axis=0, tiled=True),
        lax.all_gather(norm2_shift, ("blk", "head"), axis=0, tiled=True),
    )
    attn_cols, out_rows, ffn_cols = (
        lax.all_gather(jnp.stack((w_query, w_key, w_value)), "blk", axis=1, tiled=True),
        lax.all_gather(w_out, "blk", axis=1, tiled=True),
        lax.all_gather(jnp.stack((w_in, w_back)), "blk", axis=1, tiled=True),
    )
    seq_count, local_len, model_dim = tokens.shape
    token_shape = (seq_count, local_len, model_dim)
    head_id = lax.axis_index("head")
    width_part = attn_cols.shape[2]
    bq_part = lax.dynamic_slice_in_dim(bq_full, head_id * width_part, width_part).astype(f32)
    bv_part = lax.dynamic_slice_in_dim(bv_full, head_id * width_part, width_part).astype(f32)
    wide_rows = token_rows(tokens)
    wide_len = wide_rows.shape[1]
    wide_flat = wide_rows.reshape(-1, model_dim)
    head_shape = (seq_count, wide_len, width_part)
    wide_shape = (seq_count, wide_len, model_dim)
    query_heads = (
        (jnp.dot(wide_flat, attn_cols[0], preferred_element_type=f32) + bq_part)
        .astype(bf16)
        .reshape(head_shape)
    )
    key_heads = (
        jnp.dot(wide_flat, attn_cols[1], preferred_element_type=f32)
        .astype(bf16)
        .reshape(head_shape)
    )
    value_heads = (
        (jnp.dot(wide_flat, attn_cols[2], preferred_element_type=f32) + bv_part)
        .astype(bf16)
        .reshape(head_shape)
    )
    query4 = split_heads(query_heads)
    key4 = split_heads(key_heads)
    value4 = split_heads(value_heads)
    stat_shape = query4.shape[:3]
    pieces = (
        lax.all_gather(key_heads, "blk", axis=1, tiled=True),
        lax.all_gather(value_heads, "blk", axis=1, tiled=True),
    )
    maxima = jnp.full(stat_shape, -1e30, f32)
    scores = score_block(query4, split_heads(pieces[0]))
    new_max = jnp.maximum(maxima, jnp.max(scores, axis=-1))
    weights = jnp.exp(scores - new_max[..., None])
    totals = jnp.sum(weights, axis=-1)
    summed = jnp.einsum(
        "sqgk,skge->sqge", weights.astype(bf16), split_heads(pieces[1]), preferred_element_type=f32
    )
    maxima, totals, summed = (new_max, totals, summed)
    log_sums = maxima + jnp.log(totals)
    attended4 = summed / totals[..., None]
    attended_heads = attended4.reshape(head_shape).astype(bf16)
    attended_flat = attended_heads.reshape(-1, width_part)
    branch_terms = jnp.dot(attended_flat, out_rows, preferred_element_type=f32).reshape(wide_shape)
    branch = token_partials(branch_terms).reshape(-1, model_dim) + bo_full.astype(f32)
    flat_rows = tokens.reshape(-1, model_dim)
    normed, norm1_pull = jax.vjp(
        layer_norm, flat_rows.astype(f32) + branch, gain_one.astype(f32), shift_one.astype(f32)
    )
    normed_low = normed.astype(bf16)
    ffn_full = lax.all_gather(ffn_cols, "head", axis=2, tiled=True)
    pre_act = jnp.dot(normed_low, ffn_full[0], preferred_element_type=f32) + bin_full.astype(f32)
    hidden_act, gelu_pull = jax.vjp(gelu_exact, pre_act)
    hidden_low = hidden_act.astype(bf16)
    ffn_out = contract_cols(hidden_low, ffn_full[1]) + bback_full.astype(f32)
    final, norm2_pull = jax.vjp(
        layer_norm, normed + ffn_out, gain_two.astype(f32), shift_two.astype(f32)
    )
    output = final.astype(bf16).reshape(token_shape)
    d_second, grad_norm2_gain, grad_norm2_shift = norm2_pull(
        cotangent.reshape(-1, model_dim).astype(f32)
    )
    d_ffn = d_second.astype(bf16)
    grad_b_back = jnp.sum(d_ffn.astype(f32), axis=0)
    grad_back_whole = contract_rows(d_ffn, hidden_low)
    d_hidden = jnp.dot(d_ffn, ffn_full[1], preferred_element_type=f32)
    d_pre = gelu_pull(d_hidden)[0].astype(bf16)
    grad_b_in = jnp.sum(d_pre.astype(f32), axis=0)
    grad_in_whole = contract_rows(normed_low, d_pre)
    ffn_grad_parts = lax.psum_scatter(
        jnp.stack((grad_in_whole, grad_back_whole)).astype(jnp.bfloat16),
        "head",
        scatter_dimension=2,
        tiled=True,
    ).astype(jnp.float32)
    d_normed = d_second + contract_cols(d_pre, ffn_full[0])
    d_first, grad_norm1_gain, grad_norm1_shift = norm1_pull(d_normed)
    d_branch = d_first.astype(bf16)
    grad_b_out = jnp.sum(d_branch.astype(f32), axis=0)
    wide_dbranch = token_rows(d_branch.reshape(token_shape)).reshape(-1, model_dim)
    grad_out_part = contract_rows(attended_flat, wide_dbranch)
    grad_heads = contract_cols(wide_dbranch, out_rows).astype(bf16).reshape(head_shape)
    grads4 = split_heads(grad_heads)
    deltas = jnp.sum(grads4.astype(f32) * attended4, axis=-1)
    row_stats = (
        lax.all_gather(log_sums, "blk", axis=1, tiled=True),
        lax.all_gather(deltas, "blk", axis=1, tiled=True),
    )
    pieces = (
        lax.all_gather(key_heads, "blk", axis=1, tiled=True),
        lax.all_gather(value_heads, "blk", axis=1, tiled=True),
        lax.all_gather(query_heads, "blk", axis=1, tiled=True),
        lax.all_gather(grad_heads, "blk", axis=1, tiled=True),
    )
    piece_keys = split_heads(pieces[0])
    piece_values = split_heads(pieces[1])
    piece_queries = split_heads(pieces[2])
    piece_grads = split_heads(pieces[3])
    piece_sums = row_stats[0]
    piece_deltas = row_stats[1]
    own_probs, own_scores = score_grads(query4, piece_keys, piece_values, grads4, log_sums, deltas)
    d_query = score_scale * jnp.einsum(
        "sqgk,skge->sqge", own_scores, piece_keys, preferred_element_type=f32
    )
    probs_low, d_scores = score_grads(
        piece_queries, key4, value4, piece_grads, piece_sums, piece_deltas
    )
    key_acc = score_scale * jnp.einsum(
        "sqgk,sqge->skge", d_scores, piece_queries, preferred_element_type=f32
    )
    value_acc = jnp.einsum("sqgk,sqge->skge", probs_low, piece_grads, preferred_element_type=f32)
    d_query_low = d_query.reshape(-1, width_part).astype(bf16)
    d_key_low = key_acc.reshape(-1, width_part).astype(bf16)
    d_value_low = value_acc.reshape(-1, width_part).astype(bf16)
    grad_b_query = place_part(
        jnp.sum(d_query_low.astype(f32), axis=0), model_dim, head_id * width_part
    )
    grad_b_value = place_part(
        jnp.sum(d_value_low.astype(f32), axis=0), model_dim, head_id * width_part
    )
    attn_grad_parts = jnp.stack(
        (
            contract_rows(wide_flat, d_query_low),
            contract_rows(wide_flat, d_key_low),
            contract_rows(wide_flat, d_value_low),
        )
    )
    token_terms = (
        contract_cols(d_query_low, attn_cols[0])
        + contract_cols(d_key_low, attn_cols[1])
        + contract_cols(d_value_low, attn_cols[2])
    )
    d_tokens = d_first + token_partials(token_terms.reshape(wide_shape)).reshape(-1, model_dim)
    grad_tokens = d_tokens.astype(bf16).reshape(token_shape)
    attn_sums, grad_w_out, ffn_sums = (
        lax.psum_scatter(attn_grad_parts, "blk", scatter_dimension=1, tiled=True),
        lax.psum_scatter(grad_out_part, "blk", scatter_dimension=1, tiled=True),
        lax.psum_scatter(ffn_grad_parts, "blk", scatter_dimension=1, tiled=True),
    )
    (
        grad_b_query,
        grad_b_value,
        grad_b_out,
        grad_norm1_gain,
        grad_norm1_shift,
        grad_b_in,
        grad_b_back,
        grad_norm2_gain,
        grad_norm2_shift,
    ) = (
        lax.psum_scatter(grad_b_query, ("blk", "head"), scatter_dimension=0, tiled=True),
        lax.psum_scatter(grad_b_value, ("blk", "head"), scatter_dimension=0, tiled=True),
        lax.psum_scatter(grad_b_out, ("blk", "head"), scatter_dimension=0, tiled=True),
        lax.psum_scatter(grad_norm1_gain, ("blk", "head"), scatter_dimension=0, tiled=True),
        lax.psum_scatter(grad_norm1_shift, ("blk", "head"), scatter_dimension=0, tiled=True),
        lax.psum_scatter(grad_b_in, ("blk", "head"), scatter_dimension=0, tiled=True),
        lax.psum_scatter(grad_b_back, ("blk", "head"), scatter_dimension=0, tiled=True),
        lax.psum_scatter(grad_norm2_gain, ("blk", "head"), scatter_dimension=0, tiled=True),
        lax.psum_scatter(grad_norm2_shift, ("blk", "head"), scatter_dimension=0, tiled=True),
    )
    return (
        output,
        grad_tokens,
        attn_sums[0],
        attn_sums[1],
        attn_sums[2],
        grad_w_out,
        grad_b_query,
        grad_b_value,
        grad_b_out,
        grad_norm1_gain,
        grad_norm1_shift,
        ffn_sums[0],
        ffn_sums[1],
        grad_b_in,
        grad_b_back,
        grad_norm2_gain,
        grad_norm2_shift,
    )


def solution(mesh):
    in_specs = (
        P(None, ("blk", "head"), None),
        P("blk", "head"),
        P("blk", "head"),
        P("blk", "head"),
        P("head", "blk"),
        P(("blk", "head")),
        P(("blk", "head")),
        P(("blk", "head")),
        P(("blk", "head")),
        P(("blk", "head")),
        P("blk", "head"),
        P("blk", "head"),
        P(("blk", "head")),
        P(("blk", "head")),
        P(("blk", "head")),
        P(("blk", "head")),
        P(None, ("blk", "head"), None),
    )
    out_specs = (
        P(None, ("blk", "head"), None),
        P(None, ("blk", "head"), None),
        P("blk", "head"),
        P("blk", "head"),
        P("blk", "head"),
        P("head", "blk"),
        P(("blk", "head")),
        P(("blk", "head")),
        P(("blk", "head")),
        P(("blk", "head")),
        P(("blk", "head")),
        P("blk", "head"),
        P("blk", "head"),
        P(("blk", "head")),
        P(("blk", "head")),
        P(("blk", "head")),
        P(("blk", "head")),
    )
    return jax.shard_map(
        per_device, mesh=mesh, in_specs=in_specs, out_specs=out_specs, check_vma=False
    )
```

profile of v0, /device:TPU:0, one launch (start us, length us, event | category | flops | bytes accessed | tf_op | source)
XLA Modules:
  0.0 1111.3 jit_solution(8364598492528295790)
XLA Ops:
  8.1 1.6 pad_maximum_fusion.3
  9.7 30.6 %all-gather.13.cloned.1.call-done = bf16[2,256,1024]{2,1,0:T(8,128)(2,1)} async-done(((bf16[2,64,1024]{2,1,0:T(8,128)(2,1)}), bf16[2,256,1024]{2,1,0:T(8,128)(2,1)}) %all-gather.13.cloned.1.call-update) | async-done | bytes 1048592 | tf_op jit(solution)/shard_map/all_gather | solution.py:53
  40.3 27.7 %all-gather.11.cloned.1.call-done = bf16[3,1024,256]{2,1,0:T(8,128)(2,1)} async-done(((bf16[3,128,256]{2,1,0:T(8,128)(2,1)}), bf16[3,1024,256]{2,1,0:T(8,128)(2,1)}) %all-gather.11.cloned.1.call-update) | async-done | bytes 1572880 | tf_op jit(solution)/shard_map/all_gather | solution.py:100
  68.0 2.0 fusion.59
  72.8 39.7 %all-reduce.18 = (bf16[1024]{0:T(1024)(128)(2,1)S(1)}, bf16[1024]{0:T(1024)(128)(2,1)S(1)}, bf16[1024]{0:T(1024)(128)(2,1)S(1)}, bf16[1024]{0:T(1024)(128)(2,1)S...) all-reduce(bf16[1024]{0:T(1024)(128)(2,1)S(1)} %dynamic-update-slic, ...), channel_id=1, replica_groups=mesh['blk'=8,'head'=4] {'blk','head'}, use_global_device_ids=true, to_apply=%add.4 | all-reduce | flops 8192 | bytes 32768
  113.1 0.8 reshape.243
  113.9 1.8 pad_maximum_fusion.2
  115.8 13.4 %all_gather.71 = bf16[256,1024]{1,0:T(8,128)(2,1)} all-gather(bf16[256,128]{1,0:T(8,128)(2,1)S(1)} %copy-done.26), channel_id=1, replica_groups=mesh['blk'=8,'head'=4] {'blk'}, dimensions={1}, use_global_device_ids=true | all-gather | bytes 589824 | tf_op jit(solution)/shard_map/all_gather | solution.py:101
  130.5 2.5 copy.68
  133.0 18.9 %all-gather.15.cloned.1.call-done = bf16[2,2048,256]{1,0,2:T(2,128)(2,1)} async-done(((bf16[2,256,256]{1,0,2:T(2,128)(2,1)}), bf16[2,2048,256]{1,0,2:T(2,128)(2,1)}) %all-gather.15.cloned.1.call-update) | async-done | bytes 2097168 | tf_op jit(solution)/shard_map/all_gather | solution.py:136
  151.8 2.5 copy.67
  154.3 8.5 bitcast_reduce_fusion
  162.8 8.5 fusion.7
  171.3 10.2 fusion.101
  181.5 1.4 convolution_convert_fusion
  183.0 7.9 all-gather.19.cloned.1.call-done
  191.6 75.8 %all-gather = bf16[32,1,128]{2,1,0:T(2,128)(2,1)S(1)} all-gather(bf16[1,1,128]{2,1,0:T(2,128)(2,1)S(1)} %bitcast.308), channel_id=1, replica_groups=mesh['blk'=8,'head'=4] {'blk','head'}, dimensions={0}, use_global_device_ids=true | all-gather | bytes 8448 | tf_op jit(solution)/shard_map/all_gather | solution.py:94
  267.4 1.1 fusion.92
  268.6 1.2 multiply_reduce_fusion.4
  269.9 1.1 add_convert_fusion.3
  271.0 1.1 fusion.77
  272.1 235.4 %all-gather.21.cloned.1.call-done = bf16[2,1024,4096]{2,1,0:T(8,128)(2,1)} async-done(((bf16[2,1024,1024]{2,1,0:T(8,128)(2,1)}), bf16[2,1024,4096]{2,1,0:T(8,128)(2,1)}) %all-gather.21.cloned.1.call-update) | async-done | bytes 16777232 | tf_op jit(solution)/shard_map/all_gather | solution.py:158
  507.5 8.2 multiply_convert_fusion
  515.8 3.0 fusion.102
  519.4 1.0 fusion.100
  520.5 7.0 convert_reduce_fusion
  527.5 3.6 multiply_reduce_fusion
  531.3 0.8 copy-done.5
  532.1 1.4 convert_reduce_fusion.3
  534.4 25.4 %all-gather.23.cloned.1.call-done = bf16[2,256,1024]{2,1,0:T(8,128)(2,1)} async-done(((bf16[2,64,1024]{2,1,0:T(8,128)(2,1)}), bf16[2,256,1024]{2,1,0:T(8,128)(2,1)}) %all-gather.23.cloned.1.call-update) | async-done | bytes 1048592 | tf_op jit(solution)/shard_map/all_gather | solution.py:53
  559.8 2.4 convolution_convert_fusion.1
  562.5 3.6 convert_bitcast_fusion
  566.2 2.4 convert_bitcast_fusion.1
  568.6 6.8 pad_maximum_fusion
  575.5 0.9 copy-done.18
  576.4 0.8 reshape_reshape.14
  577.9 19.8 %all-gather.25.cloned.1.call-done = bf16[2,2048,256]{1,0,2:T(2,128)(2,1)} async-done(((bf16[2,256,256]{1,0,2:T(2,128)(2,1)}), bf16[2,2048,256]{1,0,2:T(2,128)(2,1)}) %all-gather.25.cloned.1.call-update) | async-done | bytes 2097168 | tf_op jit(solution)/shard_map/all_gather | solution.py:199
  597.8 2.5 copy.77
  600.3 9.3 all_gather.83
  609.6 8.1 fusion.85
  617.7 2.0 reshape.283
  619.7 2.0 copy.73
  621.7 1.2 multiply_reduce_fusion.1
  622.8 14.0 %convert_reduce_fusion.5 = (f32[4,64]{1,0:T(4,128)}, bf16[2,256,4,64]{1,3,2,0:T(8,128)(2,1)}) fusion(bf16[2,2048,4,64]{1,3,2,0:T(8,128)(2,1)} %bitcast.279, f32[2,4,2048,256]{3,2,1,0:T(8,128)} %get-tuple-element.107, f32[2,256,4]{1,2,0:T(4,128)S(1)} %multiply_reduce_fusion.1, f32[2,256,4]{1,2,0:T(4,128)S(1)} %log_add_fusion, ...), kind=kOutput, calls=%fused_computation.104 | convolution fusion | flops 1095237376 | bytes 21513216 | tf_op jit(solution)/shard_map/sqgk,skge->sqge/dot_general | solution.py:209
  636.9 1.3 copy.76
  638.2 8.6 all_gather.85
  646.8 2.8 fusion.80
  649.7 4.0 copy.79
  653.6 13.7 %fusion.62 = bf16[2,256,4,64]{1,3,2,0:T(8,128)(2,1)} fusion(bf16[2,2048,4,64]{1,3,2,0:T(8,128)(2,1)S(1)} %bitcast.271, f32[2,4,256,2048]{3,2,1,0:T(8,128)} %fusion.85, f32[2,2048,4]{1,2,0:T(4,128)S(1)} %all_gather.85, f32[2,2048,4]{1,2,0:T(4,128)S(1)} %all_gather.83, bf16[2,2048,4,64]{1,3,2,0:T(8,128)(2,1)} %bitcast.280, ...), kind=kOutput, calls=%fused_computation.76 | convolution fusion | flops 1094975488 | bytes 21626880 | tf_op jit(solution)/shard_map/sqgk,sqge->skge/dot_general | solution.py:215
  667.3 1.2 copy.82
  668.6 9.7 convert_reduce_fusion.4
  679.8 1.5 add_convert_fusion
  682.9 1.9 pad_maximum_fusion.1
  684.9 226.0 %reduce-scatter.15.cloned.1.call-done = bf16[2,1024,1024]{2,1,0:T(8,128)(2,1)} async-done(((bf16[2,1024,4096]{2,1,0:T(8,128)(2,1)}), bf16[2,1024,1024]{2,1,0:T(8,128)(2,1)}) %reduce-scatter.15.cloned.1.call-update) | async-done | bytes 4194320 | tf_op jit(solution)/shard_map/reduce_scatter | solution.py:177
  911.0 6.5 convert_element_type.236
  917.6 1.1 copy-done.16
  918.7 1.4 convolution_bitcast_fusion
  920.8 41.9 %all-reduce.17 = (f32[1024]{0:T(1024)S(1)}, f32[1024]{0:T(1024)S(1)}, f32[1024]{0:T(1024)S(1)}, f32[1024]{0:T(1024)S(1)}, f32[1024]{0:T(1024)S(1)}, /*index=5*/f...) all-reduce(f32[1024]{0:T(1024)S(1)} %dynamic_update_slice.6, ...), channel_id=6, replica_groups=mesh['blk'=8,'head'=4] {'blk','head'}, use_global_device_ids=true, to_apply=%region_16.0.clone | all-reduce | flops 12288 | bytes 98304
  967.9 1.8 fusion.71
  969.7 20.2 %reduce-scatter.11.cloned.1.call-done = f32[3,128,256]{1,2,0:T(8,128)} async-done(((f32[3,1024,256]{1,2,0:T(8,128)}), f32[3,128,256]{1,2,0:T(8,128)}) %reduce-scatter.11.cloned.1.call-update) | async-done | bytes 393232 | tf_op jit(solution)/shard_map/reduce_scatter | solution.py:243
  989.9 1.1 slice_bitcast_fusion.27
  993.3 71.3 %reduce-scatter.17.cloned.1.call-done = f32[2,128,1024]{2,1,0:T(8,128)} async-done(((f32[2,1024,1024]{2,1,0:T(8,128)}), f32[2,128,1024]{2,1,0:T(8,128)}) %reduce-scatter.17.cloned.1.call-update) | async-done | bytes 1048592 | tf_op jit(solution)/shard_map/reduce_scatter | solution.py:245
  1064.6 2.3 slice_bitcast_fusion.16
  1066.9 37.7 %reduce-scatter.13.cloned.1.call-done = f32[256,128]{1,0:T(8,128)} async-done(((f32[256,1024]{1,0:T(8,128)}), f32[256,128]{1,0:T(8,128)}) %reduce-scatter.13.cloned.1.call-update) | async-done | bytes 131088 | tf_op jit(solution)/shard_map/reduce_scatter | solution.py:244
  (193 shorter events, 20.8 us)
Async XLA Ops:
  7.2 63.7 %copy-start.36 = (bf16[32]{0:T(256)(128)(2,1)S(1)}, bf16[32]{0:T(256)(128)(2,1)}, u32[]{:S(2)}) copy-start(bf16[32]{0:T(256)(128)(2,1)} %param.26) | copy-start | bytes 196
  7.2 64.0 %copy-start.37 = (bf16[32]{0:T(256)(128)(2,1)S(1)}, bf16[32]{0:T(256)(128)(2,1)}, u32[]{:S(2)}) copy-start(bf16[32]{0:T(256)(128)(2,1)} %param.25) | copy-start | bytes 196
  7.2 64.2 %copy-start.38 = (bf16[32]{0:T(256)(128)(2,1)S(1)}, bf16[32]{0:T(256)(128)(2,1)}, u32[]{:S(2)}) copy-start(bf16[32]{0:T(256)(128)(2,1)} %param.24) | copy-start | bytes 196
  7.2 64.4 %copy-start.39 = (bf16[32]{0:T(256)(128)(2,1)S(1)}, bf16[32]{0:T(256)(128)(2,1)}, u32[]{:S(2)}) copy-start(bf16[32]{0:T(256)(128)(2,1)} %param.23) | copy-start | bytes 196
  7.2 64.6 %copy-start.40 = (bf16[32]{0:T(256)(128)(2,1)S(1)}, bf16[32]{0:T(256)(128)(2,1)}, u32[]{:S(2)}) copy-start(bf16[32]{0:T(256)(128)(2,1)} %param.22) | copy-start | bytes 196
  7.2 64.9 %copy-start.41 = (bf16[32]{0:T(256)(128)(2,1)S(1)}, bf16[32]{0:T(256)(128)(2,1)}, u32[]{:S(2)}) copy-start(bf16[32]{0:T(256)(128)(2,1)} %param.30) | copy-start | bytes 196
  7.3 65.1 %copy-start.42 = (bf16[32]{0:T(256)(128)(2,1)S(1)}, bf16[32]{0:T(256)(128)(2,1)}, u32[]{:S(2)}) copy-start(bf16[32]{0:T(256)(128)(2,1)} %param.32) | copy-start | bytes 196
  7.3 65.3 %copy-start.43 = (bf16[32]{0:T(256)(128)(2,1)S(1)}, bf16[32]{0:T(256)(128)(2,1)}, u32[]{:S(2)}) copy-start(bf16[32]{0:T(256)(128)(2,1)} %param.31) | copy-start | bytes 196
  7.3 33.1 %all-gather.13.cloned.1.call-start = ((), (), s32[]{:S(2)}) async-start(), calls=%async_computation.7 | async-start | bytes 1310720 | tf_op jit(solution)/shard_map/all_gather | solution.py:53
  8.0 60.0 %all-gather.11.cloned.1.call-start = ((), (), s32[]{:S(2)}) async-start(), calls=%async_computation.6 | async-start | bytes 1769472 | tf_op jit(solution)/shard_map/all_gather | solution.py:100
  9.7 120.8 %all-gather.17.cloned.1.call-start = ((), (), s32[]{:S(2)}) async-start(), calls=%async_computation.9 | async-start | bytes 2359296 | tf_op jit(solution)/shard_map/all_gather | solution.py:135
  40.3 72.2 %copy-start = (bf16[2,256,1024]{2,1,0:T(8,128)(2,1)S(1)}, bf16[2,256,1024]{2,1,0:T(8,128)(2,1)}, u32[]{:S(2)}) copy-start(bf16[2,256,1024]{2,1,0:T(8,128)(2,1)} %all-gather.13.cloned.1.call-done) | copy-start | bytes 3145732
  68.0 44.5 %copy-start.13 = (bf16[3,1024,256]{2,1,0:T(8,128)(2,1)S(1)}, bf16[3,1024,256]{2,1,0:T(8,128)(2,1)}, u32[]{:S(2)}) copy-start(bf16[3,1024,256]{2,1,0:T(8,128)(2,1)} %all-gather.11.cloned.1.call-done) | copy-start | bytes 4718596
  70.0 45.7 %copy-start.17 = (bf16[512,256]{0,1:T(8,128)(2,1)}, bf16[512,256]{0,1:T(8,128)(2,1)S(1)}, u32[]{:S(2)}) copy-start(bf16[512,256]{0,1:T(8,128)(2,1)S(1)} %fusion.59) | copy-start | bytes 786436
  70.0 43.9 %copy-start.25 = (bf16[128,1024]{1,0:T(8,128)(2,1)S(1)}, bf16[128,1024]{1,0:T(8,128)(2,1)}, u32[]{:S(2)}) copy-start(bf16[128,1024]{1,0:T(8,128)(2,1)} %param.28) | copy-start | bytes 786436
  70.8 81.0 %all-gather.15.cloned.1.call-start = ((), (), s32[]{:S(2)}) async-start(), calls=%async_computation.8 | async-start | bytes 2359296 | tf_op jit(solution)/shard_map/all_gather | solution.py:136
  112.6 3.2 copy-start.26
  113.1 16.7 %copy-start.19 = (bf16[512,256]{0,1:T(8,128)(2,1)}, bf16[512,256]{0,1:T(8,128)(2,1)S(1)}, u32[]{:S(2)}) copy-start(bf16[512,256]{0,1:T(8,128)(2,1)S(1)} %fusion.61) | copy-start | bytes 786436
  113.9 77.0 %all-gather.19.cloned.1.call-start = ((), (), s32[]{:S(2)}) async-start(), calls=%async_computation.11 | async-start | bytes 4718592 | tf_op jit(solution)/shard_map/all_gather | solution.py:102
  115.8 151.6 %reduce-scatter.7.cloned.1.call-start = ((), (), s32[]{:S(2)}) async-start(), calls=%async_computation.10 | async-start | bytes 1310720 | tf_op jit(solution)/shard_map/reduce_scatter | solution.py:57
  129.8 0.7 copy-start.21
  133.0 21.4 %copy-start.1 = (bf16[2,2048,256]{1,2,0:T(8,128)(2,1)}, bf16[2,2048,256]{1,2,0:T(8,128)(2,1)S(1)}, u32[]{:S(2)}) copy-start(bf16[2,2048,256]{1,2,0:T(8,128)(2,1)S(1)} %copy.68) | copy-start | bytes 6291460
  154.3 17.0 %copy-start.3 = (bf16[2,2048,256]{1,2,0:T(8,128)(2,1)}, bf16[2,2048,256]{1,2,0:T(8,128)(2,1)S(1)}, u32[]{:S(2)}) copy-start(bf16[2,2048,256]{1,2,0:T(8,128)(2,1)S(1)} %copy.67) | copy-start | bytes 6291460
  171.3 10.2 copy-start.11
  182.9 324.6 %all-gather.21.cloned.1.call-start = ((), (), s32[]{:S(2)}) async-start(), calls=%async_computation.12 | async-start | bytes 20971520 | tf_op jit(solution)/shard_map/all_gather | solution.py:158
  190.9 0.7 copy-start.34
  190.9 76.5 %copy-start.4 = (bf16[2,64,1024]{2,1,0:T(8,128)(2,1)S(1)}, bf16[2,64,1024]{2,1,0:T(8,128)(2,1)}, u32[]{:S(2)}) copy-start(bf16[2,64,1024]{2,1,0:T(8,128)(2,1)} %param.17) | copy-start | bytes 786436
  190.9 368.9 %all-gather.23.cloned.1.call-start = ((), (), s32[]{:S(2)}) async-start(), calls=%async_computation.13 | async-start | bytes 1310720 | tf_op jit(solution)/shard_map/all_gather | solution.py:53
  507.5 8.3 copy-start.35
  515.8 3.1 copy-start.15
  515.8 3.2 copy-start.7
  527.5 3.6 copy-start.23
  531.0 2.5 copy-start.22
  531.3 0.8 copy-start.5
  531.3 34.8 %copy-start.32 = (f32[128]{0:T(128)}, f32[128]{0:T(128)S(1)}, u32[]{:S(2)}) copy-start(f32[128]{0:T(128)S(1)} %negate_multiply_fusion.1) | copy-start | bytes 1540
  533.5 64.2 %all-gather.25.cloned.1.call-start = ((), (), s32[]{:S(2)}) async-start(), calls=%async_computation.14 | async-start | bytes 2359296 | tf_op jit(solution)/shard_map/all_gather | solution.py:199
  534.4 115.3 %all-gather.27.cloned.1.call-start = ((), (), s32[]{:S(2)}) async-start(), calls=%async_computation.15 | async-start | bytes 2359296 | tf_op jit(solution)/shard_map/all_gather | solution.py:200
  562.2 3.9 copy-start.24
  562.2 348.8 %reduce-scatter.15.cloned.1.call-start = ((), (), s32[]{:S(2)}) async-start(), calls=%async_computation.19 | async-start | bytes 20971520 | tf_op jit(solution)/shard_map/reduce_scatter | solution.py:177
  575.4 0.9 copy-start.18
  575.4 1.7 copy-start.20
  575.4 392.5 %reduce-scatter.9.cloned.1.call-start = ((), (), s32[]{:S(2)}) async-start(), calls=%async_computation.16 | async-start | bytes 1310720 | tf_op jit(solution)/shard_map/reduce_scatter | solution.py:57
  597.8 11.8 %copy-start.12 = (bf16[2,256,4,64]{1,0,3,2:T(2,128)(2,1)S(1)}, bf16[2,256,4,64]{1,0,3,2:T(2,128)(2,1)}, u32[]{:S(2)}) copy-start(bf16[2,256,4,64]{1,0,3,2:T(2,128)(2,1)} %reshape_reshape.14) | copy-start | bytes 786436
  638.2 8.6 copy-start.9
  668.6 10.0 copy-start.14
  678.3 1.6 copy-start.2
  679.8 1.8 copy-start.10
  681.4 308.6 %reduce-scatter.11.cloned.1.call-start = ((), (), s32[]{:S(2)}) async-start(), calls=%async_computation.17 | async-start | bytes 3538944 | tf_op jit(solution)/shard_map/reduce_scatter | solution.py:243
  684.9 379.7 %reduce-scatter.17.cloned.1.call-start = ((), (), s32[]{:S(2)}) async-start(), calls=%async_computation.20 | async-start | bytes 9437184 | tf_op jit(solution)/shard_map/reduce_scatter | solution.py:245
  917.5 1.2 copy-start.16
  917.5 2.7 copy-start.8
  917.5 2.7 copy-start.31
  917.5 3.2 copy-start.27
  917.5 3.2 copy-start.28
  917.5 3.2 copy-start.29
  917.5 3.2 copy-start.30
  917.6 50.4 %copy-start.6 = (f32[128,1024]{1,0:T(8,128)S(1)}, f32[128,1024]{1,0:T(8,128)}, u32[]{:S(2)}) copy-start(f32[128,1024]{1,0:T(8,128)} %copy-done.5) | copy-start | bytes 1572868
  917.6 50.3 %copy-start.33 = (f32[128]{0:T(128)S(1)}, f32[128]{0:T(128)}, u32[]{:S(2)}) copy-start(f32[128]{0:T(128)} %copy-done.32) | copy-start | bytes 1540
  917.6 187.0 %reduce-scatter.13.cloned.1.call-start = ((), (), s32[]{:S(2)}) async-start(), calls=%async_computation.18 | async-start | bytes 1179648 | tf_op jit(solution)/shard_map/reduce_scatter | solution.py:244
Sparse Core Ops, SparseCore 0:
  9.7 30.6 all-gather.12
  42.8 25.1 all-gather.10
  71.0 36.8 all-gather.16
  114.0 37.7 all-gather.14
  154.1 36.7 all-gather.18
  193.0 27.2 reduce-scatter.6
  222.0 285.4 all-gather.20
  533.6 26.1 all-gather.22
  561.8 35.9 all-gather.24
  600.2 27.8 all-gather.26
  630.7 280.2 reduce-scatter.14
  913.1 28.0 reduce-scatter.8
  945.0 44.9 reduce-scatter.10
  993.3 71.2 reduce-scatter.16
  1068.5 35.9 reduce-scatter.12
where the time goes:
time: 1120 us; the launch traced here: 1110 us
  waiting for transfers between devices  722 us (64%)
  blocking collectives  189 us (17%)
  matrix products  106 us (9%)
  local copies, waits for them, and re-layouts  40.5 us (4%)
  other arithmetic  38 us (3%)
  between operations  14.8 us (1%)
    all_gather x1, waiting for transfers between devices, per_device(): ffn_full = lax.all_gather(ffn_cols, 'head', axis=2, tiled=True)  235 us
    reduce_scatter x1, waiting for transfers between devices, per_device(): lax.psum_scatter(jnp.stack((grad_in_whole, grad_back_whole)).astype(jnp.b...  226 us
    unnamed x2, blocking collectives  81.6 us
    all_gather x1, blocking collectives, per_device(): lax.all_gather(b_in, ('blk', 'head'), axis=0, tiled=True)  75.8 us
    reduce_scatter x1, waiting for transfers between devices, per_device(): lax.psum_scatter(ffn_grad_parts, 'blk', scatter_dimension=1, tiled=True)  71.3 us
    all_gather x2, waiting for transfers between devices, token_rows(): return lax.all_gather(local, 'head', axis=1, tiled=True)  56 us
    reduce_scatter x1, waiting for transfers between devices, per_device(): lax.psum_scatter(grad_out_part, 'blk', scatter_dimension=1, tiled=True)  37.7 us
    all_gather x1, waiting for transfers between devices, per_device(): lax.all_gather(jnp.stack((w_query, w_key, w_value)), 'blk', axis=1, tiled...  27.7 us
  transfers between devices with their start and end apart: 15, of which 11 were waited for; matrix products, arithmetic and copies ran while one was open for 14% of the time, Pallas kernels for 0%

commit v1 on v0

--- a/solution.py
+++ b/solution.py
@@ -1,6 +1,11 @@
+import functools
+import math
+
 import jax
 import jax.numpy as jnp
 from jax import lax
+from jax.experimental import pallas as pl
+from jax.experimental.pallas import tpu as pltpu
 from jax.sharding import PartitionSpec as P
 
 HEAD_DIM = 64
@@ -286,6 +291,637 @@
     )
 
 
+MESH = pl.DeviceIdType.MESH
+F32 = jnp.float32
+BF16 = jnp.bfloat16
+VMEM_LIMIT = 60 * 2**20
+
+
+def dot_nn(left, right):
+    return jnp.dot(left, right, preferred_element_type=F32)
+
+
+class Place:
+    def __init__(self):
+        self.b = lax.axis_index("blk")
+        self.z = lax.axis_index("head")
+        self.y = self.b // 4
+        self.x = (self.b // 2) % 2
+        self.c = self.b % 2
+        self.q = self.b // 2
+
+    def chip(self, r):
+        return ((self.y + r // 2) % 2) * 2 + (self.x + r % 2) % 2
+
+    def peer(self, r):
+        return (2 * self.chip(r) + self.c, self.z)
+
+    def sibling(self):
+        return (2 * self.q + 1 - self.c, self.z)
+
+
+def remote(src, dst, send_sem, recv_sem, device):
+    return pltpu.make_async_remote_copy(
+        src_ref=src,
+        dst_ref=dst,
+        send_sem=send_sem,
+        recv_sem=recv_sem,
+        device_id=device,
+        device_id_type=MESH,
+    )
+
+
+def wait_bytes(view, sem):
+    pltpu.make_async_copy(view, view, sem).wait()
+
+
+def greet_all(at):
+    barrier = pltpu.get_barrier_semaphore()
+    flat = at.b * 4 + at.z
+
+    def greet(step, carry):
+        other = (flat + step) % 32
+        pl.semaphore_signal(
+            barrier, inc=1, device_id=(other // 4, other % 4), device_id_type=MESH
+        )
+        return carry
+
+    lax.fori_loop(1, 32, greet, 0)
+    pl.semaphore_wait(barrier, 31)
+
+
+def half(core):
+    return pl.ds(pl.multiple_of(core * 128, 128), 128)
+
+
+def lanes(index):
+    return pl.ds(pl.multiple_of(index * 128, 128), 128)
+
+
+def by_rows(count, size, step):
+    def body(i, carry):
+        step(pl.ds(pl.multiple_of(i * size, size), size))
+        return carry
+
+    lax.fori_loop(0, count // size, body, 0)
+
+
+def row_sums(count, size, width, step):
+    def body(i, carry):
+        parts = step(pl.ds(pl.multiple_of(i * size, size), size))
+        return tuple(
+            kept + jnp.sum(part.reshape(size // 8, 8, width), axis=0)
+            for kept, part in zip(carry, parts)
+        )
+
+    n = step.count
+    sums = lax.fori_loop(
+        0, count // size, body, tuple(jnp.zeros((8, width), F32) for _ in range(n))
+    )
+    return tuple(jnp.sum(s, axis=0, keepdims=True) for s in sums)
+
+
+class Exchange:
+    def __init__(self, at, send, recv, send_sib, recv_sib):
+        self.at, self.send, self.recv = at, send, recv
+        self.send_sib, self.recv_sib = send_sib, recv_sib
+
+    def gather_start(self, slots):
+        at = self.at
+        mine = slots.at[at.q, half(at.c)]
+        for r in (1, 2, 3):
+            remote(mine, mine, self.send.at[r], self.recv.at[r], at.peer(r)).start()
+        remote(mine, mine, self.send_sib.at[0], self.recv_sib.at[0], at.sibling()).start()
+
+    def gather_step(self, slots, r):
+        at = self.at
+        chip = at.chip(r)
+        block = slots.at[chip, half(at.c)]
+        if r:
+            wait_bytes(block, self.recv.at[r])
+            remote(
+                block, block, self.send_sib.at[r], self.recv_sib.at[r], at.sibling()
+            ).start()
+        wait_bytes(slots.at[chip, half(1 - at.c)], self.recv_sib.at[r])
+        return chip
+
+    def gather_end(self, slots):
+        at = self.at
+        for r in range(4):
+            block = slots.at[at.chip(r), half(at.c)]
+            if r:
+                wait_bytes(slots.at[at.q, half(at.c)], self.send.at[r])
+            wait_bytes(block, self.send_sib.at[r])
+
+    def scatter_put(self, terms, out_sib, in_sib, r):
+        at = self.at
+        out_sib[r] = terms[r, half(1 - at.c)].astype(BF16)
+        remote(
+            out_sib.at[r], in_sib.at[r], self.send_sib.at[r], self.recv_sib.at[r], at.sibling()
+        ).start()
+
+    def scatter_pass(self, terms, in_sib, out, into, r):
+        at = self.at
+        wait_bytes(in_sib.at[r], self.recv_sib.at[r])
+        total = terms[r, half(at.c)] + in_sib[r].astype(F32)
+        if r:
+            out[r] = total.astype(BF16)
+            remote(out.at[r], into.at[r], self.send.at[r], self.recv.at[r], at.peer(r)).start()
+        else:
+            terms[0, half(at.c)] = total
+
+    def scatter_arrive(self, into):
+        for r in (1, 2, 3):
+            wait_bytes(into.at[r], self.recv.at[r])
+
+    def scatter_end(self, out_sib, out):
+        for r in range(4):
+            wait_bytes(out_sib.at[r], self.send_sib.at[r])
+            if r:
+                wait_bytes(out.at[r], self.send.at[r])
+
+
+def norm_rows(values):
+    centre = jnp.mean(values, axis=-1, keepdims=True)
+    centred = values - centre
+    spread = jnp.mean(centred * centred, axis=-1, keepdims=True)
+    scale = lax.rsqrt(spread + NORM_EPS)
+    return centred * scale, scale
+
+
+def norm_back(grad, unit, scale):
+    centre = jnp.mean(grad, axis=-1, keepdims=True)
+    along = jnp.mean(grad * unit, axis=-1, keepdims=True)
+    return (grad - centre - unit * along) * scale
+
+
+def ffn_kernel(
+    x_ref,
+    att_ref,
+    wo_ref,
+    cot_ref,
+    par_ref,
+    bin_ref,
+    win_ref,
+    wback_ref,
+    out_ref,
+    d1_ref,
+    db_ref,
+    gwin_ref,
+    gwback_ref,
+    pg_ref,
+    gbin_ref,
+    wi,
+    wb,
+    n1,
+    unit1,
+    scale1,
+    d2,
+    norm_slots,
+    grad_slots,
+    hid,
+    slope,
+    pre,
+    terms,
+    sib_out,
+    sib_in,
+    peer_out,
+    peer_in,
+    gsend,
+    grecv_in,
+    grecv_back,
+    send,
+    recv,
+    send_sib,
+    recv_sib,
+    w_send,
+    w_recv,
+    g_send,
+    g_recv,
+):
+    at = Place()
+    flat = at.b * 4 + at.z
+    greet_all(at)
+
+    mine_rows = lanes(at.b)
+    mine_cols = lanes(at.z)
+    local = []
+    for k, (src, dst) in enumerate(((win_ref, wi), (wback_ref, wb))):
+        cp = pltpu.make_async_copy(
+            src.at[:, lanes(at.b)], dst.at[mine_rows, mine_cols], w_recv.at[k]
+        )
+        cp.start()
+
+        def push(step, carry, src=src, dst=dst, k=k):
+            other = (flat + step) % 32
+            remote(
+                src.at[:, lanes(other // 4)],
+                dst.at[mine_rows, mine_cols],
+                w_send.at[k],
+                w_recv.at[k],
+                (other // 4, other % 4),
+            ).start()
+            return carry
+
+        lax.fori_loop(1, 32, push, 0)
+
+    def param(i):
+        return par_ref[i : i + 1, :]
+
+    n1[...] = dot_nn(att_ref[...], wo_ref[...])
+
+    def first_norm(rows):
+        unit, scale = norm_rows(x_ref[rows].astype(F32) + n1[rows] + param(2))
+        unit1[rows] = unit
+        scale1[rows] = jnp.broadcast_to(scale, (32, 128))
+        n1[rows] = unit * param(3) + param(4)
+
+    by_rows(128, 32, first_norm)
+    norm_slots[at.q, half(at.c)] = n1[...].astype(BF16)
+    gather = Exchange(at, send.at[0], recv.at[0], send_sib.at[0], recv_sib.at[0])
+    gather.gather_start(norm_slots)
+
+    wait_bytes(wi, w_recv.at[0])
+    wait_bytes(wb, w_recv.at[1])
+
+    scatter = Exchange(at, send.at[1], recv.at[1], send_sib.at[1], recv_sib.at[1])
+    for r in range(4):
+        chip = gather.gather_step(norm_slots, r)
+        pre[...] = dot_nn(norm_slots[chip], wi[...])
+
+        def activate(rows, r=r):
+            u = pre[rows] + bin_ref[...]
+            cdf = 0.5 * (1.0 + lax.erf(u * math.sqrt(0.5)))
+            bell = jnp.exp(-0.5 * u * u) * (1.0 / math.sqrt(2.0 * math.pi))
+            hid[r, rows] = (u * cdf).astype(BF16)
+            slope[r, rows] = cdf + u * bell
+
+        by_rows(256, 32, activate)
+        terms[r] = contract_cols(hid[r], wb[...])
+        scatter.scatter_put(terms, sib_out.at[0], sib_in.at[0], r)
+        if r:
+            scatter.scatter_pass(terms, sib_in.at[0], peer_out.at[0], peer_in.at[0], r - 1)
+    scatter.scatter_pass(terms, sib_in.at[0], peer_out.at[0], peer_in.at[0], 3)
+    scatter.scatter_arrive(peer_in.at[0])
+
+    core_rows = pl.multiple_of(at.c * 128, 128)
+
+    def second_norm(rows):
+        own = pl.ds(pl.multiple_of(core_rows + rows.start, 32), 32)
+        total = (
+            terms[0, own]
+            + peer_in[0, 1, rows].astype(F32)
+            + peer_in[0, 2, rows].astype(F32)
+            + peer_in[0, 3, rows].astype(F32)
+        )
+        unit, scale = norm_rows(n1[rows] + total + param(5))
+        out_ref[rows] = (unit * param(6) + param(7)).astype(BF16)
+        g = cot_ref[rows].astype(F32)
+        d = norm_back(g * param(6), unit, scale)
+        d2[rows] = d
+        low = d.astype(BF16)
+        grad_slots[at.q, own] = low
+        return g * unit, g, low.astype(F32)
+
+    second_norm.count = 3
+    sums = row_sums(128, 32, 1024, second_norm)
+    pg_ref[6:7, :] = sums[0]
+    pg_ref[7:8, :] = sums[1]
+    pg_ref[5:6, :] = sums[2]
+
+    gather2 = Exchange(at, send.at[2], recv.at[2], send_sib.at[2], recv_sib.at[2])
+    gather2.gather_start(grad_slots)
+    scatter2 = Exchange(at, send.at[3], recv.at[3], send_sib.at[3], recv_sib.at[3])
+    gbin = jnp.zeros((1, 512), F32)
+    for r in range(4):
+        chip = gather2.gather_step(grad_slots, r)
+        pre[...] = dot_nn(grad_slots[chip], wb[...])
+
+        def deactivate(rows, r=r):
+            low = (pre[rows] * slope[r, rows]).astype(BF16)
+            pre[rows] = low.astype(F32)
+            return (low.astype(F32),)
+
+        deactivate.count = 1
+        gbin = gbin + row_sums(256, 32, 512, deactivate)[0]
+        dpre = pre[...].astype(BF16)
+        slope[r] = pre[...]
+        terms[r] = contract_cols(dpre, wi[...])
+        if r == 0:
+            scatter.scatter_end(sib_out.at[0], peer_out.at[0])
+        scatter2.scatter_put(terms, sib_out.at[1], sib_in.at[1], r)
+        if r:
+            scatter2.scatter_pass(terms, sib_in.at[1], peer_out.at[1], peer_in.at[1], r - 1)
+    scatter2.scatter_pass(terms, sib_in.at[1], peer_out.at[1], peer_in.at[1], 3)
+    gbin_ref[...] = gbin
+
+    def weight_grad(slots, right, which, into):
+        def one(step, carry):
+            other = (at.b + step) % 8
+            total = jnp.zeros((128, 512), F32)
+            for r in range(4):
+                total += contract_rows(slots[at.chip(r), :, lanes(other)], right(r))
+            gsend[which, other] = total.astype(BF16)
+            for k in range(4):
+                plane = (at.z + k) % 4
+                src = gsend.at[which, other, :, lanes(plane)]
+                dst = into.at[at.z, :, lanes(at.b)]
+
+                def away():
+                    remote(
+                        src, dst, g_send.at[which], g_recv.at[which], (other, plane)
+                    ).start()
+
+                if k:
+                    away()
+                else:
+                    pl.when(step != 0)(away)
+
+                    @pl.when(step == 0)
+                    def _():
+                        pltpu.make_async_copy(src, dst, g_recv.at[which]).start()
+
+            return carry
+
+        lax.fori_loop(0, 8, one, 0)
+
+    weight_grad(grad_slots, lambda r: hid[r], 1, grecv_back)
+    weight_grad(norm_slots, lambda r: slope[r].astype(BF16), 0, grecv_in)
+
+    scatter2.scatter_arrive(peer_in.at[1])
+
+    def first_back(rows):
+        own = pl.ds(pl.multiple_of(core_rows + rows.start, 32), 32)
+        total = (
+            d2[rows]
+            + terms[0, own]
+            + peer_in[1, 1, rows].astype(F32)
+            + peer_in[1, 2, rows].astype(F32)
+            + peer_in[1, 3, rows].astype(F32)
+        )
+        unit = unit1[rows]
+        d = norm_back(total * param(3), unit, scale1[rows][:, :1])
+        d1_ref[rows] = d
+        low = d.astype(BF16)
+        db_ref[rows] = low
+        return total * unit, total, low.astype(F32)
+
+    first_back.count = 3
+    sums = row_sums(128, 32, 1024, first_back)
+    pg_ref[3:4, :] = sums[0]
+    pg_ref[4:5, :] = sums[1]
+    pg_ref[2:3, :] = sums[2]
+    pg_ref[0:2, :] = jnp.zeros((2, 1024), F32)
+
+    for which, into, dest in ((1, grecv_back, gwback_ref), (0, grecv_in, gwin_ref)):
+        wait_bytes(into, g_recv.at[which])
+
+        def add(rows, into=into, dest=dest):
+            dest[rows] = (
+                into[0, rows].astype(F32)
+                + into[1, rows].astype(F32)
+                + into[2, rows].astype(F32)
+                + into[3, rows].astype(F32)
+            )
+
+        by_rows(128, 32, add)
+
+    gather.gather_end(norm_slots)
+    gather2.gather_end(grad_slots)
+    scatter2.scatter_end(sib_out.at[1], peer_out.at[1])
+    for k in range(2):
+        wait_bytes(wi.at[pl.ds(0, 992)], w_send.at[k])
+        wait_bytes(wi.at[pl.ds(0, 992)], g_send.at[k])
+
+
+def vmem():
+    return pl.BlockSpec(memory_space=pltpu.VMEM)
+
+
+def run_ffn(x, att, wo, cot, par, bins, win, wback):
+    shapes = (
+        ((128, 1024), BF16),
+        ((128, 1024), F32),
+        ((128, 1024), BF16),
+        ((128, 1024), F32),
+        ((128, 1024), F32),
+        ((8, 1024), F32),
+        ((1, 512), F32),
+    )
+    dma = pltpu.SemaphoreType.DMA
+    return pl.pallas_call(
+        ffn_kernel,
+        out_shape=[jax.ShapeDtypeStruct(s, t) for s, t in shapes],
+        in_specs=[vmem()] * 8,
+        out_specs=[vmem()] * 7,
+        scratch_shapes=[
+            pltpu.VMEM((1024, 512), BF16),
+            pltpu.VMEM((1024, 512), BF16),
+            pltpu.VMEM((128, 1024), F32),
+            pltpu.VMEM((128, 1024), F32),
+            pltpu.VMEM((128, 128), F32),
+            pltpu.VMEM((128, 1024), F32),
+            pltpu.VMEM((4, 256, 1024), BF16),
+            pltpu.VMEM((4, 256, 1024), BF16),
+            pltpu.VMEM((4, 256, 512), BF16),
+            pltpu.VMEM((4, 256, 512), F32),
+            pltpu.VMEM((256, 512), F32),
+            pltpu.VMEM((4, 256, 1024), F32),
+            pltpu.VMEM((2, 4, 128, 1024), BF16),
+            pltpu.VMEM((2, 4, 128, 1024), BF16),
+            pltpu.VMEM((2, 4, 128, 1024), BF16),
+            pltpu.VMEM((2, 4, 128, 1024), BF16),
+            pltpu.VMEM((2, 8, 128, 512), BF16),
+            pltpu.VMEM((4, 128, 1024), BF16),
+            pltpu.VMEM((4, 128, 1024), BF16),
+            dma((4, 4)),
+            dma((4, 4)),
+            dma((4, 4)),
+            dma((4, 4)),
+            dma((2,)),
+            dma((2,)),
+            dma((2,)),
+            dma((2,)),
+        ],
+        compiler_params=pltpu.CompilerParams(
+            collective_id=1, has_side_effects=True, vmem_limit_bytes=VMEM_LIMIT
+        ),
+    )(x, att, wo, cot, par, bins, win, wback)
+
+
+def fast_device(
+    tokens,
+    w_query,
+    w_key,
+    w_value,
+    w_out,
+    b_query,
+    b_value,
+    b_out,
+    norm1_gain,
+    norm1_shift,
+    w_in,
+    w_back,
+    b_in,
+    b_back,
+    norm2_gain,
+    norm2_shift,
+    cotangent,
+):
+    f32 = jnp.float32
+    bf16 = jnp.bfloat16
+    score_scale = HEAD_DIM ** (-0.5)
+    b_id = lax.axis_index("blk")
+    small = jnp.concatenate(
+        (b_query, b_value, b_out, norm1_gain, norm1_shift, b_back, norm2_gain, norm2_shift, b_in)
+    )
+    smalls = lax.all_gather(small, ("blk", "head"), axis=0)
+    vectors = smalls[:, :256].reshape(32, 8, 32).transpose(1, 0, 2).reshape(8, 1024).astype(f32)
+    bin_full = smalls[:, 256:].reshape(4, 8, 128)
+    bins = lax.dynamic_index_in_dim(bin_full, b_id, 1, False).reshape(1, 512).astype(f32)
+    attn_cols, out_rows = (
+        lax.all_gather(jnp.stack((w_query, w_key, w_value)), "blk", axis=1, tiled=True),
+        lax.all_gather(w_out, "blk", axis=1, tiled=True),
+    )
+    seq_count, local_len, model_dim = tokens.shape
+    token_shape = (seq_count, local_len, model_dim)
+    head_id = lax.axis_index("head")
+    width_part = attn_cols.shape[2]
+    bq_part = lax.dynamic_slice_in_dim(vectors[0], head_id * width_part, width_part)
+    bv_part = lax.dynamic_slice_in_dim(vectors[1], head_id * width_part, width_part)
+    wide_rows = token_rows(tokens)
+    wide_len = wide_rows.shape[1]
+    wide_flat = wide_rows.reshape(-1, model_dim)
+    head_shape = (seq_count, wide_len, width_part)
+    wide_shape = (seq_count, wide_len, model_dim)
+    query_heads = (
+        (jnp.dot(wide_flat, attn_cols[0], preferred_element_type=f32) + bq_part)
+        .astype(bf16)
+        .reshape(head_shape)
+    )
+    key_heads = (
+        jnp.dot(wide_flat, attn_cols[1], preferred_element_type=f32)
+        .astype(bf16)
+        .reshape(head_shape)
+    )
+    value_heads = (
+        (jnp.dot(wide_flat, attn_cols[2], preferred_element_type=f32) + bv_part)
+        .astype(bf16)
+        .reshape(head_shape)
+    )
+    query4 = split_heads(query_heads)
+    key4 = split_heads(key_heads)
+    value4 = split_heads(value_heads)
+    pieces = (
+        lax.all_gather(key_heads, "blk", axis=1, tiled=True),
+        lax.all_gather(value_heads, "blk", axis=1, tiled=True),
+    )
+    scores = score_block(query4, split_heads(pieces[0]))
+    maxima = jnp.max(scores, axis=-1)
+    weights = jnp.exp(scores - maxima[..., None])
+    totals = jnp.sum(weights, axis=-1)
+    summed = jnp.einsum(
+        "sqgk,skge->sqge", weights.astype(bf16), split_heads(pieces[1]), preferred_element_type=f32
+    )
+    log_sums = maxima + jnp.log(totals)
+    attended4 = summed / totals[..., None]
+    attended_heads = attended4.reshape(head_shape).astype(bf16)
+    attended_flat = attended_heads.reshape(-1, width_part)
+    att = lax.all_to_all(attended_heads, "head", split_axis=1, concat_axis=2, tiled=True)
+    wo = lax.all_gather(out_rows, "head", axis=0, tiled=True)
+    flat_rows = tokens.reshape(-1, model_dim)
+    output, d_first, d_branch, gw_in, gw_back, pg, gbin = run_ffn(
+        flat_rows,
+        att.reshape(-1, model_dim),
+        wo,
+        cotangent.reshape(-1, model_dim),
+        vectors,
+        bins,
+        w_in,
+        w_back,
+    )
+    wide_dbranch = token_rows(d_branch.reshape(token_shape)).reshape(-1, model_dim)
+    grad_out_part = contract_rows(attended_flat, wide_dbranch)
+    grad_heads = contract_cols(wide_dbranch, out_rows).astype(bf16).reshape(head_shape)
+    grads4 = split_heads(grad_heads)
+    deltas = jnp.sum(grads4.astype(f32) * attended4, axis=-1)
+    row_stats = (
+        lax.all_gather(log_sums, "blk", axis=1, tiled=True),
+        lax.all_gather(deltas, "blk", axis=1, tiled=True),
+    )
+    piece_keys = split_heads(pieces[0])
+    piece_values = split_heads(pieces[1])
+    piece_queries = split_heads(lax.all_gather(query_heads, "blk", axis=1, tiled=True))
+    piece_grads = split_heads(lax.all_gather(grad_heads, "blk", axis=1, tiled=True))
+    own_probs, own_scores = score_grads(query4, piece_keys, piece_values, grads4, log_sums, deltas)
+    d_query = score_scale * jnp.einsum(
+        "sqgk,skge->sqge", own_scores, piece_keys, preferred_element_type=f32
+    )
+    probs_low, d_scores = score_grads(
+        piece_queries, key4, value4, piece_grads, row_stats[0], row_stats[1]
+    )
+    key_acc = score_scale * jnp.einsum(
+        "sqgk,sqge->skge", d_scores, piece_queries, preferred_element_type=f32
+    )
+    value_acc = jnp.einsum("sqgk,sqge->skge", probs_low, piece_grads, preferred_element_type=f32)
+    d_query_low = d_query.reshape(-1, width_part).astype(bf16)
+    d_key_low = key_acc.reshape(-1, width_part).astype(bf16)
+    d_value_low = value_acc.reshape(-1, width_part).astype(bf16)
+    grad_b_query = place_part(
+        jnp.sum(d_query_low.astype(f32), axis=0), model_dim, head_id * width_part
+    )
+    grad_b_value = place_part(
+        jnp.sum(d_value_low.astype(f32), axis=0), model_dim, head_id * width_part
+    )
+    attn_grad_parts = jnp.stack(
+        (
+            contract_rows(wide_flat, d_query_low),
+            contract_rows(wide_flat, d_key_low),
+            contract_rows(wide_flat, d_value_low),
+        )
+    )
+    token_terms = (
+        contract_cols(d_query_low, attn_cols[0])
+        + contract_cols(d_key_low, attn_cols[1])
+        + contract_cols(d_value_low, attn_cols[2])
+    )
+    d_tokens = d_first + token_partials(token_terms.reshape(wide_shape)).reshape(-1, model_dim)
+    grad_tokens = d_tokens.astype(bf16).reshape(token_shape)
+    attn_sums, grad_w_out = (
+        lax.psum_scatter(attn_grad_parts, "blk", scatter_dimension=1, tiled=True),
+        lax.psum_scatter(grad_out_part, "blk", scatter_dimension=1, tiled=True),
+    )
+    gb_in = lax.dynamic_update_slice(
+        jnp.zeros((4, 8, 128), f32), gbin.reshape(4, 1, 128), (0, b_id, 0)
+    )
+    vec = jnp.concatenate(
+        (grad_b_query[None], grad_b_value[None], pg[2:]), axis=0
+    )
+    vec = vec.reshape(8, 32, 32).transpose(1, 0, 2).reshape(32, 256)
+    vec = jnp.concatenate((vec, gb_in.reshape(32, 128)), axis=1)
+    own = lax.psum_scatter(vec, ("blk", "head"), scatter_dimension=0, tiled=True).reshape(384)
+    parts = [own[32 * i : 32 * i + 32] for i in range(8)]
+    return (
+        output.reshape(token_shape),
+        grad_tokens,
+        attn_sums[0],
+        attn_sums[1],
+        attn_sums[2],
+        grad_w_out,
+        parts[0],
+        parts[1],
+        parts[2],
+        parts[3],
+        parts[4],
+        gw_in,
+        gw_back,
+        own[256:],
+        parts[5],
+        parts[6],
+        parts[7],
+    )
+
+
 def solution(mesh):
     in_specs = (
         P(None, ("blk", "head"), None),
@@ -325,6 +961,8 @@
         P(("blk", "head")),
         P(("blk", "head")),
     )
+    sizes = (mesh.shape["blk"], mesh.shape["head"])
+    body = fast_device if sizes == (8, 4) else per_device
     return jax.shard_map(
-        per_device, mesh=mesh, in_specs=in_specs, out_specs=out_specs, check_vma=False
-    )
+        body, mesh=mesh, in_specs=in_specs, out_specs=out_specs, check_vma=False
+    )

time: 1120 us -> 658 us (0.59)
  waiting for transfers between devices: 722 us -> 217 us
  Pallas kernels: 0 us -> 141 us
  blocking collectives: 189 us -> 138 us
  matrix products: 106 us -> 79 us
  other arithmetic: 38 us -> 15.5 us
    reduce_scatter x4 -> x2, waiting for transfers between devices: 355 us -> 63.1 us  [the longest x1 36.5 us: fast_device(): lax.psum_scatter(grad_out_part, 'blk', scatter_dimension=1, tiled=True)]
    all_gather x7 -> x6, waiting for transfers between devices: 310 us -> 79.5 us  [the longest x1 34.4 us: fast_device(): lax.all_gather(query_heads, 'blk', axis=1, tiled=True)]
    pallas_call x0 -> x1, Pallas kernels: none -> 141 us  [run_ffn(): pl.pallas_call(ffn_kernel, out_shape=[jax.ShapeDtypeStruct(s, t) for s, t...]
    unnamed x2 -> x1, blocking collectives: 81.6 us -> 39.8 us
    dot_general x10 -> x7, matrix products: 67.1 us -> 50.3 us  [the longest x1 13.6 us: fast_device(): jnp.einsum('sqgk,sqge->skge', d_scores, piece_queries, preferred_element_...]
    all_to_all x0 -> x1, waiting for transfers between devices: none -> 14.5 us  [fast_device(): lax.all_to_all(attended_heads, 'head', split_axis=1, concat_axis=2, tiled...]
  transfers between devices with their start and end apart: 15 -> 12, of which waited for: 11 -> 9; matrix products, arithmetic and copies ran while one was open for 14% -> 14% of each run, Pallas kernels for 0% -> 0%
where the time goes in v1:
time: 658 us; the launch traced here: 648 us
  waiting for transfers between devices  217 us (33%)
  Pallas kernels  141 us (21%)
  blocking collectives  138 us (21%)
  matrix products  79 us (12%)
  local copies, waits for them, and re-layouts  37.1 us (6%)
  other arithmetic  15.5 us (2%)
  between operations  14.7 us (2%)
    pallas_call x1, Pallas kernels, run_ffn(): pl.pallas_call(ffn_kernel, out_shape=[jax.ShapeDtypeStruct(s, t) for s, t...  141 us
    all_gather x1, blocking collectives, fast_device(): smalls = lax.all_gather(small, ('blk', 'head'), axis=0)  68.2 us
    all_gather x2, waiting for transfers between devices, token_rows(): return lax.all_gather(local, 'head', axis=1, tiled=True)  59.2 us
    unnamed x1, blocking collectives  39.8 us
    reduce_scatter x1, waiting for transfers between devices, fast_device(): lax.psum_scatter(grad_out_part, 'blk', scatter_dimension=1, tiled=True)  36.5 us
    all_gather x1, waiting for transfers between devices, fast_device(): lax.all_gather(query_heads, 'blk', axis=1, tiled=True)  34.4 us
    all_gather x1, waiting for transfers between devices, fast_device(): lax.all_gather(jnp.stack((w_query, w_key, w_value)), 'blk', axis=1, tiled...  27.7 us
    reduce_scatter x1, waiting for transfers between devices, fast_device(): lax.psum_scatter(attn_grad_parts, 'blk', scatter_dimension=1, tiled=True)  26.6 us
  transfers between devices with their start and end apart: 12, of which 9 were waited for; matrix products, arithmetic and copies ran while one was open for 14% of the time, Pallas kernels for 0%

profile of v1, /device:TPU:0, one launch (start us, length us, event | category | flops | bytes accessed | tf_op | source)
XLA Modules:
  0.0 647.9 jit_solution(17249059596177269636)
XLA Ops:
  7.3 0.7 all-gather.13.cloned.1.call-update
  8.1 1.6 pad_maximum_fusion.1
  9.7 30.6 %all-gather.13.cloned.1.call-done = bf16[2,256,1024]{2,1,0:T(8,128)(2,1)} async-done(((bf16[2,64,1024]{2,1,0:T(8,128)(2,1)}), bf16[2,256,1024]{2,1,0:T(8,128)(2,1)}) %all-gather.13.cloned.1.call-update) | async-done | bytes 1048592 | tf_op jit(solution)/shard_map/all_gather | solution.py:58
  40.4 27.7 %all-gather.11.cloned.1.call-done = bf16[3,1024,256]{2,1,0:T(8,128)(2,1)} async-done(((bf16[3,128,256]{2,1,0:T(8,128)(2,1)}), bf16[3,1024,256]{2,1,0:T(8,128)(2,1)}) %all-gather.11.cloned.1.call-update) | async-done | bytes 1572880 | tf_op jit(solution)/shard_map/all_gather | solution.py:783
  68.1 2.0 fusion.45
  70.1 0.8 reshape.180
  71.1 68.2 %all-gather.1 = bf16[32,1,384]{2,1,0:T(2,128)(2,1)S(1)} all-gather(bf16[1,1,384]{2,1,0:T(2,128)(2,1)S(1)} %reshape.204), channel_id=2, replica_groups=mesh['blk'=8,'head'=4] {'blk','head'}, dimensions={0}, use_global_device_ids=true | all-gather | bytes 25344 | tf_op jit(solution)/shard_map/all_gather | solution.py:778
  139.3 0.6 copy-done.19
  140.8 0.8 reshape.178
  141.7 12.1 %all_gather.45 = bf16[256,1024]{1,0:T(8,128)(2,1)} all-gather(bf16[256,128]{1,0:T(8,128)(2,1)S(1)} %copy-done.20), channel_id=1, replica_groups=mesh['blk'=8,'head'=4] {'blk'}, dimensions={1}, use_global_device_ids=true | all-gather | bytes 589824 | tf_op jit(solution)/shard_map/all_gather | solution.py:784
  153.8 1.2 fusion.46
  155.0 1.0 reshape_reshape.12
  156.0 2.5 copy.74
  158.5 16.9 %all-gather.15.cloned.1.call-done = bf16[2,2048,256]{1,0,2:T(2,128)(2,1)} async-done(((bf16[2,256,256]{1,0,2:T(2,128)(2,1)}), bf16[2,2048,256]{1,0,2:T(2,128)(2,1)}) %all-gather.15.cloned.1.call-update) | async-done | bytes 2097168 | tf_op jit(solution)/shard_map/all_gather | solution.py:817
  175.4 2.5 copy.73
  177.9 8.5 %bitcast_reduce_fusion = (f32[2,256,4]{1,2,0:T(4,128)S(1)}, f32[2,4,2048,256]{3,2,1,0:T(8,128)}) fusion(bf16[2,2048,4,64]{1,3,2,0:T(8,128)(2,1)S(1)} %bitcast.251, bf16[2,256,4,64]{1,0,3,2:T(2,128)(2,1)S(1)} %reshape_reshape.12), kind=kOutput, calls=%fused_computation.10 | convolution fusion | flops 545257472 | bytes 19144704 | tf_op jit(solution)/shard_map/sqge,skge->sqgk/dot_general | solution.py:45
  186.4 8.5 %fusion.7 = f32[2,256,4]{1,2,0:T(4,128)S(1)} fusion(f32[2,4,2048,256]{3,2,1,0:T(8,128)} %get-tuple-element.96, f32[2,256,4]{1,2,0:T(4,128)S(1)} %get-tuple-element.95), kind=kLoop, calls=%fused_computation.13 | loop fusion | flops 12580864 | bytes 16793600 | tf_op jit(solution)/shard_map/reduce_sum | solution.py:822
  194.9 9.5 %fusion.70 = (bf16[2,256,4,64]{1,3,2,0:T(8,128)(2,1)S(1)}, f32[2,256,4,64]{1,3,2,0:T(8,128)}) fusion(f32[2,256,4]{1,2,0:T(4,128)S(1)} %fusion.7, bf16[2,2048,4,64]{1,3,2,0:T(8,128)(2,1)S(1)} %bitcast.255, f32[2,4,2048,256]{3,2,1,0:T(8,128)} %get-tuple-element.96, f32[2,256,4]{1,2,0:T(4,128)S(1)} %get-tuple-element.95), kind=kOutput, calls=%fused_computation.92 | convolution fusion | flops 549715968 | bytes 19677184 | tf_op jit(solution)/shard_map/sqgk,skge->sqge/dot_general | solution.py:823
  204.4 0.9 copy.77
  205.3 4.8 all-to-all-start
  210.3 0.7 convert_element_type.118.par_ref
  211.0 0.7 slice_bitcast_fusion.12
  212.3 14.5 %all-to-all-done = bf16[2,256,256]{2,0,1:T(2,128)(2,1)S(1)} async-done(((bf16[2,256,256]{2,0,1:T(2,128)(2,1)}), bf16[2,256,256]{2,0,1:T(2,128)(2,1)S(1)}, u32[]{:S(2)}, u32[]{:S(2)}) %all-to-all-start) | async-done | bytes 262176 | tf_op jit(solution)/shard_map/all_to_all | solution.py:830
  227.1 0.7 copy.106
  228.4 141.0 %shard_map.296 = (bf16[128,1024]{1,0:T(8,128)(2,1)}, f32[128,1024]{1,0:T(8,128)}, bf16[128,1024]{1,0:T(8,128)(2,1)}, f32[128,1024]{1,0:T(8,128)}, f32[128,1024]{...) custom-call(bf16[128,1024]{1,0:T(8,128)(2,1)} %bitcast.266, bf16[128,1024]{1,0:T(8,128)(2,1)} %bitcast.268, ...), custom_call_target="tpu_custom_call" | custom-call | tf_op jit(solution)/shard_map/pallas_call | solution.py:712
  369.4 0.8 reshape.188
  370.3 28.6 %all-gather.21.cloned.1.call-done = bf16[2,256,1024]{2,1,0:T(8,128)(2,1)} async-done(((bf16[2,64,1024]{2,1,0:T(8,128)(2,1)}), bf16[2,256,1024]{2,1,0:T(8,128)(2,1)}) %all-gather.21.cloned.1.call-update) | async-done | bytes 1048592 | tf_op jit(solution)/shard_map/all_gather | solution.py:58
  398.9 2.4 convolution_convert_fusion
  401.4 0.8 reshape_reshape.14
  402.2 0.8 reshape_reshape.15
  402.9 34.4 %all-gather.23.cloned.1.call-done = bf16[2,2048,256]{1,0,2:T(2,128)(2,1)} async-done(((bf16[2,256,256]{1,0,2:T(2,128)(2,1)}), bf16[2,2048,256]{1,0,2:T(2,128)(2,1)}) %all-gather.23.cloned.1.call-update) | async-done | bytes 2097168 | tf_op jit(solution)/shard_map/all_gather | solution.py:854
  437.3 2.5 copy.86
  439.8 9.4 %all_gather.49 = f32[2,2048,4]{1,2,0:T(4,128)S(1)} all-gather(f32[2,256,4]{1,2,0:T(4,128)S(1)} %bitcast.290), channel_id=1, replica_groups=mesh['blk'=8,'head'=4] {'blk'}, dimensions={1}, use_global_device_ids=true | all-gather | bytes 73728 | tf_op jit(solution)/shard_map/all_gather | solution.py:849
  449.2 8.1 %fusion.62 = f32[2,4,256,2048]{3,2,1,0:T(8,128)} fusion(bf16[2,2048,4,64]{1,3,2,0:T(8,128)(2,1)S(1)} %bitcast.243, bf16[2,256,4,64]{1,0,3,2:T(2,128)(2,1)S(1)} %copy-done.7), kind=kOutput, calls=%fused_computation.58 | convolution fusion | flops 536870912 | bytes 19136512 | tf_op jit(solution)/shard_map/sqge,skge->sqgk/dot_general | solution.py:45
  457.4 2.0 reshape.208
  459.4 2.0 copy.82
  461.3 1.2 multiply_reduce_fusion
  462.5 13.4 %convert_reduce_fusion.1 = (f32[4,64]{1,0:T(4,128)S(1)}, bf16[2,256,4,64]{1,3,2,0:T(8,128)(2,1)}) fusion(bf16[2,2048,4,64]{1,3,2,0:T(8,128)(2,1)} %bitcast.252, f32[2,4,2048,256]{3,2,1,0:T(8,128)} %get-tuple-element.96, f32[2,256,4]{1,2,0:T(4,128)S(1)} %multiply_reduce_fusion, f32[2,256,4]{1,2,0:T(4,128)S(1)} %bitcast.291, ...), kind=kOutput, calls=%fused_computation.53 | convolution fusion | flops 1095237376 | bytes 21513216 | tf_op jit(solution)/shard_map/sqgk,skge->sqge/dot_general | solution.py:857
  476.0 1.2 copy.85
  477.2 8.3 %all_gather.51 = f32[2,2048,4]{1,2,0:T(4,128)S(1)} all-gather(f32[2,256,4]{1,2,0:T(4,128)S(1)} %multiply_reduce_fusion), channel_id=1, replica_groups=mesh['blk'=8,'head'=4] {'blk'}, dimensions={1}, use_global_device_ids=true | all-gather | bytes 73728 | tf_op jit(solution)/shard_map/all_gather | solution.py:850
  485.6 2.9 fusion.59
  488.4 4.0 copy.88
  492.4 10.1 %convert_reduce_fusion = (f32[4,64]{1,0:T(4,128)S(1)}, bf16[2,256,4,64]{1,3,2,0:T(8,128)(2,1)}) fusion(bf16[2,2048,4,64]{1,3,2,0:T(8,128)(2,1)} %bitcast.253, f32[2,4,256,2048]{3,2,1,0:T(8,128)} %fusion.62, f32[2,2048,4]{1,2,0:T(4,128)S(1)} %all_gather.49), kind=kOutput, calls=%fused_computation.52 | convolution fusion | flops 549846784 | bytes 19203072 | tf_op jit(solution)/shard_map/sqgk,sqge->skge/dot_general | solution.py:866
  502.5 13.6 %fusion.48 = bf16[2,256,4,64]{1,3,2,0:T(8,128)(2,1)} fusion(bf16[2,2048,4,64]{1,3,2,0:T(8,128)(2,1)S(1)} %bitcast.244, f32[2,4,256,2048]{3,2,1,0:T(8,128)} %fusion.62, f32[2,2048,4]{1,2,0:T(4,128)S(1)} %all_gather.51, f32[2,2048,4]{1,2,0:T(4,128)S(1)} %all_gather.49, bf16[2,2048,4,64]{1,3,2,0:T(8,128)(2,1)} %bitcast.254, ...), kind=kOutput, calls=%fused_computation.44 | convolution fusion | flops 1094975488 | bytes 21626880 | tf_op jit(solution)/shard_map/sqgk,sqge->skge/dot_general | solution.py:863
  516.1 1.4 copy.91
  517.5 1.2 copy.93
  518.8 1.5 fusion.58
  520.3 2.6 add_convert_fusion
  524.5 1.9 pad_maximum_fusion
  526.5 1.1 copy-done.9
  527.6 1.4 convolution_bitcast_fusion
  529.7 39.8 %all-reduce = f32[32,384]{1,0:T(8,128)S(1)} all-reduce(f32[32,384]{1,0:T(8,128)S(1)} %pad_maximum_fusion.2), channel_id=6, replica_groups=mesh['blk'=8,'head'=4] {'blk','head'}, use_global_device_ids=true, to_apply=%region_8.9.clone | all-reduce | flops 12288 | bytes 98304
  569.5 0.6 dynamic-slice_bitcast_fusion.3
  570.1 0.6 dynamic-slice_bitcast_fusion
  570.7 1.7 fusion.57
  572.4 26.6 %reduce-scatter.6.cloned.1.call-done = f32[3,128,256]{1,2,0:T(8,128)} async-done(((f32[3,1024,256]{1,2,0:T(8,128)}), f32[3,128,256]{1,2,0:T(8,128)}) %reduce-scatter.6.cloned.1.call-update) | async-done | bytes 393232 | tf_op jit(solution)/shard_map/reduce_scatter | solution.py:891
  599.0 1.1 slice_bitcast_fusion.9
  600.1 0.8 copy.96
  600.8 0.8 copy.97
  601.6 0.8 copy.98
  602.3 36.5 %reduce-scatter.8.cloned.1.call-done = f32[256,128]{1,0:T(8,128)} async-done(((f32[256,1024]{1,0:T(8,128)}), f32[256,128]{1,0:T(8,128)}) %reduce-scatter.8.cloned.1.call-update) | async-done | bytes 131088 | tf_op jit(solution)/shard_map/reduce_scatter | solution.py:892
  638.9 0.7 copy.127
  639.6 0.8 copy.128
  640.4 0.8 copy.129
  (122 shorter events, 5.4 us)
Async XLA Ops:
  7.2 63.7 %copy-start.23 = (bf16[32]{0:T(256)(128)(2,1)S(1)}, bf16[32]{0:T(256)(128)(2,1)}, u32[]{:S(2)}) copy-start(bf16[32]{0:T(256)(128)(2,1)} %param.22) | copy-start | bytes 196
  7.2 63.7 %copy-start.24 = (bf16[32]{0:T(256)(128)(2,1)S(1)}, bf16[32]{0:T(256)(128)(2,1)}, u32[]{:S(2)}) copy-start(bf16[32]{0:T(256)(128)(2,1)} %param.23) | copy-start | bytes 196
  7.2 63.7 %copy-start.25 = (bf16[32]{0:T(256)(128)(2,1)S(1)}, bf16[32]{0:T(256)(128)(2,1)}, u32[]{:S(2)}) copy-start(bf16[32]{0:T(256)(128)(2,1)} %param.24) | copy-start | bytes 196
  7.2 63.7 %copy-start.26 = (bf16[32]{0:T(256)(128)(2,1)S(1)}, bf16[32]{0:T(256)(128)(2,1)}, u32[]{:S(2)}) copy-start(bf16[32]{0:T(256)(128)(2,1)} %param.25) | copy-start | bytes 196
  7.2 63.7 %copy-start.27 = (bf16[32]{0:T(256)(128)(2,1)S(1)}, bf16[32]{0:T(256)(128)(2,1)}, u32[]{:S(2)}) copy-start(bf16[32]{0:T(256)(128)(2,1)} %param.26) | copy-start | bytes 196
  7.2 63.7 %copy-start.28 = (bf16[32]{0:T(256)(128)(2,1)S(1)}, bf16[32]{0:T(256)(128)(2,1)}, u32[]{:S(2)}) copy-start(bf16[32]{0:T(256)(128)(2,1)} %param.30) | copy-start | bytes 196
  7.3 63.7 %copy-start.29 = (bf16[32]{0:T(256)(128)(2,1)S(1)}, bf16[32]{0:T(256)(128)(2,1)}, u32[]{:S(2)}) copy-start(bf16[32]{0:T(256)(128)(2,1)} %param.31) | copy-start | bytes 196
  7.3 63.7 %copy-start.30 = (bf16[32]{0:T(256)(128)(2,1)S(1)}, bf16[32]{0:T(256)(128)(2,1)}, u32[]{:S(2)}) copy-start(bf16[32]{0:T(256)(128)(2,1)} %param.32) | copy-start | bytes 196
  7.3 63.7 %copy-start.31 = (bf16[128]{0:T(256)(128)(2,1)S(1)}, bf16[128]{0:T(256)(128)(2,1)}, u32[]{:S(2)}) copy-start(bf16[128]{0:T(256)(128)(2,1)} %param.29) | copy-start | bytes 772
  7.3 33.1 %all-gather.13.cloned.1.call-start = ((), (), s32[]{:S(2)}) async-start(), calls=%async_computation.5 | async-start | bytes 1310720 | tf_op jit(solution)/shard_map/all_gather | solution.py:58
  8.0 60.0 %all-gather.11.cloned.1.call-start = ((), (), s32[]{:S(2)}) async-start(), calls=%async_computation.4 | async-start | bytes 1769472 | tf_op jit(solution)/shard_map/all_gather | solution.py:783
  9.7 146.3 %all-gather.17.cloned.1.call-start = ((), (), s32[]{:S(2)}) async-start(), calls=%async_computation.7 | async-start | bytes 2359296 | tf_op jit(solution)/shard_map/all_gather | solution.py:816
  40.4 99.9 %copy-start = (bf16[2,256,1024]{2,1,0:T(8,128)(2,1)S(1)}, bf16[2,256,1024]{2,1,0:T(8,128)(2,1)}, u32[]{:S(2)}) copy-start(bf16[2,256,1024]{2,1,0:T(8,128)(2,1)} %all-gather.13.cloned.1.call-done) | copy-start | bytes 3145732
  68.0 72.3 %copy-start.8 = (bf16[3,1024,256]{2,1,0:T(8,128)(2,1)S(1)}, bf16[3,1024,256]{2,1,0:T(8,128)(2,1)}, u32[]{:S(2)}) copy-start(bf16[3,1024,256]{2,1,0:T(8,128)(2,1)} %all-gather.11.cloned.1.call-done) | copy-start | bytes 4718596
  68.1 73.6 %copy-start.20 = (bf16[256,128]{1,0:T(8,128)(2,1)S(1)}, bf16[256,128]{1,0:T(8,128)(2,1)}, u32[]{:S(2)}) copy-start(bf16[256,128]{1,0:T(8,128)(2,1)} %param.21) | copy-start | bytes 196612
  70.0 84.9 %copy-start.10 = (bf16[512,256]{0,1:T(8,128)(2,1)}, bf16[512,256]{0,1:T(8,128)(2,1)S(1)}, u32[]{:S(2)}) copy-start(bf16[512,256]{0,1:T(8,128)(2,1)S(1)} %fusion.45) | copy-start | bytes 786436
  70.9 104.6 %all-gather.15.cloned.1.call-start = ((), (), s32[]{:S(2)}) async-start(), calls=%async_computation.6 | async-start | bytes 2359296 | tf_op jit(solution)/shard_map/all_gather | solution.py:817
  139.3 0.6 copy-start.19
  140.8 15.2 %copy-start.12 = (bf16[512,256]{0,1:T(8,128)(2,1)}, bf16[512,256]{0,1:T(8,128)(2,1)S(1)}, u32[]{:S(2)}) copy-start(bf16[512,256]{0,1:T(8,128)(2,1)S(1)} %fusion.47) | copy-start | bytes 786436
  141.6 86.8 %all-gather.19.cloned.1.call-start = ((), (), s32[]{:S(2)}) async-start(), calls=%async_computation.8 | async-start | bytes 2621440 | tf_op jit(solution)/shard_map/all_gather | solution.py:831
  158.5 27.9 %copy-start.1 = (bf16[2,2048,256]{1,2,0:T(8,128)(2,1)}, bf16[2,2048,256]{1,2,0:T(8,128)(2,1)S(1)}, u32[]{:S(2)}) copy-start(bf16[2,2048,256]{1,2,0:T(8,128)(2,1)S(1)} %copy.74) | copy-start | bytes 6291460
  177.9 17.0 %copy-start.3 = (bf16[2,2048,256]{1,2,0:T(8,128)(2,1)}, bf16[2,2048,256]{1,2,0:T(8,128)(2,1)S(1)}, u32[]{:S(2)}) copy-start(bf16[2,2048,256]{1,2,0:T(8,128)(2,1)S(1)} %copy.73) | copy-start | bytes 6291460
  205.3 164.2 %copy-start.14 = (bf16[512,256]{0,1:T(8,128)(2,1)S(1)}, bf16[512,256]{0,1:T(8,128)(2,1)}, u32[]{:S(2)}) copy-start(bf16[512,256]{0,1:T(8,128)(2,1)} %fusion.46) | copy-start | bytes 786436
  205.3 21.6 %all-to-all-start = ((bf16[2,256,256]{2,0,1:T(2,128)(2,1)}), bf16[2,256,256]{2,0,1:T(2,128)(2,1)S(1)}, u32[]{:S(2)}, u32[]{:S(2)}) async-start(bf16[2,256,256]{2,0,1:T(2,128)(2,1)} %copy.77), calls=%async_computation | async-start | bytes 524288 | tf_op jit(solution)/shard_map/all_to_all | solution.py:830
  210.1 188.9 %all-gather.21.cloned.1.call-start = ((), (), s32[]{:S(2)}) async-start(), calls=%async_computation.9 | async-start | bytes 1310720 | tf_op jit(solution)/shard_map/all_gather | solution.py:58
  210.3 188.6 %copy-start.6 = (bf16[256,1024]{1,0:T(8,128)(2,1)S(1)}, bf16[256,1024]{1,0:T(8,128)(2,1)}, u32[]{:S(2)}) copy-start(bf16[256,1024]{1,0:T(8,128)(2,1)} %all_gather.45) | copy-start | bytes 1572868
  228.4 173.0 %copy-start.11 = (bf16[512,256]{0,1:T(8,128)(2,1)S(1)}, bf16[512,256]{0,1:T(8,128)(2,1)}, u32[]{:S(2)}) copy-start(bf16[512,256]{0,1:T(8,128)(2,1)} %copy-done.10) | copy-start | bytes 786436
  228.4 173.8 %copy-start.13 = (bf16[512,256]{0,1:T(8,128)(2,1)S(1)}, bf16[512,256]{0,1:T(8,128)(2,1)}, u32[]{:S(2)}) copy-start(bf16[512,256]{0,1:T(8,128)(2,1)} %copy-done.12) | copy-start | bytes 786436
  369.4 67.9 %all-gather.23.cloned.1.call-start = ((), (), s32[]{:S(2)}) async-start(), calls=%async_computation.10 | async-start | bytes 2359296 | tf_op jit(solution)/shard_map/all_gather | solution.py:854
  370.2 118.2 %all-gather.25.cloned.1.call-start = ((), (), s32[]{:S(2)}) async-start(), calls=%async_computation.11 | async-start | bytes 2359296 | tf_op jit(solution)/shard_map/all_gather | solution.py:855
  401.3 169.3 %reduce-scatter.4.cloned.1.call-start = ((), (), s32[]{:S(2)}) async-start(), calls=%async_computation.12 | async-start | bytes 1310720 | tf_op jit(solution)/shard_map/reduce_scatter | solution.py:62
  437.3 12.0 %copy-start.7 = (bf16[2,256,4,64]{1,0,3,2:T(2,128)(2,1)S(1)}, bf16[2,256,4,64]{1,0,3,2:T(2,128)(2,1)}, u32[]{:S(2)}) copy-start(bf16[2,256,4,64]{1,0,3,2:T(2,128)(2,1)} %reshape_reshape.14) | copy-start | bytes 786436
  477.2 8.3 %copy-start.4 = (bf16[32,8,2,256]{3,1,2,0:T(8,128)(2,1)}, bf16[32,8,2,256]{3,1,2,0:T(8,128)(2,1)S(1)}, u32[]{:S(2)}) copy-start(bf16[32,8,2,256]{3,1,2,0:T(8,128)(2,1)S(1)} %copy.107) | copy-start | bytes 786436
  516.1 4.2 copy-start.2
  520.3 2.9 copy-start.5
  522.9 76.1 %reduce-scatter.6.cloned.1.call-start = ((), (), s32[]{:S(2)}) async-start(), calls=%async_computation.13 | async-start | bytes 3538944 | tf_op jit(solution)/shard_map/reduce_scatter | solution.py:891
  526.4 1.2 copy-start.9
  526.4 2.7 copy-start.21
  526.4 2.7 copy-start.22
  526.4 44.3 %copy-start.17 = (f32[128,1024]{1,0:T(8,128)S(1)}, f32[128,1024]{1,0:T(8,128)}, u32[]{:S(2)}) copy-start(f32[128,1024]{1,0:T(8,128)} %get-tuple-element.25) | copy-start | bytes 1572868
  526.4 112.4 %copy-start.18 = (bf16[128,1024]{1,0:T(8,128)(2,1)S(1)}, bf16[128,1024]{1,0:T(8,128)(2,1)}, u32[]{:S(2)}) copy-start(bf16[128,1024]{1,0:T(8,128)(2,1)} %get-tuple-element.24) | copy-start | bytes 786436
  526.4 112.4 %reduce-scatter.8.cloned.1.call-start = ((), (), s32[]{:S(2)}) async-start(), calls=%async_computation.14 | async-start | bytes 1179648 | tf_op jit(solution)/shard_map/reduce_scatter | solution.py:892
  529.1 110.5 %copy-start.16 = (f32[128,1024]{1,0:T(8,128)S(1)}, f32[128,1024]{1,0:T(8,128)}, u32[]{:S(2)}) copy-start(f32[128,1024]{1,0:T(8,128)} %get-tuple-element.133) | copy-start | bytes 1572868
  529.1 111.3 %copy-start.15 = (f32[128,1024]{1,0:T(8,128)S(1)}, f32[128,1024]{1,0:T(8,128)}, u32[]{:S(2)}) copy-start(f32[128,1024]{1,0:T(8,128)} %get-tuple-element.134) | copy-start | bytes 1572868
Sparse Core Ops, SparseCore 0:
  9.7 30.6 all-gather.12
  42.8 25.1 all-gather.10
  71.0 36.4 all-gather.16
  141.7 33.6 all-gather.14
  176.8 51.5 all-gather.18
  369.5 29.3 all-gather.20
  401.3 35.9 all-gather.22
  439.8 27.8 all-gather.24
  523.0 27.3 reduce-scatter.3
  554.0 44.9 reduce-scatter.5
  602.8 36.0 reduce-scatter.7

commit v2 on v1

--- a/solution.py
+++ b/solution.py
@@ -455,6 +455,71 @@
     return (grad - centre - unit * along) * scale
 
 
+def send_or_copy(src, dst, send_sem, recv_sem, device, own):
+    def away():
+        remote(src, dst, send_sem, recv_sem, device).start()
+
+    if own is None:
+        away()
+        return
+    pl.when(jnp.logical_not(own))(away)
+
+    @pl.when(own)
+    def _():
+        pltpu.make_async_copy(src, dst, recv_sem).start()
+
+
+def push_weights(at, src, dst, send_sem, recv_sem):
+    rows, cols = lanes(at.b), lanes(at.z)
+    flat = at.b * 4 + at.z
+    pltpu.make_async_copy(src.at[:, lanes(at.b)], dst.at[rows, cols], recv_sem).start()
+
+    def push(step, carry):
+        other = (flat + step) % 32
+        remote(
+            src.at[:, lanes(other // 4)],
+            dst.at[rows, cols],
+            send_sem,
+            recv_sem,
+            (other // 4, other % 4),
+        ).start()
+        return carry
+
+    lax.fori_loop(1, 32, push, 0)
+
+
+def push_grads(at, blocks, into, send_sem, recv_sem):
+    def one(step, carry):
+        other = (at.b + step) % 8
+        for k in range(4):
+            plane = (at.z + k) % 4
+            send_or_copy(
+                blocks.at[other, :, lanes(plane)],
+                into.at[at.z, :, lanes(at.b)],
+                send_sem,
+                recv_sem,
+                (other, plane),
+                step == 0 if k == 0 else None,
+            )
+        return carry
+
+    lax.fori_loop(0, 8, one, 0)
+
+
+def take_grads(into, dest, recv_sem):
+    wait_bytes(into, recv_sem)
+
+    def add(rows):
+        dest[rows] = (
+            into[0, rows].astype(F32)
+            + into[1, rows].astype(F32)
+            + into[2, rows].astype(F32)
+            + into[3, rows].astype(F32)
+        )
+
+    by_rows(128, 32, add)
+
+
 def ffn_kernel(
     x_ref,
     att_ref,
@@ -462,16 +527,16 @@
     cot_ref,
     par_ref,
     bin_ref,
-    win_ref,
+    wi,
     wback_ref,
     out_ref,
     d1_ref,
     db_ref,
-    gwin_ref,
+    da_ref,
+    gin_ref,
     gwback_ref,
     pg_ref,
     gbin_ref,
-    wi,
     wb,
     n1,
     unit1,
@@ -488,8 +553,8 @@
     peer_out,
     peer_in,
     gsend,
-    grecv_in,
     grecv_back,
+    da_send,
     send,
     recv,
     send_sib,
@@ -498,32 +563,14 @@
     w_recv,
     g_send,
     g_recv,
+    a_send,
+    a_recv,
 ):
     at = Place()
     flat = at.b * 4 + at.z
     greet_all(at)
 
-    mine_rows = lanes(at.b)
-    mine_cols = lanes(at.z)
-    local = []
-    for k, (src, dst) in enumerate(((win_ref, wi), (wback_ref, wb))):
-        cp = pltpu.make_async_copy(
-            src.at[:, lanes(at.b)], dst.at[mine_rows, mine_cols], w_recv.at[k]
-        )
-        cp.start()
-
-        def push(step, carry, src=src, dst=dst, k=k):
-            other = (flat + step) % 32
-            remote(
-                src.at[:, lanes(other // 4)],
-                dst.at[mine_rows, mine_cols],
-                w_send.at[k],
-                w_recv.at[k],
-                (other // 4, other % 4),
-            ).start()
-            return carry
-
-        lax.fori_loop(1, 32, push, 0)
+    push_weights(at, wback_ref, wb, w_send, w_recv)
 
     def param(i):
         return par_ref[i : i + 1, :]
@@ -541,8 +588,7 @@
     gather = Exchange(at, send.at[0], recv.at[0], send_sib.at[0], recv_sib.at[0])
     gather.gather_start(norm_slots)
 
-    wait_bytes(wi, w_recv.at[0])
-    wait_bytes(wb, w_recv.at[1])
+    wait_bytes(wb, w_recv)
 
     scatter = Exchange(at, send.at[1], recv.at[1], send_sib.at[1], recv_sib.at[1])
     for r in range(4):
@@ -615,38 +661,20 @@
     scatter2.scatter_pass(terms, sib_in.at[1], peer_out.at[1], peer_in.at[1], 3)
     gbin_ref[...] = gbin
 
-    def weight_grad(slots, right, which, into):
+    def weight_grad(slots, right, into):
         def one(step, carry):
             other = (at.b + step) % 8
             total = jnp.zeros((128, 512), F32)
             for r in range(4):
                 total += contract_rows(slots[at.chip(r), :, lanes(other)], right(r))
-            gsend[which, other] = total.astype(BF16)
-            for k in range(4):
-                plane = (at.z + k) % 4
-                src = gsend.at[which, other, :, lanes(plane)]
-                dst = into.at[at.z, :, lanes(at.b)]
-
-                def away():
-                    remote(
-                        src, dst, g_send.at[which], g_recv.at[which], (other, plane)
-                    ).start()
-
-                if k:
-                    away()
-                else:
-                    pl.when(step != 0)(away)
-
-                    @pl.when(step == 0)
-                    def _():
-                        pltpu.make_async_copy(src, dst, g_recv.at[which]).start()
-
+            into[other] = total.astype(BF16)
             return carry
 
         lax.fori_loop(0, 8, one, 0)
 
-    weight_grad(grad_slots, lambda r: hid[r], 1, grecv_back)
-    weight_grad(norm_slots, lambda r: slope[r].astype(BF16), 0, grecv_in)
+    weight_grad(grad_slots, lambda r: hid[r], gsend)
+    push_grads(at, gsend, grecv_back, g_send, g_recv)
+    weight_grad(norm_slots, lambda r: slope[r].astype(BF16), gin_ref)
 
     scatter2.scatter_arrive(peer_in.at[1])
 
@@ -673,80 +701,698 @@
     pg_ref[2:3, :] = sums[2]
     pg_ref[0:2, :] = jnp.zeros((2, 1024), F32)
 
-    for which, into, dest in ((1, grecv_back, gwback_ref), (0, grecv_in, gwin_ref)):
-        wait_bytes(into, g_recv.at[which])
-
-        def add(rows, into=into, dest=dest):
-            dest[rows] = (
-                into[0, rows].astype(F32)
-                + into[1, rows].astype(F32)
-                + into[2, rows].astype(F32)
-                + into[3, rows].astype(F32)
+    da_send[...] = contract_cols(db_ref[...], wo_ref[...]).astype(BF16)
+    place = at.q * 4 + at.z
+
+    def give(step, carry):
+        for k in range(4):
+            chip = (at.q + step) % 4
+            plane = (at.z + k) % 4
+            pair = 4 * (plane // 2) + chip
+            src = da_send.at[pl.ds(pl.multiple_of((plane % 2) * 64, 64), 64), lanes(pair)]
+            dst = da_ref.at[pl.ds(pl.multiple_of(place * 64, 64), 64)]
+            send_or_copy(
+                src, dst, a_send, a_recv, (2 * chip + at.c, plane), step == 0 if k == 0 else None
             )
-
-        by_rows(128, 32, add)
+        return carry
+
+    lax.fori_loop(0, 4, give, 0)
+    wait_bytes(da_ref, a_recv)
+    wait_bytes(da_ref.at[pl.ds(0, 960)], a_send)
+    take_grads(grecv_back, gwback_ref, g_recv)
 
     gather.gather_end(norm_slots)
     gather2.gather_end(grad_slots)
     scatter2.scatter_end(sib_out.at[1], peer_out.at[1])
-    for k in range(2):
-        wait_bytes(wi.at[pl.ds(0, 992)], w_send.at[k])
-        wait_bytes(wi.at[pl.ds(0, 992)], g_send.at[k])
+    wait_bytes(wb.at[pl.ds(0, 992)], w_send)
+    wait_bytes(wb.at[pl.ds(0, 992)], g_send)
 
 
 def vmem():
     return pl.BlockSpec(memory_space=pltpu.VMEM)
 
 
-def run_ffn(x, att, wo, cot, par, bins, win, wback):
+DMA = pltpu.SemaphoreType.DMA
+
+
+def head_mask(h):
+    lane = lax.broadcasted_iota(jnp.int32, (1, 128), 1)
+    return jnp.where(lane // HEAD_DIM == h, 1.0, 0.0).astype(F32)
+
+
+def slot_rows(index):
+    return pl.ds(pl.multiple_of(index * 64, 64), 64)
+
+
+def chip_rows(index):
+    return pl.ds(pl.multiple_of(index * 256, 256), 256)
+
+
+def core_rows(index):
+    return pl.ds(pl.multiple_of(index * 1024, 1024), 1024)
+
+
+def attend_kernel(
+    x_ref,
+    wq_ref,
+    wk_ref,
+    wv_ref,
+    wout_ref,
+    small_ref,
+    win_ref,
+    xs,
+    wqkv,
+    queries,
+    keys_all,
+    values_all,
+    mixed,
+    log_sums,
+    att,
+    wo,
+    par,
+    bins,
+    wi,
+    smalls,
+    proj,
+    scores,
+    att_send,
+    z_send,
+    z_recv,
+    p_send,
+    p_recv,
+    w_send,
+    w_recv,
+    o_send,
+    o_recv,
+    k_send,
+    k_recv,
+    misc_send,
+    misc_recv,
+):
+    at = Place()
+    flat = at.b * 4 + at.z
+    place = at.q * 4 + at.z
+    parity = at.z % 2
+    greet_all(at)
+
+    for dz in (1, 3, 2):
+        plane = (at.z + dz) % 4
+        remote(
+            x_ref.at[slot_rows(plane % 2)],
+            xs.at[slot_rows(place)],
+            z_send.at[dz],
+            z_recv.at[dz],
+            (at.b, plane),
+        ).start()
+    own = pltpu.make_async_copy(x_ref.at[slot_rows(parity)], xs.at[slot_rows(place)], z_recv.at[0])
+    own.start()
+
+    for dx in range(2):
+        for dz in range(2):
+            column = (at.x + dx) % 2
+            plane = 2 * (at.z // 2) + (at.z + dz) % 2
+            target = 2 * (parity * 2 + column) + at.c
+            mine = jnp.logical_and(
+                parity == at.y, jnp.logical_and(column == at.x, plane == at.z)
+            )
+            for k, w in enumerate((wq_ref, wk_ref, wv_ref)):
+                send_or_copy(
+                    w.at[:, lanes(column)],
+                    wqkv.at[lanes(at.b), pl.ds(k * 128, 128)],
+                    w_send.at[0],
+                    w_recv.at[0],
+                    (target, plane),
+                    mine if dx == 0 and dz == 0 else None,
+                )
+
+    pltpu.make_async_copy(small_ref, smalls.at[flat], misc_recv.at[0]).start()
+
+    def spread(step, carry):
+        other = (flat + step) % 32
+        remote(
+            small_ref,
+            smalls.at[flat],
+            misc_send.at[0],
+            misc_recv.at[0],
+            (other // 4, other % 4),
+        ).start()
+        return carry
+
+    lax.fori_loop(1, 32, spread, 0)
+
+    col = wo.at[pl.ds(pl.multiple_of(at.z * 256, 256), 256), lanes(at.b)]
+    pltpu.make_async_copy(wout_ref, col, o_recv.at[0]).start()
+    for dz in range(1, 4):
+        remote(
+            wout_ref, col, o_send.at[0], o_recv.at[0], (at.b, (at.z + dz) % 4)
+        ).start()
+
+    for dz in (0, 1, 3, 2):
+        block = xs.at[slot_rows(at.q * 4 + (at.z - dz + 4) % 4)]
+        wait_bytes(block, z_recv.at[dz])
+        for r in (1, 2, 3):
+            remote(block, block, p_send.at[r, dz], p_recv.at[r, dz], at.peer(r)).start()
+
+    wait_bytes(wqkv.at[pl.ds(0, 512)], w_recv.at[0])
+    for r in range(4):
+        part = wqkv.at[lanes(2 * at.chip(r) + at.c)]
+        remote(part, part, w_send.at[1], w_recv.at[1], at.sibling()).start()
+
+    wait_bytes(smalls, misc_recv.at[0])
+    for b in range(8):
+        total = smalls[4 * b].astype(F32)
+        for z in range(1, 4):
+            total += smalls[4 * b + z].astype(F32)
+        par[:, 128 * b : 128 * b + 128] = total[0:8]
+    for h in range(4):
+        bins[0:1, 128 * h : 128 * h + 128] = smalls[8 * h + at.b].astype(F32)[8:9]
+    pair = 4 * (at.z // 2) + at.q
+    bias_q = par[0:1, lanes(pair)]
+    bias_v = par[1:2, lanes(pair)]
+    wait_bytes(wqkv.at[pl.ds(0, 512)], w_recv.at[1])
+
+    for r in range(4):
+        chip = at.chip(r)
+        if r:
+            for dz in (0, 1, 3, 2):
+                wait_bytes(xs.at[slot_rows(0)], p_recv.at[r, dz])
+        rows = chip_rows(chip)
+        proj[...] = dot_nn(xs[rows], wqkv[...])
+        queries[rows] = (proj[:, 0:128] + bias_q).astype(BF16)
+        own_rows = chip_rows(at.c * 4 + chip)
+        keys_all[own_rows] = proj[:, 128:256].astype(BF16)
+        values_all[own_rows] = (proj[:, 256:384] + bias_v).astype(BF16)
+        for k, ref in enumerate((keys_all, values_all)):
+            view = ref.at[own_rows]
+            remote(view, view, k_send.at[k, r], k_recv.at[k, r], at.sibling()).start()
+
+    whole = wo.at[:, lanes(at.b)]
+    wait_bytes(whole, o_recv.at[0])
+    for r in (1, 2, 3):
+        remote(whole, whole, o_send.at[r], o_recv.at[r], at.peer(r)).start()
+    remote(whole, whole, o_send.at[4], o_recv.at[4], at.sibling()).start()
+    push_weights(at, win_ref, wi, misc_send.at[1], misc_recv.at[1])
+
+    for r in range(4):
+        for k, ref in enumerate((keys_all, values_all)):
+            wait_bytes(ref.at[pl.ds(0, 256)], k_recv.at[k, r])
+
+    sequence = parity
+
+    def attend(step, carry):
+        chip = (at.q + 1 + step) % 4
+        rows = chip_rows(chip)
+        outs = []
+        logs = []
+        for h in range(2):
+            q = (queries[rows].astype(F32) * head_mask(h) * HEAD_DIM**-0.5).astype(BF16)
+            scores[...] = contract_cols(q, keys_all[...])
+            top = jnp.max(scores[...], axis=-1, keepdims=True)
+            weights = jnp.exp(scores[...] - top)
+            total = jnp.sum(weights, axis=-1, keepdims=True)
+            outs.append(dot_nn(weights.astype(BF16), values_all[...]) / total)
+            logs.append(top + jnp.log(total))
+        first = head_mask(0) > 0.5
+        merged = jnp.where(first, outs[0], outs[1])
+        mixed[rows] = merged
+        log_sums[rows] = jnp.where(first, logs[0], logs[1])
+        att_send[rows] = merged.astype(BF16)
+        for k in range(4):
+            plane = (at.z + 1 + k) % 4
+            send_or_copy(
+                att_send.at[slot_rows(chip * 4 + plane)],
+                att.at[slot_rows(sequence), lanes(pair)],
+                misc_send.at[2],
+                misc_recv.at[2],
+                (2 * chip + at.c, plane),
+                step == 3 if k == 3 else None,
+            )
+        return carry
+
+    lax.fori_loop(0, 4, attend, 0)
+
+    for r in (1, 2, 3):
+        part = wo.at[:, lanes(2 * at.chip(r) + at.c)]
+        wait_bytes(part, o_recv.at[r])
+        remote(part, part, o_send.at[4 + r], o_recv.at[4 + r], at.sibling()).start()
+    for r in range(4):
+        wait_bytes(whole, o_recv.at[4 + r])
+    wait_bytes(wi, misc_recv.at[1])
+    wait_bytes(att, misc_recv.at[2])
+
+    for dz in range(1, 4):
+        wait_bytes(xs.at[slot_rows(0)], z_send.at[dz])
+    for r in (1, 2, 3):
+        for dz in range(4):
+            wait_bytes(xs.at[slot_rows(0)], p_send.at[r, dz])
+    away = jnp.logical_not(parity == at.y)
+
+    @pl.when(away)
+    def _():
+        wait_bytes(wqkv.at[pl.ds(0, 512)], w_send.at[0])
+
+    @pl.when(jnp.logical_not(away))
+    def _():
+        wait_bytes(wqkv.at[pl.ds(0, 384)], w_send.at[0])
+
+    wait_bytes(wqkv.at[pl.ds(0, 512)], w_send.at[1])
+    wait_bytes(smalls.at[pl.ds(0, 31)], misc_send.at[0])
+    wait_bytes(wo.at[pl.ds(0, 768), pl.ds(0, 128)], o_send.at[0])
+    for r in range(1, 8):
+        wait_bytes(whole, o_send.at[r])
+    for r in range(4):
+        for k in range(2):
+            wait_bytes(keys_all.at[pl.ds(0, 256)], k_send.at[k, r])
+    wait_bytes(wi.at[pl.ds(0, 992)], misc_send.at[1])
+    wait_bytes(att_send.at[pl.ds(0, 960)], misc_send.at[2])
+
+
+def grads_kernel(
+    xs,
+    wqkv,
+    queries,
+    keys_all,
+    values_all,
+    mixed,
+    log_sums,
+    da_ref,
+    d1_ref,
+    att,
+    db_ref,
+    pg_ref,
+    gbin_ref,
+    gin_ref,
+    gtok_ref,
+    gq_ref,
+    gk_ref,
+    gv_ref,
+    gout_ref,
+    gwin_ref,
+    small_ref,
+    q_turned,
+    da_turned,
+    s_buf,
+    p_buf,
+    d_buf,
+    dq,
+    dk_turned,
+    dv_turned,
+    dk,
+    dv,
+    sib_k,
+    sib_v,
+    dqkv,
+    terms,
+    x_out,
+    x_in,
+    x_sum,
+    x_own,
+    z_out,
+    z_in,
+    w_sib_out,
+    w_sib_in,
+    w_out,
+    w_in,
+    sib_out,
+    sib_in,
+    peer_out,
+    peer_in,
+    o_out,
+    o_in,
+    vec,
+    notes,
+    notes_in,
+    grecv,
+    kv_send,
+    kv_recv,
+    x_send,
+    x_recv,
+    z_send,
+    z_recv,
+    ws_send,
+    ws_recv,
+    send,
+    recv,
+    send_sib,
+    recv_sib,
+    o_send,
+    o_recv,
+    misc_send,
+    misc_recv,
+):
+    at = Place()
+    flat = at.b * 4 + at.z
+    parity = at.z % 2
+    pair = 4 * (at.z // 2) + at.q
+    greet_all(at)
+
+    push_grads(at, gin_ref, grecv, misc_send.at[0], misc_recv.at[0])
+
+    out_scatter = Exchange(at, send, recv, send_sib, recv_sib)
+    for r in range(4):
+        terms[r] = contract_rows(db_ref[:, chip_rows(at.chip(r))], att[...])
+        out_scatter.scatter_put(terms, sib_out, sib_in, r)
+
+    q_turned[...] = queries[...].astype(F32).T.astype(BF16)
+    da_turned[...] = da_ref[...].astype(F32).T.astype(BF16)
+    dk_turned[...] = jnp.zeros_like(dk_turned)
+    dv_turned[...] = jnp.zeros_like(dv_turned)
+
+    def attend(step, carry):
+        rows = chip_rows(step)
+        parts = []
+        for h in range(2):
+            mask = head_mask(h)
+            grad = da_ref[rows].astype(F32) * mask
+            delta = jnp.sum(grad * mixed[rows], axis=-1, keepdims=True)
+            q = (queries[rows].astype(F32) * mask * HEAD_DIM**-0.5).astype(BF16)
+            s_buf[...] = contract_cols(q, keys_all[...])
+            d_buf[...] = contract_cols(grad.astype(BF16), values_all[...])
+            logs = log_sums[rows][:, h * HEAD_DIM : h * HEAD_DIM + 1]
+            probs = jnp.exp(s_buf[...] - logs)
+            p_buf[...] = probs.astype(BF16)
+            low = (probs * (d_buf[...] - delta)).astype(BF16)
+            band = pl.ds(h * HEAD_DIM, HEAD_DIM)
+            dv_turned[band] += dot_nn(da_turned[band, rows], p_buf[...])
+            dk_turned[band] += dot_nn(q_turned[band, rows], low)
+            parts.append(dot_nn(low, keys_all[...]))
+        dq[rows] = jnp.where(head_mask(0) > 0.5, parts[0], parts[1]) * HEAD_DIM**-0.5
+        return carry
+
+    lax.fori_loop(0, 4, attend, 0)
+    for r in range(4):
+        out_scatter.scatter_pass(terms, sib_in, peer_out, peer_in, r)
+
+    dk[...] = dk_turned[...].T * HEAD_DIM**-0.5
+    dv[...] = dv_turned[...].T
+    other = core_rows(1 - at.c)
+    mine = core_rows(at.c)
+    for k, (ref, into) in enumerate(((dk, sib_k), (dv, sib_v))):
+        remote(ref.at[other], into, kv_send.at[k], kv_recv.at[k], at.sibling()).start()
+    low = dq[...].astype(BF16)
+    dqkv[:, 0:128] = low
+    vec[...] = pg_ref[...]
+    vec[0:1, lanes(pair)] = jnp.sum(low.astype(F32), axis=0, keepdims=True)
+    wait_bytes(sib_k, kv_recv.at[0])
+    dqkv[:, 128:256] = (dk[mine] + sib_k[...]).astype(BF16)
+    wait_bytes(sib_v, kv_recv.at[1])
+    low = (dv[mine] + sib_v[...]).astype(BF16)
+    dqkv[:, 256:384] = low
+    vec[1:2, lanes(pair)] = jnp.sum(low.astype(F32), axis=0, keepdims=True)
+
+    for r in (3, 1, 2, 0):
+        part = contract_cols(dqkv[chip_rows(at.chip(r))], wqkv[...])
+        if r:
+            x_out[r] = part.astype(BF16)
+            remote(x_out.at[r], x_in.at[r], x_send.at[r], x_recv.at[r], at.peer(r)).start()
+        else:
+            x_sum[...] = part
+
+    for d in range(32):
+        notes[d, 0:8] = vec[:, 128 * (d // 4) : 128 * (d // 4) + 128]
+        notes[d, 8:16] = jnp.zeros((8, 128), F32)
+    for h in range(4):
+        notes[8 * h + at.b, 8:9] = gbin_ref[0:1, 128 * h : 128 * h + 128]
+    pltpu.make_async_copy(notes.at[flat], notes_in.at[flat], misc_recv.at[1]).start()
+
+    def spread(step, carry):
+        to = (flat + step) % 32
+        remote(
+            notes.at[to],
+            notes_in.at[flat],
+            misc_send.at[1],
+            misc_recv.at[1],
+            (to // 4, to % 4),
+        ).start()
+        return carry
+
+    lax.fori_loop(1, 32, spread, 0)
+
+    def features(b):
+        return contract_rows(xs[:, lanes(b)], dqkv[...])
+
+    for r in range(4):
+        w_sib_out[r] = features(2 * at.chip(r) + 1 - at.c)
+        remote(
+            w_sib_out.at[r], w_sib_in.at[r], ws_send.at[r], ws_recv.at[r], at.sibling()
+        ).start()
+    plane_w = 2 * (at.z // 2) + at.y
+    for r in range(4):
+        total = features(2 * at.chip(r) + at.c)
+        wait_bytes(w_sib_in.at[r], ws_recv.at[r])
+        w_out[r] = (total + w_sib_in[r]).astype(BF16)
+        send_or_copy(
+            w_out.at[r],
+            w_in.at[parity, at.x],
+            misc_send.at[2],
+            misc_recv.at[2],
+            at.peer(r)[:1] + (plane_w,),
+            plane_w == at.z if r == 0 else None,
+        )
+
+    out_scatter.scatter_arrive(peer_in)
+
+    def out_rows(rows):
+        own = pl.ds(pl.multiple_of(at.c * 128 + rows.start, 32), 32)
+        total = (
+            terms[0, own]
+            + peer_in[1, rows].astype(F32)
+            + peer_in[2, rows].astype(F32)
+            + peer_in[3, rows].astype(F32)
+        )
+        o_out[rows] = total.astype(BF16)
+
+    by_rows(128, 32, out_rows)
+    wide = pl.ds(pl.multiple_of(at.z * 256, 256), 256)
+    pltpu.make_async_copy(o_out.at[:, wide], o_in.at[0], o_recv).start()
+    for dz in range(1, 4):
+        plane = (at.z + dz) % 4
+        remote(
+            o_out.at[:, pl.ds(pl.multiple_of(plane * 256, 256), 256)],
+            o_in.at[dz],
+            o_send,
+            o_recv,
+            (at.b, plane),
+        ).start()
+
+    for r in (1, 2, 3):
+        wait_bytes(x_in.at[r], x_recv.at[r])
+    for dz in (2, 1, 3, 0):
+        plane = (at.z + dz) % 4
+        rows = slot_rows(plane)
+        total = (
+            x_sum[rows]
+            + x_in[1, rows].astype(F32)
+            + x_in[2, rows].astype(F32)
+            + x_in[3, rows].astype(F32)
+        )
+        if dz:
+            z_out[dz] = total.astype(BF16)
+            remote(
+                z_out.at[dz], z_in.at[dz], z_send.at[dz], z_recv.at[dz], (at.b, plane)
+            ).start()
+        else:
+            x_own[...] = total
+    for dz in (1, 2, 3):
+        wait_bytes(z_in.at[dz], z_recv.at[dz])
+    same = slot_rows(parity)
+    gtok_ref[same] = (d1_ref[same] + x_own[...] + z_in[2].astype(F32)).astype(BF16)
+    cross = slot_rows(1 - parity)
+    gtok_ref[cross] = (d1_ref[cross] + z_in[1].astype(F32) + z_in[3].astype(F32)).astype(BF16)
+
+    wait_bytes(o_in, o_recv)
+    gout_ref[...] = (
+        o_in[0].astype(F32) + o_in[1].astype(F32) + o_in[2].astype(F32) + o_in[3].astype(F32)
+    )
+    wait_bytes(w_in, misc_recv.at[2])
+    for x in range(2):
+        total = w_in[0, x].astype(F32) + w_in[1, x].astype(F32)
+        for k, ref in enumerate((gq_ref, gk_ref, gv_ref)):
+            ref[:, 128 * x : 128 * x + 128] = total[:, 128 * k : 128 * k + 128]
+    wait_bytes(notes_in, misc_recv.at[1])
+    total = notes_in[0]
+    for d in range(1, 32):
+        total += notes_in[d]
+    small_ref[...] = total
+    take_grads(grecv, gwin_ref, misc_recv.at[0])
+
+    for k in range(2):
+        wait_bytes(sib_k, kv_send.at[k])
+    out_scatter.scatter_end(sib_out, peer_out)
+    wait_bytes(o_in.at[pl.ds(0, 3)], o_send)
+    for r in range(4):
+        wait_bytes(w_sib_out.at[r], ws_send.at[r])
+        if r:
+            wait_bytes(x_out.at[r], x_send.at[r])
+            wait_bytes(z_out.at[r], z_send.at[r])
+    wait_bytes(xs.at[pl.ds(0, 496)], misc_send.at[0])
+    wait_bytes(notes.at[pl.ds(0, 31)], misc_send.at[1])
+
+    @pl.when(plane_w == at.z)
+    def _():
+        wait_bytes(w_out.at[pl.ds(0, 3)], misc_send.at[2])
+
+    @pl.when(plane_w != at.z)
+    def _():
+        wait_bytes(w_out, misc_send.at[2])
+
+
+def run_kernel(body, shapes, scratch, ident, args):
+    return pl.pallas_call(
+        body,
+        out_shape=[jax.ShapeDtypeStruct(s, t) for s, t in shapes],
+        in_specs=[vmem()] * len(args),
+        out_specs=[vmem()] * len(shapes),
+        scratch_shapes=scratch,
+        compiler_params=pltpu.CompilerParams(
+            collective_id=ident, has_side_effects=True, vmem_limit_bytes=VMEM_LIMIT
+        ),
+    )(*args)
+
+
+def run_attend(*args):
+    shapes = (
+        ((1024, 1024), BF16),
+        ((1024, 384), BF16),
+        ((1024, 128), BF16),
+        ((2048, 128), BF16),
+        ((2048, 128), BF16),
+        ((1024, 128), F32),
+        ((1024, 128), F32),
+        ((128, 1024), BF16),
+        ((1024, 1024), BF16),
+        ((8, 1024), F32),
+        ((1, 512), F32),
+        ((1024, 512), BF16),
+    )
+    scratch = [
+        pltpu.VMEM((32, 16, 128), BF16),
+        pltpu.VMEM((256, 384), F32),
+        pltpu.VMEM((256, 2048), F32),
+        pltpu.VMEM((1024, 128), BF16),
+        DMA((4,)),
+        DMA((4,)),
+        DMA((4, 4)),
+        DMA((4, 4)),
+        DMA((2,)),
+        DMA((2,)),
+        DMA((8,)),
+        DMA((8,)),
+        DMA((2, 4)),
+        DMA((2, 4)),
+        DMA((3,)),
+        DMA((3,)),
+    ]
+    return run_kernel(attend_kernel, shapes, scratch, 1, args)
+
+
+def run_ffn(*args):
     shapes = (
         ((128, 1024), BF16),
         ((128, 1024), F32),
         ((128, 1024), BF16),
-        ((128, 1024), F32),
+        ((1024, 128), BF16),
+        ((8, 128, 512), BF16),
         ((128, 1024), F32),
         ((8, 1024), F32),
         ((1, 512), F32),
     )
-    dma = pltpu.SemaphoreType.DMA
-    return pl.pallas_call(
-        ffn_kernel,
-        out_shape=[jax.ShapeDtypeStruct(s, t) for s, t in shapes],
-        in_specs=[vmem()] * 8,
-        out_specs=[vmem()] * 7,
-        scratch_shapes=[
-            pltpu.VMEM((1024, 512), BF16),
-            pltpu.VMEM((1024, 512), BF16),
-            pltpu.VMEM((128, 1024), F32),
-            pltpu.VMEM((128, 1024), F32),
-            pltpu.VMEM((128, 128), F32),
-            pltpu.VMEM((128, 1024), F32),
-            pltpu.VMEM((4, 256, 1024), BF16),
-            pltpu.VMEM((4, 256, 1024), BF16),
-            pltpu.VMEM((4, 256, 512), BF16),
-            pltpu.VMEM((4, 256, 512), F32),
-            pltpu.VMEM((256, 512), F32),
-            pltpu.VMEM((4, 256, 1024), F32),
-            pltpu.VMEM((2, 4, 128, 1024), BF16),
-            pltpu.VMEM((2, 4, 128, 1024), BF16),
-            pltpu.VMEM((2, 4, 128, 1024), BF16),
-            pltpu.VMEM((2, 4, 128, 1024), BF16),
-            pltpu.VMEM((2, 8, 128, 512), BF16),
-            pltpu.VMEM((4, 128, 1024), BF16),
-            pltpu.VMEM((4, 128, 1024), BF16),
-            dma((4, 4)),
-            dma((4, 4)),
-            dma((4, 4)),
-            dma((4, 4)),
-            dma((2,)),
-            dma((2,)),
-            dma((2,)),
-            dma((2,)),
-        ],
-        compiler_params=pltpu.CompilerParams(
-            collective_id=1, has_side_effects=True, vmem_limit_bytes=VMEM_LIMIT
-        ),
-    )(x, att, wo, cot, par, bins, win, wback)
+    scratch = [
+        pltpu.VMEM((1024, 512), BF16),
+        pltpu.VMEM((128, 1024), F32),
+        pltpu.VMEM((128, 1024), F32),
+        pltpu.VMEM((128, 128), F32),
+        pltpu.VMEM((128, 1024), F32),
+        pltpu.VMEM((4, 256, 1024), BF16),
+        pltpu.VMEM((4, 256, 1024), BF16),
+        pltpu.VMEM((4, 256, 512), BF16),
+        pltpu.VMEM((4, 256, 512), F32),
+        pltpu.VMEM((256, 512), F32),
+        pltpu.VMEM((4, 256, 1024), F32),
+        pltpu.VMEM((2, 4, 128, 1024), BF16),
+        pltpu.VMEM((2, 4, 128, 1024), BF16),
+        pltpu.VMEM((2, 4, 128, 1024), BF16),
+        pltpu.VMEM((2, 4, 128, 1024), BF16),
+        pltpu.VMEM((8, 128, 512), BF16),
+        pltpu.VMEM((4, 128, 1024), BF16),
+        pltpu.VMEM((128, 1024), BF16),
+        DMA((4, 4)),
+        DMA((4, 4)),
+        DMA((4, 4)),
+        DMA((4, 4)),
+        DMA,
+        DMA,
+        DMA,
+        DMA,
+        DMA,
+        DMA,
+    ]
+    return run_kernel(ffn_kernel, shapes, scratch, 2, args)
+
+
+def run_grads(*args):
+    shapes = (
+        ((128, 1024), BF16),
+        ((128, 256), F32),
+        ((128, 256), F32),
+        ((128, 256), F32),
+        ((128, 256), F32),
+        ((128, 1024), F32),
+        ((16, 128), F32),
+    )
+    scratch = [
+        pltpu.VMEM((128, 1024), BF16),
+        pltpu.VMEM((128, 1024), BF16),
+        pltpu.VMEM((256, 2048), F32),
+        pltpu.VMEM((256, 2048), BF16),
+        pltpu.VMEM((256, 2048), F32),
+        pltpu.VMEM((1024, 128), F32),
+        pltpu.VMEM((128, 2048), F32),
+        pltpu.VMEM((128, 2048), F32),
+        pltpu.VMEM((2048, 128), F32),
+        pltpu.VMEM((2048, 128), F32),
+        pltpu.VMEM((1024, 128), F32),
+        pltpu.VMEM((1024, 128), F32),
+        pltpu.VMEM((1024, 384), BF16),
+        pltpu.VMEM((4, 256, 1024), F32),
+        pltpu.VMEM((4, 256, 1024), BF16),
+        pltpu.VMEM((4, 256, 1024), BF16),
+        pltpu.VMEM((256, 1024), F32),
+        pltpu.VMEM((64, 1024), F32),
+        pltpu.VMEM((4, 64, 1024), BF16),
+        pltpu.VMEM((4, 64, 1024), BF16),
+        pltpu.VMEM((4, 128, 384), F32),
+        pltpu.VMEM((4, 128, 384), F32),
+        pltpu.VMEM((4, 128, 384), BF16),
+        pltpu.VMEM((2, 2, 128, 384), BF16),
+        pltpu.VMEM((4, 128, 1024), BF16),
+        pltpu.VMEM((4, 128, 1024), BF16),
+        pltpu.VMEM((4, 128, 1024), BF16),
+        pltpu.VMEM((4, 128, 1024), BF16),
+        pltpu.VMEM((128, 1024), BF16),
+        pltpu.VMEM((4, 128, 256), BF16),
+        pltpu.VMEM((8, 1024), F32),
+        pltpu.VMEM((32, 16, 128), F32),
+        pltpu.VMEM((32, 16, 128), F32),
+        pltpu.VMEM((4, 128, 1024), BF16),
+        DMA((2,)),
+        DMA((2,)),
+        DMA((4,)),
+        DMA((4,)),
+        DMA((4,)),
+        DMA((4,)),
+        DMA((4,)),
+        DMA((4,)),
+        DMA((4,)),
+        DMA((4,)),
+        DMA((4,)),
+        DMA((4,)),
+        DMA,
+        DMA,
+        DMA((3,)),
+        DMA((3,)),
+    ]
+    return run_kernel(grads_kernel, shapes, scratch, 3, args)
 
 
 def fast_device(
@@ -768,157 +1414,60 @@
     norm2_shift,
     cotangent,
 ):
-    f32 = jnp.float32
-    bf16 = jnp.bfloat16
-    score_scale = HEAD_DIM ** (-0.5)
-    b_id = lax.axis_index("blk")
-    small = jnp.concatenate(
-        (b_query, b_value, b_out, norm1_gain, norm1_shift, b_back, norm2_gain, norm2_shift, b_in)
-    )
-    smalls = lax.all_gather(small, ("blk", "head"), axis=0)
-    vectors = smalls[:, :256].reshape(32, 8, 32).transpose(1, 0, 2).reshape(8, 1024).astype(f32)
-    bin_full = smalls[:, 256:].reshape(4, 8, 128)
-    bins = lax.dynamic_index_in_dim(bin_full, b_id, 1, False).reshape(1, 512).astype(f32)
-    attn_cols, out_rows = (
-        lax.all_gather(jnp.stack((w_query, w_key, w_value)), "blk", axis=1, tiled=True),
-        lax.all_gather(w_out, "blk", axis=1, tiled=True),
-    )
-    seq_count, local_len, model_dim = tokens.shape
-    token_shape = (seq_count, local_len, model_dim)
     head_id = lax.axis_index("head")
-    width_part = attn_cols.shape[2]
-    bq_part = lax.dynamic_slice_in_dim(vectors[0], head_id * width_part, width_part)
-    bv_part = lax.dynamic_slice_in_dim(vectors[1], head_id * width_part, width_part)
-    wide_rows = token_rows(tokens)
-    wide_len = wide_rows.shape[1]
-    wide_flat = wide_rows.reshape(-1, model_dim)
-    head_shape = (seq_count, wide_len, width_part)
-    wide_shape = (seq_count, wide_len, model_dim)
-    query_heads = (
-        (jnp.dot(wide_flat, attn_cols[0], preferred_element_type=f32) + bq_part)
-        .astype(bf16)
-        .reshape(head_shape)
-    )
-    key_heads = (
-        jnp.dot(wide_flat, attn_cols[1], preferred_element_type=f32)
-        .astype(bf16)
-        .reshape(head_shape)
-    )
-    value_heads = (
-        (jnp.dot(wide_flat, attn_cols[2], preferred_element_type=f32) + bv_part)
-        .astype(bf16)
-        .reshape(head_shape)
-    )
-    query4 = split_heads(query_heads)
-    key4 = split_heads(key_heads)
-    value4 = split_heads(value_heads)
-    pieces = (
-        lax.all_gather(key_heads, "blk", axis=1, tiled=True),
-        lax.all_gather(value_heads, "blk", axis=1, tiled=True),
-    )
-    scores = score_block(query4, split_heads(pieces[0]))
-    maxima = jnp.max(scores, axis=-1)
-    weights = jnp.exp(scores - maxima[..., None])
-    totals = jnp.sum(weights, axis=-1)
-    summed = jnp.einsum(
-        "sqgk,skge->sqge", weights.astype(bf16), split_heads(pieces[1]), preferred_element_type=f32
-    )
-    log_sums = maxima + jnp.log(totals)
-    attended4 = summed / totals[..., None]
-    attended_heads = attended4.reshape(head_shape).astype(bf16)
-    attended_flat = attended_heads.reshape(-1, width_part)
-    att = lax.all_to_all(attended_heads, "head", split_axis=1, concat_axis=2, tiled=True)
-    wo = lax.all_gather(out_rows, "head", axis=0, tiled=True)
-    flat_rows = tokens.reshape(-1, model_dim)
-    output, d_first, d_branch, gw_in, gw_back, pg, gbin = run_ffn(
-        flat_rows,
-        att.reshape(-1, model_dim),
-        wo,
-        cotangent.reshape(-1, model_dim),
-        vectors,
-        bins,
-        w_in,
-        w_back,
-    )
-    wide_dbranch = token_rows(d_branch.reshape(token_shape)).reshape(-1, model_dim)
-    grad_out_part = contract_rows(attended_flat, wide_dbranch)
-    grad_heads = contract_cols(wide_dbranch, out_rows).astype(bf16).reshape(head_shape)
-    grads4 = split_heads(grad_heads)
-    deltas = jnp.sum(grads4.astype(f32) * attended4, axis=-1)
-    row_stats = (
-        lax.all_gather(log_sums, "blk", axis=1, tiled=True),
-        lax.all_gather(deltas, "blk", axis=1, tiled=True),
-    )
-    piece_keys = split_heads(pieces[0])
-    piece_values = split_heads(pieces[1])
-    piece_queries = split_heads(lax.all_gather(query_heads, "blk", axis=1, tiled=True))
-    piece_grads = split_heads(lax.all_gather(grad_heads, "blk", axis=1, tiled=True))
-    own_probs, own_scores = score_grads(query4, piece_keys, piece_values, grads4, log_sums, deltas)
-    d_query = score_scale * jnp.einsum(
-        "sqgk,skge->sqge", own_scores, piece_keys, preferred_element_type=f32
-    )
-    probs_low, d_scores = score_grads(
-        piece_queries, key4, value4, piece_grads, row_stats[0], row_stats[1]
-    )
-    key_acc = score_scale * jnp.einsum(
-        "sqgk,sqge->skge", d_scores, piece_queries, preferred_element_type=f32
-    )
-    value_acc = jnp.einsum("sqgk,sqge->skge", probs_low, piece_grads, preferred_element_type=f32)
-    d_query_low = d_query.reshape(-1, width_part).astype(bf16)
-    d_key_low = key_acc.reshape(-1, width_part).astype(bf16)
-    d_value_low = value_acc.reshape(-1, width_part).astype(bf16)
-    grad_b_query = place_part(
-        jnp.sum(d_query_low.astype(f32), axis=0), model_dim, head_id * width_part
-    )
-    grad_b_value = place_part(
-        jnp.sum(d_value_low.astype(f32), axis=0), model_dim, head_id * width_part
-    )
-    attn_grad_parts = jnp.stack(
-        (
-            contract_rows(wide_flat, d_query_low),
-            contract_rows(wide_flat, d_key_low),
-            contract_rows(wide_flat, d_value_low),
-        )
-    )
-    token_terms = (
-        contract_cols(d_query_low, attn_cols[0])
-        + contract_cols(d_key_low, attn_cols[1])
-        + contract_cols(d_value_low, attn_cols[2])
-    )
-    d_tokens = d_first + token_partials(token_terms.reshape(wide_shape)).reshape(-1, model_dim)
-    grad_tokens = d_tokens.astype(bf16).reshape(token_shape)
-    attn_sums, grad_w_out = (
-        lax.psum_scatter(attn_grad_parts, "blk", scatter_dimension=1, tiled=True),
-        lax.psum_scatter(grad_out_part, "blk", scatter_dimension=1, tiled=True),
-    )
-    gb_in = lax.dynamic_update_slice(
-        jnp.zeros((4, 8, 128), f32), gbin.reshape(4, 1, 128), (0, b_id, 0)
-    )
-    vec = jnp.concatenate(
-        (grad_b_query[None], grad_b_value[None], pg[2:]), axis=0
-    )
-    vec = vec.reshape(8, 32, 32).transpose(1, 0, 2).reshape(32, 256)
-    vec = jnp.concatenate((vec, gb_in.reshape(32, 128)), axis=1)
-    own = lax.psum_scatter(vec, ("blk", "head"), scatter_dimension=0, tiled=True).reshape(384)
-    parts = [own[32 * i : 32 * i + 32] for i in range(8)]
+    token_shape = tokens.shape
+    model_dim = tokens.shape[2]
+    x = tokens.reshape(-1, model_dim)
+    vectors = jnp.stack(
+        (b_query, b_value, b_out, norm1_gain, norm1_shift, b_back, norm2_gain, norm2_shift)
+    )
+    spread = jnp.where(
+        lax.broadcasted_iota(jnp.int32, (1, 128), 1) // 32 == head_id,
+        jnp.tile(vectors, (1, 4)),
+        jnp.zeros((), BF16),
+    )
+    small = jnp.concatenate((spread, b_in[None], jnp.zeros((7, 128), BF16)), axis=0)
+    xs, wqkv, queries, keys_all, values_all, mixed, log_sums, att, wo, par, bins, wi = run_attend(
+        x, w_query, w_key, w_value, w_out, small, w_in
+    )
+    output, d_first, d_branch, da, g_in, gw_back, pg, gbin = run_ffn(
+        x, att, wo, cotangent.reshape(-1, model_dim), par, bins, wi, w_back
+    )
+    grad_tokens, gq, gk, gv, gout, gw_in, notes = run_grads(
+        xs,
+        wqkv,
+        queries,
+        keys_all,
+        values_all,
+        mixed,
+        log_sums,
+        da,
+        d_first,
+        att,
+        d_branch,
+        pg,
+        gbin,
+        g_in,
+    )
+    own = lax.dynamic_slice(notes, (0, head_id * 32), (8, 32))
     return (
         output.reshape(token_shape),
-        grad_tokens,
-        attn_sums[0],
-        attn_sums[1],
-        attn_sums[2],
-        grad_w_out,
-        parts[0],
-        parts[1],
-        parts[2],
-        parts[3],
-        parts[4],
+        grad_tokens.reshape(token_shape),
+        gq,
+        gk,
+        gv,
+        gout.T,
+        own[0],
+        own[1],
+        own[2],
+        own[3],
+        own[4],
         gw_in,
         gw_back,
-        own[256:],
-        parts[5],
-        parts[6],
-        parts[7],
+        notes[8],
+        own[5],
+        own[6],
+        own[7],
     )
 
 

time: 658 us -> 274 us (0.42); the launches traced: 648 us -> 272 us
  waiting for transfers between devices: 217 us -> 0 us
  blocking collectives: 138 us -> 0 us
  Pallas kernels: 141 us -> 256 us
  matrix products: 79 us -> 0 us
  local copies, waits for them, and re-layouts: 37.1 us -> 13.9 us
  other arithmetic: 15.5 us -> 1.34 us
  between operations: 14.7 us -> 0.73 us
    all_gather x8 -> x0, waiting for transfers between devices: 139 us -> none  [the longest x2 59.2 us: token_rows(): return lax.all_gather(local, 'head', axis=1, tiled=True)]
    pallas_call x1 -> x3, Pallas kernels: 141 us -> 256 us  [run_kernel(): pl.pallas_call(body, out_shape=[jax.ShapeDtypeStruct(s, t) for s, t in sh...]
    all_gather x4 -> x0, blocking collectives: 98 us -> none  [the longest x1 68.2 us: fast_device(): smalls = lax.all_gather(small, ('blk', 'head'), axis=0)]
    dot_general x17 -> x0, matrix products: 79 us -> none  [the longest x2 16.6 us: score_block(): jnp.einsum('sqge,skge->sqgk', queries4, keys4, preferred_element_type=jnp...]
    reduce_scatter x3 -> x0, waiting for transfers between devices: 63.1 us -> none  [the longest x1 36.5 us: fast_device(): lax.psum_scatter(grad_out_part, 'blk', scatter_dimension=1, tiled=True)]
    unnamed x1 -> x0, blocking collectives: 39.8 us -> none
    all_to_all x1 -> x0, waiting for transfers between devices: 14.5 us -> none  [fast_device(): lax.all_to_all(attended_heads, 'head', split_axis=1, concat_axis=2, tiled...]
    all_gather x4 -> x0, local copies, waits for them, and re-layouts: 11.4 us -> none  [the longest x1 3.99 us: fast_device(): lax.all_gather(grad_heads, 'blk', axis=1, tiled=True)]
  transfers between devices with their start and end apart: 12 -> 0, of which waited for: 9 -> 0; matrix products, arithmetic and copies ran while one was open for 14% -> 0% of each run, Pallas kernels for 0% -> 0%
where the time goes in v2:
time: 274 us; the launch traced here: 272 us
  Pallas kernels  256 us (93%)
  local copies, waits for them, and re-layouts  13.9 us (5%)
    pallas_call x3, Pallas kernels, run_kernel(): pl.pallas_call(body, out_shape=[jax.ShapeDtypeStruct(s, t) for s, t in sh...  256 us
    unnamed x14, local copies, waits for them, and re-layouts  10.3 us

profile of v2, /device:TPU:0, one launch (start us, length us, event | category | flops | bytes accessed | tf_op | source)
XLA Modules:
  0.0 272.1 jit_solution(12864084756972961)
XLA Ops:
  0.7 0.1 pad.2.clone
  0.8 0.8 stack.35
  1.6 0.1 tile.10
  1.7 1.3 maximum_maximum_fusion.small_ref
  3.0 72.4 %shard_map.296 = (bf16[1024,1024]{1,0:T(8,128)(2,1)}, bf16[1024,384]{1,0:T(8,128)(2,1)}, bf16[1024,128]{1,0:T(8,128)(2,1)}, bf16[2048,128]{1,0:T(8,128)(2,1)}, b...) custom-call(bf16[128,1024]{1,0:T(8,128)(2,1)} %bitcast.32, ...), custom_call_target="tpu_custom_call" | custom-call | tf_op jit(solution)/shard_map/pallas_call | solution.py:1241
  75.3 106.4 %shard_map.297 = (bf16[128,1024]{1,0:T(8,128)(2,1)}, f32[128,1024]{1,0:T(8,128)}, bf16[128,1024]{1,0:T(8,128)(2,1)}, bf16[1024,128]{1,0:T(8,128)(2,1)}, bf16[8,1...) custom-call(bf16[128,1024]{1,0:T(8,128)(2,1)} %bitcast.33, ...), custom_call_target="tpu_custom_call" | custom-call | tf_op jit(solution)/shard_map/pallas_call | solution.py:1241
  181.7 0.0 copy-start.2
  181.7 77.5 %shard_map.298 = (bf16[128,1024]{1,0:T(8,128)(2,1)}, f32[128,256]{1,0:T(8,128)}, f32[128,256]{1,0:T(8,128)}, f32[128,256]{1,0:T(8,128)}, f32[128,256]{1,0:T(8,12...) custom-call(bf16[1024,1024]{1,0:T(8,128)(2,1)} %get-tuple-element.50.xs, bf16[1024,384]{1,0:T(8,128)(2,1)} %get-tuple-element.51.wqkv, ...), custom_call_target="tpu_custom_call" | custom-call | tf_op jit(solution)/shard_map/pallas_call | solution.py:1241
  259.2 0.0 copy-start.1
  259.2 0.0 copy-start
  259.2 1.3 slice_bitcast_fusion.3
  260.5 0.7 constant_dynamic-slice_fusion
  261.3 0.5 slice_bitcast_fusion
  261.8 1.7 copy.34
  263.5 0.0 copy-done.2
  263.5 0.7 copy.42
  264.2 1.7 copy.43
  265.8 1.6 copy.44
  267.4 1.6 copy.45
  269.0 1.6 copy.46
  270.5 0.0 copy-done.1
  270.5 0.8 copy.47
  271.3 0.0 copy-done
  271.3 0.8 copy.48
  (4 shorter events, 0.0 us)
Async XLA Ops:
  181.7 81.7 %copy-start.2 = (bf16[128,1024]{1,0:T(8,128)(2,1)S(1)}, bf16[128,1024]{1,0:T(8,128)(2,1)}, u32[]{:S(2)}) copy-start(bf16[128,1024]{1,0:T(8,128)(2,1)} %get-tuple-element.49) | copy-start | bytes 786436
  259.2 11.3 %copy-start.1 = (f32[128,1024]{1,0:T(8,128)S(1)}, f32[128,1024]{1,0:T(8,128)}, u32[]{:S(2)}) copy-start(f32[128,1024]{1,0:T(8,128)} %get-tuple-element.124) | copy-start | bytes 1572868
  259.2 12.1 %copy-start = (f32[128,1024]{1,0:T(8,128)S(1)}, f32[128,1024]{1,0:T(8,128)}, u32[]{:S(2)}) copy-start(f32[128,1024]{1,0:T(8,128)} %get-tuple-element.125) | copy-start | bytes 1572868

commit v3 on v0

--- a/solution.py
+++ b/solution.py
@@ -1,6 +1,11 @@
+import functools
+import math
+
 import jax
 import jax.numpy as jnp
 from jax import lax
+from jax.experimental import pallas as pl
+from jax.experimental.pallas import tpu as pltpu
 from jax.sharding import PartitionSpec as P
 
 HEAD_DIM = 64
@@ -286,6 +291,1130 @@
     )
 
 
+MESH = pl.DeviceIdType.MESH
+F32 = jnp.float32
+BF16 = jnp.bfloat16
+VMEM_LIMIT = 60 * 2**20
+
+
+def dot_nn(left, right):
+    return jnp.dot(left, right, preferred_element_type=F32)
+
+
+class Place:
+    def __init__(self):
+        self.b = lax.axis_index("blk")
+        self.z = lax.axis_index("head")
+        self.y = self.b // 4
+        self.x = (self.b // 2) % 2
+        self.c = self.b % 2
+        self.q = self.b // 2
+
+    def chip(self, r):
+        return ((self.y + r // 2) % 2) * 2 + (self.x + r % 2) % 2
+
+    def peer(self, r):
+        return (2 * self.chip(r) + self.c, self.z)
+
+    def sibling(self):
+        return (2 * self.q + 1 - self.c, self.z)
+
+
+def remote(src, dst, send_sem, recv_sem, device):
+    return pltpu.make_async_remote_copy(
+        src_ref=src,
+        dst_ref=dst,
+        send_sem=send_sem,
+        recv_sem=recv_sem,
+        device_id=device,
+        device_id_type=MESH,
+    )
+
+
+def wait_bytes(view, sem):
+    pltpu.make_async_copy(view, view, sem).wait()
+
+
+def greet_all(at):
+    barrier = pltpu.get_barrier_semaphore()
+    flat = at.b * 4 + at.z
+
+    def greet(step, carry):
+        other = (flat + step) % 32
+        pl.semaphore_signal(
+            barrier, inc=1, device_id=(other // 4, other % 4), device_id_type=MESH
+        )
+        return carry
+
+    lax.fori_loop(1, 32, greet, 0)
+    pl.semaphore_wait(barrier, 31)
+
+
+def half(core):
+    return pl.ds(pl.multiple_of(core * 128, 128), 128)
+
+
+def lanes(index):
+    return pl.ds(pl.multiple_of(index * 128, 128), 128)
+
+
+def by_rows(count, size, step):
+    def body(i, carry):
+        step(pl.ds(pl.multiple_of(i * size, size), size))
+        return carry
+
+    lax.fori_loop(0, count // size, body, 0)
+
+
+def row_sums(count, size, width, step):
+    def body(i, carry):
+        parts = step(pl.ds(pl.multiple_of(i * size, size), size))
+        return tuple(
+            kept + jnp.sum(part.reshape(size // 8, 8, width), axis=0)
+            for kept, part in zip(carry, parts)
+        )
+
+    n = step.count
+    sums = lax.fori_loop(
+        0, count // size, body, tuple(jnp.zeros((8, width), F32) for _ in range(n))
+    )
+    return tuple(jnp.sum(s, axis=0, keepdims=True) for s in sums)
+
+
+class Exchange:
+    def __init__(self, at, send, recv, send_sib, recv_sib):
+        self.at, self.send, self.recv = at, send, recv
+        self.send_sib, self.recv_sib = send_sib, recv_sib
+
+    def gather_start(self, slots):
+        at = self.at
+        mine = slots.at[at.q, half(at.c)]
+        for r in (1, 2, 3):
+            remote(mine, mine, self.send.at[r], self.recv.at[r], at.peer(r)).start()
+        remote(mine, mine, self.send_sib.at[0], self.recv_sib.at[0], at.sibling()).start()
+
+    def gather_step(self, slots, r):
+        at = self.at
+        chip = at.chip(r)
+        block = slots.at[chip, half(at.c)]
+        if r:
+            wait_bytes(block, self.recv.at[r])
+            remote(
+                block, block, self.send_sib.at[r], self.recv_sib.at[r], at.sibling()
+            ).start()
+        wait_bytes(slots.at[chip, half(1 - at.c)], self.recv_sib.at[r])
+        return chip
+
+    def gather_end(self, slots):
+        at = self.at
+        for r in range(4):
+            block = slots.at[at.chip(r), half(at.c)]
+            if r:
+                wait_bytes(slots.at[at.q, half(at.c)], self.send.at[r])
+            wait_bytes(block, self.send_sib.at[r])
+
+    def scatter_put(self, terms, out_sib, in_sib, r):
+        at = self.at
+        out_sib[r] = terms[r, half(1 - at.c)].astype(BF16)
+        remote(
+            out_sib.at[r], in_sib.at[r], self.send_sib.at[r], self.recv_sib.at[r], at.sibling()
+        ).start()
+
+    def scatter_pass(self, terms, in_sib, out, into, r):
+        at = self.at
+        wait_bytes(in_sib.at[r], self.recv_sib.at[r])
+        total = terms[r, half(at.c)] + in_sib[r].astype(F32)
+        if r:
+            out[r] = total.astype(BF16)
+            remote(out.at[r], into.at[r], self.send.at[r], self.recv.at[r], at.peer(r)).start()
+        else:
+            terms[0, half(at.c)] = total
+
+    def scatter_arrive(self, into):
+        for r in (1, 2, 3):
+            wait_bytes(into.at[r], self.recv.at[r])
+
+    def scatter_end(self, out_sib, out):
+        for r in range(4):
+            wait_bytes(out_sib.at[r], self.send_sib.at[r])
+            if r:
+                wait_bytes(out.at[r], self.send.at[r])
+
+
+def norm_rows(values):
+    centre = jnp.mean(values, axis=-1, keepdims=True)
+    centred = values - centre
+    spread = jnp.mean(centred * centred, axis=-1, keepdims=True)
+    scale = lax.rsqrt(spread + NORM_EPS)
+    return centred * scale, scale
+
+
+def norm_back(grad, unit, scale):
+    centre = jnp.mean(grad, axis=-1, keepdims=True)
+    along = jnp.mean(grad * unit, axis=-1, keepdims=True)
+    return (grad - centre - unit * along) * scale
+
+
+def send_or_copy(src, dst, send_sem, recv_sem, device, own):
+    def away():
+        remote(src, dst, send_sem, recv_sem, device).start()
+
+    if own is None:
+        away()
+        return
+    pl.when(jnp.logical_not(own))(away)
+
+    @pl.when(own)
+    def _():
+        pltpu.make_async_copy(src, dst, recv_sem).start()
+
+
+class Column:
+    def __init__(self, at, ref, sems):
+        self.at, self.ref = at, ref
+        self.up_send, self.up_recv, self.down_send, self.down_recv = sems
+
+    def block(self, plane):
+        return self.ref.at[:, lanes(plane)]
+
+    def sides(self, hop, act, arriving):
+        z = self.at.z
+        if arriving:
+            below, above = z - 1 - hop, z + 1 + hop
+            pl.when(below >= 0)(lambda: act(self.block(below), 0))
+            pl.when(above <= 3)(lambda: act(self.block(above), 1))
+        else:
+            up = jnp.logical_and(z >= hop, z < 3)
+            down = jnp.logical_and(z + hop <= 3, z > 0)
+            pl.when(up)(lambda: act(self.block(z - hop), 0))
+            pl.when(down)(lambda: act(self.block(z + hop), 1))
+
+    def send(self, hop):
+        def act(block, side):
+            send = (self.up_send, self.down_send)[side].at[hop]
+            recv = (self.up_recv, self.down_recv)[side].at[hop]
+            remote(block, block, send, recv, (self.at.b, self.at.z + 1 - 2 * side)).start()
+
+        self.sides(hop, act, False)
+
+    def arrive(self, hop):
+        def act(block, side):
+            wait_bytes(block, (self.up_recv, self.down_recv)[side].at[hop])
+
+        self.sides(hop, act, True)
+
+    def end(self):
+        def wait(hop):
+            def act(block, side):
+                wait_bytes(block, (self.up_send, self.down_send)[side].at[hop])
+
+            return act
+
+        for hop in range(3):
+            self.sides(hop, wait(hop), False)
+
+
+def plane_weights(at, src, dst, send_sem, recv_sem):
+    rows, cols = lanes(at.b), lanes(at.z)
+    pltpu.make_async_copy(src.at[:, lanes(at.b)], dst.at[rows, cols], recv_sem).start()
+
+    def push(step, carry):
+        other = (at.b + step) % 8
+        remote(
+            src.at[:, lanes(other)], dst.at[rows, cols], send_sem, recv_sem, (other, at.z)
+        ).start()
+        return carry
+
+    lax.fori_loop(1, 8, push, 0)
+
+
+def column_grads(at, blocks, into, send_sem, recv_sem):
+    for dz in (2, 1, 3):
+        plane = (at.z + dz) % 4
+        remote(
+            blocks.at[:, :, lanes(plane)],
+            into.at[dz],
+            send_sem.at[dz],
+            recv_sem.at[dz],
+            (at.b, plane),
+        ).start()
+
+
+def plane_grads(at, blocks, into, sums, final, recv_sem, send_out, recv_out):
+    for dz in (1, 3, 2):
+        wait_bytes(into.at[dz], recv_sem.at[dz])
+
+    def one(step, carry):
+        other = (at.b + 1 + step) % 8
+        sums[other] = (
+            blocks[other, :, lanes(at.z)].astype(F32)
+            + into[1, other].astype(F32)
+            + into[2, other].astype(F32)
+            + into[3, other].astype(F32)
+        ).astype(BF16)
+        send_or_copy(
+            sums.at[other],
+            final.at[:, lanes(at.b)],
+            send_out,
+            recv_out,
+            (other, at.z),
+            step == 7,
+        )
+        return carry
+
+    lax.fori_loop(0, 8, one, 0)
+
+
+def head_mask(h):
+    lane = lax.broadcasted_iota(jnp.int32, (1, 128), 1)
+    return jnp.where(lane // HEAD_DIM == h, 1.0, 0.0).astype(F32)
+
+
+def slot_rows(index):
+    return pl.ds(pl.multiple_of(index * 64, 64), 64)
+
+
+def chip_rows(index):
+    return pl.ds(pl.multiple_of(index * 256, 256), 256)
+
+
+def core_rows(index):
+    return pl.ds(pl.multiple_of(index * 1024, 1024), 1024)
+
+
+INPUTS = ("x", "wq", "wk", "wv", "wout", "small", "win", "wback", "cot")
+
+RESULTS = (
+    ("out", (128, 1024), BF16),
+    ("gtok", (128, 1024), BF16),
+    ("w_in", (2, 2, 128, 384), BF16),
+    ("o_in", (4, 128, 256), BF16),
+    ("fin_in", (128, 1024), BF16),
+    ("fin_back", (128, 1024), BF16),
+    ("notes_in", (32, 16, 128), F32),
+)
+
+SCRATCH = (
+    ("xs", (1024, 1024), BF16),
+    ("wqkv", (1024, 384), BF16),
+    ("queries", (1024, 128), BF16),
+    ("keys_all", (2048, 128), BF16),
+    ("values_all", (2048, 128), BF16),
+    ("mixed", (1024, 128), F32),
+    ("log_sums", (1024, 128), F32),
+    ("att", (128, 1024), BF16),
+    ("wo", (1024, 1024), BF16),
+    ("par", (8, 1024), F32),
+    ("bins", (1, 512), F32),
+    ("wi", (1024, 512), BF16),
+    ("wb", (1024, 512), BF16),
+    ("smalls", (32, 16, 128), BF16),
+    ("proj", (256, 384), F32),
+    ("scores", (256, 2048), F32),
+    ("d_buf", (256, 2048), F32),
+    ("p_buf", (256, 2048), BF16),
+    ("att_send", (1024, 128), BF16),
+    ("n1", (128, 1024), F32),
+    ("unit1", (128, 1024), F32),
+    ("scale1", (128, 128), F32),
+    ("d2", (128, 1024), F32),
+    ("d1", (128, 1024), F32),
+    ("db", (128, 1024), BF16),
+    ("norm_slots", (4, 256, 1024), BF16),
+    ("grad_slots", (4, 256, 1024), BF16),
+    ("hid", (4, 256, 512), BF16),
+    ("slope", (4, 256, 512), F32),
+    ("pre", (256, 512), F32),
+    ("terms", (4, 256, 1024), F32),
+    ("sib_out", (2, 4, 128, 1024), BF16),
+    ("sib_in", (2, 4, 128, 1024), BF16),
+    ("peer_out", (2, 4, 128, 1024), BF16),
+    ("peer_in", (2, 4, 128, 1024), BF16),
+    ("g_back", (8, 128, 512), BF16),
+    ("g_in", (8, 128, 512), BF16),
+    ("zg_back", (4, 8, 128, 128), BF16),
+    ("zg_in", (4, 8, 128, 128), BF16),
+    ("gs_back", (8, 128, 128), BF16),
+    ("gs_in", (8, 128, 128), BF16),
+    ("da_send", (128, 1024), BF16),
+    ("da", (1024, 128), BF16),
+    ("q_turned", (128, 1024), BF16),
+    ("da_turned", (128, 1024), BF16),
+    ("dq", (1024, 128), F32),
+    ("dk_turned", (128, 2048), F32),
+    ("dv_turned", (128, 2048), F32),
+    ("out_k", (1024, 128), F32),
+    ("out_v", (1024, 128), F32),
+    ("sib_k", (1024, 128), F32),
+    ("sib_v", (1024, 128), F32),
+    ("dqkv", (1024, 384), BF16),
+    ("x_in", (4, 256, 1024), BF16),
+    ("x_sum", (256, 1024), F32),
+    ("x_own", (64, 1024), F32),
+    ("z_out", (4, 64, 1024), BF16),
+    ("z_in", (4, 64, 1024), BF16),
+    ("w_sib_out", (4, 128, 384), F32),
+    ("w_sib_in", (4, 128, 384), F32),
+    ("w_out", (4, 128, 384), BF16),
+    ("o_out", (128, 1024), BF16),
+    ("vec", (8, 1024), F32),
+    ("gbin", (1, 512), F32),
+    ("notes", (32, 16, 128), F32),
+)
+
+SEMAPHORES = (
+    ("z", (4,)),
+    ("p", (4, 4)),
+    ("w", (2,)),
+    ("o", (8,)),
+    ("kv", (2, 4)),
+    ("misc", (12,)),
+    ("col", (4, 3)),
+    ("ex", (5, 4)),
+    ("ex_sib", (5, 4)),
+    ("zg", (2, 4)),
+    ("kv2", (2,)),
+    ("dx", (4, 4)),
+    ("dz", (4,)),
+    ("ws", (4,)),
+)
+
+
+class Refs:
+    pass
+
+
+def layer_kernel(*refs):
+    v = Refs()
+    names = list(INPUTS) + [n for n, _, _ in RESULTS] + [n for n, _, _ in SCRATCH]
+    for n, _ in SEMAPHORES:
+        names += ["s_" + n, "r_" + n]
+    for name, ref in zip(names, refs):
+        setattr(v, name, ref)
+    at = Place()
+    at.flat = at.b * 4 + at.z
+    at.place = at.q * 4 + at.z
+    at.parity = at.z % 2
+    at.pair = 4 * (at.z // 2) + at.q
+    col_in = Column(at, v.wi, [s.at[0] for s in (v.s_col, v.r_col)] + [s.at[1] for s in (v.s_col, v.r_col)])
+    col_back = Column(at, v.wb, [s.at[2] for s in (v.s_col, v.r_col)] + [s.at[3] for s in (v.s_col, v.r_col)])
+    exchanges = [
+        Exchange(at, v.s_ex.at[i], v.r_ex.at[i], v.s_ex_sib.at[i], v.r_ex_sib.at[i])
+        for i in range(5)
+    ]
+    greet_all(at)
+    attend_phase(at, v, col_in, col_back)
+    ffn_phase(at, v, col_in, col_back, exchanges)
+    grads_phase(at, v, exchanges[0], exchanges[4])
+    end_phase(at, v, col_in, col_back, exchanges)
+
+
+def attend_phase(at, v, col_in, col_back):
+    xs, wqkv, wo = v.xs, v.wqkv, v.wo
+    parity, pair = at.parity, at.pair
+
+    for dz in (1, 3, 2):
+        plane = (at.z + dz) % 4
+        remote(
+            v.x.at[slot_rows(plane % 2)],
+            xs.at[slot_rows(at.place)],
+            v.s_z.at[dz],
+            v.r_z.at[dz],
+            (at.b, plane),
+        ).start()
+    pltpu.make_async_copy(
+        v.x.at[slot_rows(parity)], xs.at[slot_rows(at.place)], v.r_z.at[0]
+    ).start()
+    plane_weights(at, v.win, v.wi, v.s_misc.at[0], v.r_misc.at[0])
+
+    for dx in range(2):
+        for dz in range(2):
+            column = (at.x + dx) % 2
+            plane = 2 * (at.z // 2) + (at.z + dz) % 2
+            target = 2 * (parity * 2 + column) + at.c
+            mine = jnp.logical_and(
+                parity == at.y, jnp.logical_and(column == at.x, plane == at.z)
+            )
+            for k, w in enumerate((v.wq, v.wk, v.wv)):
+                send_or_copy(
+                    w.at[:, lanes(column)],
+                    wqkv.at[lanes(at.b), pl.ds(k * 128, 128)],
+                    v.s_w.at[0],
+                    v.r_w.at[0],
+                    (target, plane),
+                    mine if dx == 0 and dz == 0 else None,
+                )
+
+    pltpu.make_async_copy(v.small, v.smalls.at[at.flat], v.r_misc.at[1]).start()
+
+    def spread(step, carry):
+        other = (at.flat + step) % 32
+        remote(
+            v.small,
+            v.smalls.at[at.flat],
+            v.s_misc.at[1],
+            v.r_misc.at[1],
+            (other // 4, other % 4),
+        ).start()
+        return carry
+
+    lax.fori_loop(1, 32, spread, 0)
+
+    part = wo.at[pl.ds(pl.multiple_of(at.z * 256, 256), 256), lanes(at.b)]
+    pltpu.make_async_copy(v.wout, part, v.r_o.at[0]).start()
+    for dz in range(1, 4):
+        remote(v.wout, part, v.s_o.at[0], v.r_o.at[0], (at.b, (at.z + dz) % 4)).start()
+
+    for dz in (0, 1, 3, 2):
+        block = xs.at[slot_rows(at.q * 4 + (at.z - dz + 4) % 4)]
+        wait_bytes(block, v.r_z.at[dz])
+        for r in (1, 2, 3):
+            remote(block, block, v.s_p.at[r, dz], v.r_p.at[r, dz], at.peer(r)).start()
+
+    wait_bytes(v.wi.at[:, pl.ds(0, 128)], v.r_misc.at[0])
+    col_in.send(0)
+
+    wait_bytes(wqkv.at[pl.ds(0, 512)], v.r_w.at[0])
+    for r in range(4):
+        part = wqkv.at[lanes(2 * at.chip(r) + at.c)]
+        remote(part, part, v.s_w.at[1], v.r_w.at[1], at.sibling()).start()
+
+    wait_bytes(v.smalls, v.r_misc.at[1])
+    for b in range(8):
+        total = v.smalls[4 * b].astype(F32)
+        for z in range(1, 4):
+            total += v.smalls[4 * b + z].astype(F32)
+        v.par[:, 128 * b : 128 * b + 128] = total[0:8]
+    for h in range(4):
+        v.bins[0:1, 128 * h : 128 * h + 128] = v.smalls[8 * h + at.b].astype(F32)[8:9]
+    bias_q = v.par[0:1, lanes(pair)]
+    bias_v = v.par[1:2, lanes(pair)]
+    wait_bytes(wqkv.at[pl.ds(0, 512)], v.r_w.at[1])
+
+    for r in range(4):
+        chip = at.chip(r)
+        if r:
+            for dz in (0, 1, 3, 2):
+                wait_bytes(xs.at[slot_rows(0)], v.r_p.at[r, dz])
+        rows = chip_rows(chip)
+        v.proj[...] = dot_nn(xs[rows], wqkv[...])
+        v.queries[rows] = (v.proj[:, 0:128] + bias_q).astype(BF16)
+        own_rows = chip_rows(at.c * 4 + chip)
+        v.keys_all[own_rows] = v.proj[:, 128:256].astype(BF16)
+        v.values_all[own_rows] = (v.proj[:, 256:384] + bias_v).astype(BF16)
+        for k, ref in enumerate((v.keys_all, v.values_all)):
+            view = ref.at[own_rows]
+            remote(view, view, v.s_kv.at[k, r], v.r_kv.at[k, r], at.sibling()).start()
+        if r == 1:
+            col_in.arrive(0)
+            col_in.send(1)
+            plane_weights(at, v.wback, v.wb, v.s_misc.at[2], v.r_misc.at[2])
+
+    whole = wo.at[:, lanes(at.b)]
+    wait_bytes(whole, v.r_o.at[0])
+    for r in (1, 2, 3):
+        remote(whole, whole, v.s_o.at[r], v.r_o.at[r], at.peer(r)).start()
+    remote(whole, whole, v.s_o.at[4], v.r_o.at[4], at.sibling()).start()
+    col_in.arrive(1)
+    col_in.send(2)
+    wait_bytes(v.wb.at[:, pl.ds(0, 128)], v.r_misc.at[2])
+    col_back.send(0)
+
+    for r in range(4):
+        for k, ref in enumerate((v.keys_all, v.values_all)):
+            wait_bytes(ref.at[pl.ds(0, 256)], v.r_kv.at[k, r])
+
+    scores = v.scores
+
+    def attend(step, carry):
+        chip = (at.q + 1 + step) % 4
+        rows = chip_rows(chip)
+        outs = []
+        logs = []
+        for h in range(2):
+            q = (v.queries[rows].astype(F32) * head_mask(h) * HEAD_DIM**-0.5).astype(BF16)
+            scores[...] = contract_cols(q, v.keys_all[...])
+            top = jnp.max(scores[...], axis=-1, keepdims=True)
+            weights = jnp.exp(scores[...] - top)
+            total = jnp.sum(weights, axis=-1, keepdims=True)
+            outs.append(dot_nn(weights.astype(BF16), v.values_all[...]) / total)
+            logs.append(top + jnp.log(total))
+        first = head_mask(0) > 0.5
+        merged = jnp.where(first, outs[0], outs[1])
+        v.mixed[rows] = merged
+        v.log_sums[rows] = jnp.where(first, logs[0], logs[1])
+        v.att_send[rows] = merged.astype(BF16)
+        for k in range(4):
+            plane = (at.z + 1 + k) % 4
+            send_or_copy(
+                v.att_send.at[slot_rows(chip * 4 + plane)],
+                v.att.at[slot_rows(parity), lanes(pair)],
+                v.s_misc.at[3],
+                v.r_misc.at[3],
+                (2 * chip + at.c, plane),
+                step == 3 if k == 3 else None,
+            )
+        return carry
+
+    lax.fori_loop(0, 4, attend, 0)
+
+    col_back.arrive(0)
+    col_back.send(1)
+    for r in (1, 2, 3):
+        part = wo.at[:, lanes(2 * at.chip(r) + at.c)]
+        wait_bytes(part, v.r_o.at[r])
+        remote(part, part, v.s_o.at[4 + r], v.r_o.at[4 + r], at.sibling()).start()
+    for r in range(4):
+        wait_bytes(whole, v.r_o.at[4 + r])
+    wait_bytes(v.att, v.r_misc.at[3])
+
+
+def ffn_phase(at, v, col_in, col_back, exchanges):
+    n1, terms = v.n1, v.terms
+    sib_out, sib_in, peer_out, peer_in = v.sib_out, v.sib_in, v.peer_out, v.peer_in
+    gather, scatter, gather2, scatter2 = exchanges[:4]
+
+    def param(i):
+        return v.par[i : i + 1, :]
+
+    n1[...] = dot_nn(v.att[...], v.wo[...])
+
+    def first_norm(rows):
+        unit, scale = norm_rows(v.x[rows].astype(F32) + n1[rows] + param(2))
+        v.unit1[rows] = unit
+        v.scale1[rows] = jnp.broadcast_to(scale, (32, 128))
+        n1[rows] = unit * param(3) + param(4)
+
+    by_rows(128, 32, first_norm)
+    v.norm_slots[at.q, half(at.c)] = n1[...].astype(BF16)
+    gather.gather_start(v.norm_slots)
+
+    col_in.arrive(2)
+    col_back.arrive(1)
+    col_back.send(2)
+    col_back.arrive(2)
+
+    for r in range(4):
+        chip = gather.gather_step(v.norm_slots, r)
+        v.pre[...] = dot_nn(v.norm_slots[chip], v.wi[...])
+
+        def activate(rows, r=r):
+            u = v.pre[rows] + v.bins[...]
+            cdf = 0.5 * (1.0 + lax.erf(u * math.sqrt(0.5)))
+            bell = jnp.exp(-0.5 * u * u) * (1.0 / math.sqrt(2.0 * math.pi))
+            v.hid[r, rows] = (u * cdf).astype(BF16)
+            v.slope[r, rows] = cdf + u * bell
+
+        by_rows(256, 32, activate)
+        terms[r] = contract_cols(v.hid[r], v.wb[...])
+        scatter.scatter_put(terms, sib_out.at[0], sib_in.at[0], r)
+        if r:
+            scatter.scatter_pass(terms, sib_in.at[0], peer_out.at[0], peer_in.at[0], r - 1)
+    scatter.scatter_pass(terms, sib_in.at[0], peer_out.at[0], peer_in.at[0], 3)
+    scatter.scatter_arrive(peer_in.at[0])
+
+    base = pl.multiple_of(at.c * 128, 128)
+
+    def second_norm(rows):
+        own = pl.ds(pl.multiple_of(base + rows.start, 32), 32)
+        total = (
+            terms[0, own]
+            + peer_in[0, 1, rows].astype(F32)
+            + peer_in[0, 2, rows].astype(F32)
+            + peer_in[0, 3, rows].astype(F32)
+        )
+        unit, scale = norm_rows(n1[rows] + total + param(5))
+        v.out[rows] = (unit * param(6) + param(7)).astype(BF16)
+        g = v.cot[rows].astype(F32)
+        d = norm_back(g * param(6), unit, scale)
+        v.d2[rows] = d
+        low = d.astype(BF16)
+        v.grad_slots[at.q, own] = low
+        return g * unit, g, low.astype(F32)
+
+    second_norm.count = 3
+    sums = row_sums(128, 32, 1024, second_norm)
+    v.vec[6:7, :] = sums[0]
+    v.vec[7:8, :] = sums[1]
+    v.vec[5:6, :] = sums[2]
+
+    gather2.gather_start(v.grad_slots)
+    gbin = jnp.zeros((1, 512), F32)
+    for r in range(4):
+        chip = gather2.gather_step(v.grad_slots, r)
+        v.pre[...] = dot_nn(v.grad_slots[chip], v.wb[...])
+
+        def deactivate(rows, r=r):
+            low = (v.pre[rows] * v.slope[r, rows]).astype(BF16)
+            v.pre[rows] = low.astype(F32)
+            return (low.astype(F32),)
+
+        deactivate.count = 1
+        gbin = gbin + row_sums(256, 32, 512, deactivate)[0]
+        v.slope[r] = v.pre[...]
+        terms[r] = contract_cols(v.pre[...].astype(BF16), v.wi[...])
+        if r == 0:
+            scatter.scatter_end(sib_out.at[0], peer_out.at[0])
+        scatter2.scatter_put(terms, sib_out.at[1], sib_in.at[1], r)
+        if r:
+            scatter2.scatter_pass(terms, sib_in.at[1], peer_out.at[1], peer_in.at[1], r - 1)
+    scatter2.scatter_pass(terms, sib_in.at[1], peer_out.at[1], peer_in.at[1], 3)
+    v.gbin[...] = gbin
+
+    def weight_grad(slots, right, into):
+        def one(step, carry):
+            other = (at.b + step) % 8
+            total = jnp.zeros((128, 512), F32)
+            for r in range(4):
+                total += contract_rows(slots[at.chip(r), :, lanes(other)], right(r))
+            into[other] = total.astype(BF16)
+            return carry
+
+        lax.fori_loop(0, 8, one, 0)
+
+    weight_grad(v.grad_slots, lambda r: v.hid[r], v.g_back)
+    column_grads(at, v.g_back, v.zg_back, v.s_zg.at[0], v.r_zg.at[0])
+    weight_grad(v.norm_slots, lambda r: v.slope[r].astype(BF16), v.g_in)
+
+    scatter2.scatter_arrive(peer_in.at[1])
+
+    def first_back(rows):
+        own = pl.ds(pl.multiple_of(base + rows.start, 32), 32)
+        total = (
+            v.d2[rows]
+            + terms[0, own]
+            + peer_in[1, 1, rows].astype(F32)
+            + peer_in[1, 2, rows].astype(F32)
+            + peer_in[1, 3, rows].astype(F32)
+        )
+        unit = v.unit1[rows]
+        d = norm_back(total * param(3), unit, v.scale1[rows][:, :1])
+        v.d1[rows] = d
+        low = d.astype(BF16)
+        v.db[rows] = low
+        return total * unit, total, low.astype(F32)
+
+    first_back.count = 3
+    sums = row_sums(128, 32, 1024, first_back)
+    v.vec[3:4, :] = sums[0]
+    v.vec[4:5, :] = sums[1]
+    v.vec[2:3, :] = sums[2]
+    v.vec[0:2, :] = jnp.zeros((2, 1024), F32)
+
+    v.da_send[...] = contract_cols(v.db[...], v.wo[...]).astype(BF16)
+
+    def give(step, carry):
+        for k in range(4):
+            chip = (at.q + 1 + step) % 4
+            plane = (at.z + 1 + k) % 4
+            pair = 4 * (plane // 2) + chip
+            send_or_copy(
+                v.da_send.at[slot_rows(plane % 2), lanes(pair)],
+                v.da.at[slot_rows(at.place)],
+                v.s_misc.at[4],
+                v.r_misc.at[4],
+                (2 * chip + at.c, plane),
+                step == 3 if k == 3 else None,
+            )
+        return carry
+
+    lax.fori_loop(0, 4, give, 0)
+
+
+def grads_phase(at, v, gather, out_scatter):
+    xs, wqkv, terms = v.xs, v.wqkv, v.terms
+    parity, pair = at.parity, at.pair
+    sib_out, sib_in = v.sib_out.at[0], v.sib_in.at[0]
+    peer_out, peer_in = v.peer_out.at[0], v.peer_in.at[0]
+
+    for r in range(4):
+        terms[r] = contract_rows(v.db[:, chip_rows(at.chip(r))], v.att[...])
+        out_scatter.scatter_put(terms, sib_out, sib_in, r)
+        if r:
+            out_scatter.scatter_pass(terms, sib_in, peer_out, peer_in, r - 1)
+    out_scatter.scatter_pass(terms, sib_in, peer_out, peer_in, 3)
+
+    v.q_turned[...] = v.queries[...].astype(F32).T.astype(BF16)
+    v.dk_turned[...] = jnp.zeros_like(v.dk_turned)
+    v.dv_turned[...] = jnp.zeros_like(v.dv_turned)
+    wait_bytes(v.da, v.r_misc.at[4])
+    column_grads(at, v.g_in, v.zg_in, v.s_zg.at[1], v.r_zg.at[1])
+    v.da_turned[...] = v.da[...].astype(F32).T.astype(BF16)
+    s_buf, d_buf, p_buf = v.scores, v.d_buf, v.p_buf
+
+    def attend(step, carry):
+        rows = chip_rows(step)
+        parts = []
+        for h in range(2):
+            mask = head_mask(h)
+            grad = v.da[rows].astype(F32) * mask
+            delta = jnp.sum(grad * v.mixed[rows], axis=-1, keepdims=True)
+            q = (v.queries[rows].astype(F32) * mask * HEAD_DIM**-0.5).astype(BF16)
+            s_buf[...] = contract_cols(q, v.keys_all[...])
+            d_buf[...] = contract_cols(grad.astype(BF16), v.values_all[...])
+            logs = v.log_sums[rows][:, h * HEAD_DIM : h * HEAD_DIM + 1]
+            probs = jnp.exp(s_buf[...] - logs)
+            p_buf[...] = probs.astype(BF16)
+            low = (probs * (d_buf[...] - delta)).astype(BF16)
+            band = pl.ds(h * HEAD_DIM, HEAD_DIM)
+            v.dv_turned[band] += dot_nn(v.da_turned[band, rows], p_buf[...])
+            v.dk_turned[band] += dot_nn(v.q_turned[band, rows], low)
+            parts.append(dot_nn(low, v.keys_all[...]))
+        v.dq[rows] = jnp.where(head_mask(0) > 0.5, parts[0], parts[1]) * HEAD_DIM**-0.5
+        return carry
+
+    lax.fori_loop(0, 4, attend, 0)
+
+    other = core_rows(1 - at.c)
+    mine = core_rows(at.c)
+    v.out_k[...] = v.dk_turned[:, other].T * HEAD_DIM**-0.5
+    v.out_v[...] = v.dv_turned[:, other].T
+    for k, (ref, into) in enumerate(((v.out_k, v.sib_k), (v.out_v, v.sib_v))):
+        remote(ref, into, v.s_kv2.at[k], v.r_kv2.at[k], at.sibling()).start()
+    dqkv = v.dqkv
+    low = v.dq[...].astype(BF16)
+    dqkv[:, 0:128] = low
+    v.vec[0:1, lanes(pair)] = jnp.sum(low.astype(F32), axis=0, keepdims=True)
+    own_k = v.dk_turned[:, mine].T * HEAD_DIM**-0.5
+    wait_bytes(v.sib_k, v.r_kv2.at[0])
+    dqkv[:, 128:256] = (own_k + v.sib_k[...]).astype(BF16)
+    own_v = v.dv_turned[:, mine].T
+    wait_bytes(v.sib_v, v.r_kv2.at[1])
+    low = (own_v + v.sib_v[...]).astype(BF16)
+    dqkv[:, 256:384] = low
+    v.vec[1:2, lanes(pair)] = jnp.sum(low.astype(F32), axis=0, keepdims=True)
+
+    gather.gather_end(v.norm_slots)
+    x_out, x_in = v.norm_slots, v.x_in
+    for r in (3, 1, 2, 0):
+        part = contract_cols(dqkv[chip_rows(at.chip(r))], wqkv[...])
+        if r:
+            x_out[r] = part.astype(BF16)
+        else:
+            v.x_sum[...] = part
+    for dz in (2, 1, 3, 0):
+        rows = slot_rows((at.z + dz) % 4)
+        for r in (3, 1, 2):
+            remote(
+                x_out.at[r, rows],
+                x_in.at[r, rows],
+                v.s_dx.at[r, dz],
+                v.r_dx.at[r, dz],
+                at.peer(r),
+            ).start()
+
+    notes = v.notes
+    for d in range(32):
+        notes[d, 0:8] = v.vec[:, 128 * (d // 4) : 128 * (d // 4) + 128]
+        notes[d, 8:16] = jnp.zeros((8, 128), F32)
+    for h in range(4):
+        notes[8 * h + at.b, 8:9] = v.gbin[0:1, 128 * h : 128 * h + 128]
+    pltpu.make_async_copy(notes.at[at.flat], v.notes_in.at[at.flat], v.r_misc.at[5]).start()
+
+    def spread(step, carry):
+        to = (at.flat + step) % 32
+        remote(
+            notes.at[to],
+            v.notes_in.at[at.flat],
+            v.s_misc.at[5],
+            v.r_misc.at[5],
+            (to // 4, to % 4),
+        ).start()
+        return carry
+
+    lax.fori_loop(1, 32, spread, 0)
+
+    def features(b):
+        return contract_rows(xs[:, lanes(b)], dqkv[...])
+
+    for r in range(4):
+        v.w_sib_out[r] = features(2 * at.chip(r) + 1 - at.c)
+        remote(
+            v.w_sib_out.at[r], v.w_sib_in.at[r], v.s_ws.at[r], v.r_ws.at[r], at.sibling()
+        ).start()
+    plane_w = 2 * (at.z // 2) + at.y
+    for r in range(4):
+        total = features(2 * at.chip(r) + at.c)
+        wait_bytes(v.w_sib_in.at[r], v.r_ws.at[r])
+        v.w_out[r] = (total + v.w_sib_in[r]).astype(BF16)
+        send_or_copy(
+            v.w_out.at[r],
+            v.w_in.at[parity, at.x],
+            v.s_misc.at[6],
+            v.r_misc.at[6],
+            at.peer(r)[:1] + (plane_w,),
+            plane_w == at.z if r == 0 else None,
+        )
+
+    plane_grads(
+        at, v.g_back, v.zg_back, v.gs_back, v.fin_back, v.r_zg.at[0], v.s_misc.at[7], v.r_misc.at[7]
+    )
+    out_scatter.scatter_arrive(peer_in)
+
+    def out_rows(rows):
+        own = pl.ds(pl.multiple_of(at.c * 128 + rows.start, 32), 32)
+        total = (
+            terms[0, own]
+            + peer_in[1, rows].astype(F32)
+            + peer_in[2, rows].astype(F32)
+            + peer_in[3, rows].astype(F32)
+        )
+        v.o_out[rows] = total.astype(BF16)
+
+    by_rows(128, 32, out_rows)
+    wide = pl.ds(pl.multiple_of(at.z * 256, 256), 256)
+    pltpu.make_async_copy(v.o_out.at[:, wide], v.o_in.at[0], v.r_misc.at[8]).start()
+    for dz in range(1, 4):
+        plane = (at.z + dz) % 4
+        remote(
+            v.o_out.at[:, pl.ds(pl.multiple_of(plane * 256, 256), 256)],
+            v.o_in.at[dz],
+            v.s_misc.at[8],
+            v.r_misc.at[8],
+            (at.b, plane),
+        ).start()
+
+    z_out, z_in = v.z_out, v.z_in
+    for dz in (2, 1, 3, 0):
+        plane = (at.z + dz) % 4
+        rows = slot_rows(plane)
+        for r in (3, 1, 2):
+            wait_bytes(x_in.at[r, rows], v.r_dx.at[r, dz])
+        total = (
+            v.x_sum[rows]
+            + x_in[1, rows].astype(F32)
+            + x_in[2, rows].astype(F32)
+            + x_in[3, rows].astype(F32)
+        )
+        if dz:
+            z_out[dz] = total.astype(BF16)
+            remote(
+                z_out.at[dz], z_in.at[dz], v.s_dz.at[dz], v.r_dz.at[dz], (at.b, plane)
+            ).start()
+        else:
+            v.x_own[...] = total
+    plane_grads(
+        at, v.g_in, v.zg_in, v.gs_in, v.fin_in, v.r_zg.at[1], v.s_misc.at[9], v.r_misc.at[9]
+    )
+    for dz in (1, 2, 3):
+        wait_bytes(z_in.at[dz], v.r_dz.at[dz])
+    same = slot_rows(parity)
+    v.gtok[same] = (v.d1[same] + v.x_own[...] + z_in[2].astype(F32)).astype(BF16)
+    cross = slot_rows(1 - parity)
+    v.gtok[cross] = (v.d1[cross] + z_in[1].astype(F32) + z_in[3].astype(F32)).astype(BF16)
+
+    wait_bytes(v.o_in, v.r_misc.at[8])
+    wait_bytes(v.w_in, v.r_misc.at[6])
+    wait_bytes(v.notes_in, v.r_misc.at[5])
+    wait_bytes(v.fin_back, v.r_misc.at[7])
+    wait_bytes(v.fin_in, v.r_misc.at[9])
+
+
+def end_phase(at, v, col_in, col_back, exchanges):
+    gather, scatter, gather2, scatter2, out_scatter = exchanges
+    slot = v.xs.at[slot_rows(0)]
+    for dz in range(1, 4):
+        wait_bytes(slot, v.s_z.at[dz])
+    for r in (1, 2, 3):
+        for dz in range(4):
+            wait_bytes(slot, v.s_p.at[r, dz])
+            wait_bytes(slot, v.s_dx.at[r, dz])
+    near = at.parity == at.y
+
+    @pl.when(jnp.logical_not(near))
+    def _():
+        wait_bytes(v.wqkv.at[pl.ds(0, 512)], v.s_w.at[0])
+
+    @pl.when(near)
+    def _():
+        wait_bytes(v.wqkv.at[pl.ds(0, 384)], v.s_w.at[0])
+
+    wait_bytes(v.wqkv.at[pl.ds(0, 512)], v.s_w.at[1])
+    seven = v.wi.at[pl.ds(0, 896), pl.ds(0, 128)]
+    for i in (0, 2, 7, 9):
+        wait_bytes(seven, v.s_misc.at[i])
+    wait_bytes(v.smalls.at[pl.ds(0, 31)], v.s_misc.at[1])
+    wait_bytes(v.wo.at[pl.ds(0, 768), pl.ds(0, 128)], v.s_o.at[0])
+    for r in range(1, 8):
+        wait_bytes(v.wo.at[:, pl.ds(0, 128)], v.s_o.at[r])
+    for r in range(4):
+        for k in range(2):
+            wait_bytes(v.keys_all.at[pl.ds(0, 256)], v.s_kv.at[k, r])
+    for i in (3, 4):
+        wait_bytes(v.att_send.at[pl.ds(0, 960)], v.s_misc.at[i])
+    col_in.end()
+    col_back.end()
+    for dz in (1, 2, 3):
+        for k in range(2):
+            wait_bytes(v.zg_in.at[dz], v.s_zg.at[k, dz])
+        wait_bytes(v.z_out.at[dz], v.s_dz.at[dz])
+    for k in range(2):
+        wait_bytes(v.sib_k, v.s_kv2.at[k])
+    wait_bytes(v.notes.at[pl.ds(0, 31)], v.s_misc.at[5])
+    for r in range(4):
+        wait_bytes(v.w_sib_out.at[r], v.s_ws.at[r])
+    plane_w = 2 * (at.z // 2) + at.y
+
+    @pl.when(plane_w == at.z)
+    def _():
+        wait_bytes(v.w_out.at[pl.ds(0, 3)], v.s_misc.at[6])
+
+    @pl.when(plane_w != at.z)
+    def _():
+        wait_bytes(v.w_out, v.s_misc.at[6])
+
+    wait_bytes(v.o_in.at[pl.ds(0, 3)], v.s_misc.at[8])
+    gather2.gather_end(v.grad_slots)
+    scatter2.scatter_end(v.sib_out.at[1], v.peer_out.at[1])
+    out_scatter.scatter_end(v.sib_out.at[0], v.peer_out.at[0])
+
+
+def finish_kernel(
+    place_ref,
+    out_in,
+    gtok_in,
+    w_in,
+    o_in,
+    fin_in,
+    fin_back,
+    notes_in,
+    out_ref,
+    gtok_ref,
+    gq_ref,
+    gk_ref,
+    gv_ref,
+    gout_ref,
+    gwin_ref,
+    gwback_ref,
+    small_ref,
+    bin_ref,
+):
+    out_ref[...] = out_in[...]
+    gtok_ref[...] = gtok_in[...]
+    for x in range(2):
+        total = w_in[0, x].astype(F32) + w_in[1, x].astype(F32)
+        for k, ref in enumerate((gq_ref, gk_ref, gv_ref)):
+            ref[:, 128 * x : 128 * x + 128] = total[:, 128 * k : 128 * k + 128]
+    gout_ref[...] = (
+        o_in[0].astype(F32) + o_in[1].astype(F32) + o_in[2].astype(F32) + o_in[3].astype(F32)
+    ).T
+    gwin_ref[...] = fin_in[...].astype(F32)
+    gwback_ref[...] = fin_back[...].astype(F32)
+    total = notes_in[0]
+    for d in range(1, 32):
+        total += notes_in[d]
+    z = place_ref[0]
+    part = jnp.zeros((8, 32), F32)
+    for k in range(4):
+        part += jnp.where(z == k, total[0:8, 32 * k : 32 * k + 32], 0.0)
+    small_ref[...] = part
+    bin_ref[...] = total[8:9, :]
+
+
+def vmem():
+    return pl.BlockSpec(memory_space=pltpu.VMEM)
+
+
+def run_layer(*args):
+    scratch = [pltpu.VMEM(s, t) for _, s, t in SCRATCH]
+    for _, shape in SEMAPHORES:
+        scratch += [DMA(shape), DMA(shape)]
+    return pl.pallas_call(
+        layer_kernel,
+        out_shape=[jax.ShapeDtypeStruct(s, t) for _, s, t in RESULTS],
+        in_specs=[vmem()] * len(args),
+        out_specs=[vmem()] * len(RESULTS),
+        scratch_shapes=scratch,
+        compiler_params=pltpu.CompilerParams(
+            collective_id=1, has_side_effects=True, vmem_limit_bytes=VMEM_LIMIT
+        ),
+    )(*args)
+
+
+def run_finish(*args):
+    shapes = (
+        ((128, 1024), BF16),
+        ((128, 1024), BF16),
+        ((128, 256), F32),
+        ((128, 256), F32),
+        ((128, 256), F32),
+        ((256, 128), F32),
+        ((128, 1024), F32),
+        ((128, 1024), F32),
+        ((8, 32), F32),
+        ((1, 128), F32),
+    )
+    return pl.pallas_call(
+        finish_kernel,
+        out_shape=[jax.ShapeDtypeStruct(s, t) for s, t in shapes],
+        in_specs=[pl.BlockSpec(memory_space=pltpu.SMEM)] + [vmem()] * (len(args) - 1),
+        out_specs=[vmem()] * len(shapes),
+        compiler_params=pltpu.CompilerParams(vmem_limit_bytes=32 * 2**20),
+    )(*args)
+
+
+DMA = pltpu.SemaphoreType.DMA
+
+
+def fast_device(
+    tokens,
+    w_query,
+    w_key,
+    w_value,
+    w_out,
+    b_query,
+    b_value,
+    b_out,
+    norm1_gain,
+    norm1_shift,
+    w_in,
+    w_back,
+    b_in,
+    b_back,
+    norm2_gain,
+    norm2_shift,
+    cotangent,
+):
+    head_id = lax.axis_index("head")
+    token_shape = tokens.shape
+    model_dim = tokens.shape[2]
+    x = tokens.reshape(-1, model_dim)
+    vectors = jnp.stack(
+        (b_query, b_value, b_out, norm1_gain, norm1_shift, b_back, norm2_gain, norm2_shift)
+    )
+    spread = jnp.where(
+        lax.broadcasted_iota(jnp.int32, (1, 128), 1) // 32 == head_id,
+        jnp.tile(vectors, (1, 4)),
+        jnp.zeros((), BF16),
+    )
+    small = jnp.concatenate((spread, b_in[None], jnp.zeros((7, 128), BF16)), axis=0)
+    results = run_layer(
+        x, w_query, w_key, w_value, w_out, small, w_in, w_back, cotangent.reshape(-1, model_dim)
+    )
+    output, grad_tokens, gq, gk, gv, gout, gw_in, gw_back, own, gb_in = run_finish(
+        head_id.astype(jnp.int32).reshape(1), *results
+    )
+    return (
+        output.reshape(token_shape),
+        grad_tokens.reshape(token_shape),
+        gq,
+        gk,
+        gv,
+        gout,
+        own[0],
+        own[1],
+        own[2],
+        own[3],
+        own[4],
+        gw_in,
+        gw_back,
+        gb_in.reshape(-1),
+        own[5],
+        own[6],
+        own[7],
+    )
+
+
 def solution(mesh):
     in_specs = (
         P(None, ("blk", "head"), None),
@@ -325,6 +1454,8 @@
         P(("blk", "head")),
         P(("blk", "head")),
     )
+    sizes = (mesh.shape["blk"], mesh.shape["head"])
+    body = fast_device if sizes == (8, 4) else per_device
     return jax.shard_map(
-        per_device, mesh=mesh, in_specs=in_specs, out_specs=out_specs, check_vma=False
-    )
+        body, mesh=mesh, in_specs=in_specs, out_specs=out_specs, check_vma=False
+    )

time: 1120 us -> 218 us (0.19)
  waiting for transfers between devices: 722 us -> 0 us
  Pallas kernels: 0 us -> 208 us
  blocking collectives: 189 us -> 0 us
  matrix products: 106 us -> 0 us
  other arithmetic: 38 us -> 0.68 us
  local copies, waits for them, and re-layouts: 40.5 us -> 8.7 us
  between operations: 14.8 us -> 0.77 us
    all_gather x9 -> x0, waiting for transfers between devices: 366 us -> none  [the longest x1 235 us: per_device(): ffn_full = lax.all_gather(ffn_cols, 'head', axis=2, tiled=True)]
    reduce_scatter x6 -> x0, waiting for transfers between devices: 355 us -> none  [the longest x1 226 us: per_device(): lax.psum_scatter(jnp.stack((grad_in_whole, grad_back_whole)).astype(jnp.b...]
    pallas_call x0 -> x2, Pallas kernels: none -> 208 us  [the longest x1 206 us: run_layer(): pl.pallas_call(layer_kernel, out_shape=[jax.ShapeDtypeStruct(s, t) for _,...]
    all_gather x4 -> x0, blocking collectives: 107 us -> none  [the longest x1 75.8 us: per_device(): lax.all_gather(b_in, ('blk', 'head'), axis=0, tiled=True)]
    dot_general x24 -> x0, matrix products: 106 us -> none  [the longest x2 16.6 us: score_block(): jnp.einsum('sqge,skge->sqgk', queries4, keys4, preferred_element_type=jnp...]
    unnamed x2 -> x0, blocking collectives: 81.6 us -> none
    reduce_sum x11 -> x0, other arithmetic: 15.2 us -> none  [the longest x1 8.49 us: per_device(): totals = jnp.sum(weights, axis=-1)]
    another operation x5 -> x0, other arithmetic: 12.1 us -> none  [the longest x1 6.81 us: per_device(): jnp.stack((grad_in_whole, grad_back_whole)).astype(jnp.bfloat16)]
  transfers between devices with their start and end apart: 15 -> 0, of which waited for: 11 -> 0; matrix products, arithmetic and copies ran while one was open for 14% -> 0% of each run, Pallas kernels for 0% -> 0%
where the time goes in v3:
time: 218 us
  Pallas kernels  208 us (95%)
  local copies, waits for them, and re-layouts  8.7 us (4%)
    pallas_call x1, Pallas kernels, run_layer(): pl.pallas_call(layer_kernel, out_shape=[jax.ShapeDtypeStruct(s, t) for _,...  206 us
    unnamed x32, local copies, waits for them, and re-layouts  7.94 us

profile of v3, /device:TPU:0, one launch (start us, length us, event | category | flops | bytes accessed | tf_op | source)
XLA Modules:
  0.0 218.0 jit_solution(13553292282541872944)
XLA Ops:
  0.7 0.0 copy-start.15
  0.7 0.0 copy-start.11
  0.7 0.0 copy-start.12
  0.7 0.0 copy-start.13
  0.7 0.0 copy-start.14
  0.7 0.0 copy-start.8
  0.8 0.0 copy-start.9
  0.8 0.0 copy-start.10
  0.8 0.1 pad.2.clone
  0.9 0.5 copy-done.15
  1.3 0.0 copy-done.11
  1.3 0.0 copy-done.12
  1.4 0.0 copy-done.13
  1.4 0.0 copy-done.14
  1.4 0.0 copy-done.8
  1.4 0.0 copy-done.9
  1.4 0.0 copy-done.10
  1.5 0.1 tile.10
  1.6 0.0 copy-start.7
  1.6 0.6 copy-done.7
  2.2 0.7 maximum_maximum_fusion.refs_5_
  2.9 206.5 %shard_map.296 = (bf16[128,1024]{1,0:T(8,128)(2,1)}, bf16[128,1024]{1,0:T(8,128)(2,1)}, bf16[2,2,128,384]{3,2,1,0:T(8,128)(2,1)}, bf16[4,128,256]{2,1,0:T(8,128)...) custom-call(bf16[128,1024]{1,0:T(8,128)(2,1)} %bitcast.31, ...), custom_call_target="tpu_custom_call" | custom-call | tf_op jit(solution)/shard_map/pallas_call | solution.py:1322
  209.4 0.0 copy-start
  209.4 1.0 copy-done
  210.4 0.0 copy-start.1
  210.4 0.9 copy-done.1
  211.3 0.0 copy-start.2
  211.3 0.9 copy-done.2
  212.3 0.0 copy-start.3
  212.3 0.9 copy-done.3
  213.2 0.0 copy-start.4
  213.2 0.9 copy-done.4
  214.2 0.0 copy-start.5
  214.2 0.9 copy-done.5
  215.1 0.0 copy-start.6
  215.1 0.9 copy-done.6
  216.1 1.4 shard_map.297
  217.5 0.5 slice_bitcast_fusion
  (5 shorter events, 0.1 us)
Async XLA Ops:
  0.7 0.7 copy-start.15
  0.7 0.7 copy-start.11
  0.7 0.7 copy-start.12
  0.7 0.7 copy-start.13
  0.7 0.7 copy-start.14
  0.7 0.7 copy-start.8
  0.8 0.7 copy-start.9
  0.8 0.7 copy-start.10
  1.6 0.7 copy-start.7
  209.4 1.0 copy-start
  210.4 0.9 copy-start.1
  211.3 0.9 copy-start.2
  212.3 0.9 copy-start.3
  213.2 0.9 copy-start.4
  214.2 0.9 copy-start.5
  215.1 0.9 copy-start.6

commit v4 on v3

--- a/solution.py
+++ b/solution.py
@@ -294,7 +294,7 @@
 MESH = pl.DeviceIdType.MESH
 F32 = jnp.float32
 BF16 = jnp.bfloat16
-VMEM_LIMIT = 60 * 2**20
+VMEM_LIMIT = 62 * 2**20
 
 
 def dot_nn(left, right):
@@ -366,79 +366,117 @@
     lax.fori_loop(0, count // size, body, 0)
 
 
-def row_sums(count, size, width, step):
-    def body(i, carry):
-        parts = step(pl.ds(pl.multiple_of(i * size, size), size))
-        return tuple(
-            kept + jnp.sum(part.reshape(size // 8, 8, width), axis=0)
-            for kept, part in zip(carry, parts)
+class Spread:
+    def __init__(self, at, block, part, send, recv):
+        self.at, self.block, self.part = at, block, part
+        self.send, self.recv = send, recv
+
+    def start(self):
+        mine = self.block(0)
+        for i in (0, 1):
+            for r, k in ((1, i), (2, 1 - i)):
+                piece = self.part(mine, k)
+                remote(piece, piece, self.send.at[r, k], self.recv.at[r, k], self.at.peer(r)).start()
+
+    def relay(self):
+        for r, k in ((1, 0), (2, 1)):
+            piece = self.part(self.block(r), k)
+            wait_bytes(piece, self.recv.at[r, k])
+            remote(piece, piece, self.send.at[0, k], self.recv.at[0, k], self.at.peer(3 - r)).start()
+
+    def rest(self, r):
+        block = self.block(r)
+        for row, k in {1: ((1, 1),), 2: ((2, 0),), 3: ((0, 0), (0, 1))}[r]:
+            wait_bytes(self.part(block, k), self.recv.at[row, k])
+
+    def end(self):
+        mine = self.block(0)
+        for row in range(3):
+            for k in range(2):
+                wait_bytes(self.part(mine, k), self.send.at[row, k])
+
+
+def part_rows(h, core):
+    return pl.ds(pl.multiple_of(h * 128 + core * 64, 64), 64)
+
+
+class Gather:
+    def __init__(self, at, slots, h, send, recv, send_sib, recv_sib):
+        self.at, self.slots, self.h = at, slots, h
+        self.send_sib, self.recv_sib = send_sib, recv_sib
+
+        def part(block, k):
+            return block.at[pl.ds(k * 32, 32)]
+
+        self.spread = Spread(
+            at, lambda r: slots.at[at.chip(r), part_rows(h, at.c)], part, send, recv
         )
 
-    n = step.count
-    sums = lax.fori_loop(
-        0, count // size, body, tuple(jnp.zeros((8, width), F32) for _ in range(n))
-    )
-    return tuple(jnp.sum(s, axis=0, keepdims=True) for s in sums)
+    def to_sibling(self, r):
+        block = self.spread.block(r)
+        remote(
+            block, block, self.send_sib.at[r], self.recv_sib.at[r], self.at.sibling()
+        ).start()
+
+    def start(self):
+        self.spread.start()
+        self.to_sibling(0)
+
+    def relay(self):
+        self.spread.relay()
+
+    def step(self, r):
+        at = self.at
+        if r:
+            self.spread.rest(r)
+            self.to_sibling(r)
+        wait_bytes(self.slots.at[at.chip(r), part_rows(self.h, 1 - at.c)], self.recv_sib.at[r])
+        return at.chip(r)
+
+    def end(self):
+        self.spread.end()
+        for r in range(4):
+            wait_bytes(self.spread.block(r), self.send_sib.at[r])
 
 
 class Exchange:
-    def __init__(self, at, send, recv, send_sib, recv_sib):
+    def __init__(self, at, buffers, rows, send, recv, send_sib, recv_sib):
         self.at, self.send, self.recv = at, send, recv
         self.send_sib, self.recv_sib = send_sib, recv_sib
-
-    def gather_start(self, slots):
-        at = self.at
-        mine = slots.at[at.q, half(at.c)]
+        self.sib_out, self.sib_in, self.out, self.into = buffers
+        self.rows = rows
+
+    def put(self, r, theirs):
+        mine = self.sib_out.at[r, self.rows]
+        mine[...] = theirs.astype(BF16)
+        remote(
+            mine,
+            self.sib_in.at[r, self.rows],
+            self.send_sib.at[r],
+            self.recv_sib.at[r],
+            self.at.sibling(),
+        ).start()
+
+    def add(self, r, mine):
+        wait_bytes(self.sib_in.at[r, self.rows], self.recv_sib.at[r])
+        total = mine + self.sib_in[r, self.rows].astype(F32)
+        if r == 0:
+            return total
+        held = self.out.at[r, self.rows]
+        held[...] = total.astype(BF16)
+        remote(
+            held, self.into.at[r, self.rows], self.send.at[r], self.recv.at[r], self.at.peer(r)
+        ).start()
+
+    def arrive(self):
         for r in (1, 2, 3):
-            remote(mine, mine, self.send.at[r], self.recv.at[r], at.peer(r)).start()
-        remote(mine, mine, self.send_sib.at[0], self.recv_sib.at[0], at.sibling()).start()
-
-    def gather_step(self, slots, r):
-        at = self.at
-        chip = at.chip(r)
-        block = slots.at[chip, half(at.c)]
-        if r:
-            wait_bytes(block, self.recv.at[r])
-            remote(
-                block, block, self.send_sib.at[r], self.recv_sib.at[r], at.sibling()
-            ).start()
-        wait_bytes(slots.at[chip, half(1 - at.c)], self.recv_sib.at[r])
-        return chip
-
-    def gather_end(self, slots):
-        at = self.at
+            wait_bytes(self.into.at[r, self.rows], self.recv.at[r])
+
+    def end(self):
         for r in range(4):
-            block = slots.at[at.chip(r), half(at.c)]
+            wait_bytes(self.sib_out.at[r, self.rows], self.send_sib.at[r])
             if r:
-                wait_bytes(slots.at[at.q, half(at.c)], self.send.at[r])
-            wait_bytes(block, self.send_sib.at[r])
-
-    def scatter_put(self, terms, out_sib, in_sib, r):
-        at = self.at
-        out_sib[r] = terms[r, half(1 - at.c)].astype(BF16)
-        remote(
-            out_sib.at[r], in_sib.at[r], self.send_sib.at[r], self.recv_sib.at[r], at.sibling()
-        ).start()
-
-    def scatter_pass(self, terms, in_sib, out, into, r):
-        at = self.at
-        wait_bytes(in_sib.at[r], self.recv_sib.at[r])
-        total = terms[r, half(at.c)] + in_sib[r].astype(F32)
-        if r:
-            out[r] = total.astype(BF16)
-            remote(out.at[r], into.at[r], self.send.at[r], self.recv.at[r], at.peer(r)).start()
-        else:
-            terms[0, half(at.c)] = total
-
-    def scatter_arrive(self, into):
-        for r in (1, 2, 3):
-            wait_bytes(into.at[r], self.recv.at[r])
-
-    def scatter_end(self, out_sib, out):
-        for r in range(4):
-            wait_bytes(out_sib.at[r], self.send_sib.at[r])
-            if r:
-                wait_bytes(out.at[r], self.send.at[r])
+                wait_bytes(self.out.at[r, self.rows], self.send.at[r])
 
 
 def norm_rows(values):
@@ -528,41 +566,93 @@
     lax.fori_loop(1, 8, push, 0)
 
 
-def column_grads(at, blocks, into, send_sem, recv_sem):
-    for dz in (2, 1, 3):
-        plane = (at.z + dz) % 4
-        remote(
-            blocks.at[:, :, lanes(plane)],
-            into.at[dz],
-            send_sem.at[dz],
-            recv_sem.at[dz],
-            (at.b, plane),
-        ).start()
-
-
-def plane_grads(at, blocks, into, sums, final, recv_sem, send_out, recv_out):
-    for dz in (1, 3, 2):
-        wait_bytes(into.at[dz], recv_sem.at[dz])
-
-    def one(step, carry):
-        other = (at.b + 1 + step) % 8
-        sums[other] = (
-            blocks[other, :, lanes(at.z)].astype(F32)
-            + into[1, other].astype(F32)
-            + into[2, other].astype(F32)
-            + into[3, other].astype(F32)
-        ).astype(BF16)
-        send_or_copy(
-            sums.at[other],
-            final.at[:, lanes(at.b)],
-            send_out,
-            recv_out,
-            (other, at.z),
-            step == 7,
-        )
-        return carry
-
-    lax.fori_loop(0, 8, one, 0)
+class ColumnSum:
+    def __init__(self, at, blocks, passing, send, recv):
+        self.at, self.blocks, self.passing = at, blocks, passing
+        self.send_sem, self.recv_sem = send, recv
+
+    def plane(self, side, i):
+        return i if side else 3 - i
+
+    def hop(self, side):
+        return 3 - self.at.z if side else self.at.z
+
+    def next(self, side):
+        return (self.at.b, self.at.z + 1 - 2 * side)
+
+    def begin(self, which):
+        for side in range(2):
+
+            @pl.when(self.hop(side) == 0)
+            def _(side=side):
+                for i in which:
+                    remote(
+                        self.blocks.at[:, :, pl.ds(128 * self.plane(side, i), 128)],
+                        self.passing.at[side, i],
+                        self.send_sem.at[side, i],
+                        self.recv_sem.at[side, i],
+                        self.next(side),
+                    ).start()
+
+    def relay(self, hop, i):
+        for side in range(2):
+
+            @pl.when(self.hop(side) == hop)
+            def _(side=side):
+                held = self.passing.at[side, i]
+                wait_bytes(held, self.recv_sem.at[side, i])
+                cols = pl.ds(128 * self.plane(side, i), 128)
+                for b in range(8):
+                    self.passing[side, i, b] = (
+                        self.passing[side, i, b].astype(F32)
+                        + self.blocks[b, :, cols].astype(F32)
+                    ).astype(BF16)
+                remote(
+                    held,
+                    held,
+                    self.send_sem.at[side, i],
+                    self.recv_sem.at[side, i],
+                    self.next(side),
+                ).start()
+
+    def finish(self, sums, final, send_out, recv_out):
+        at = self.at
+        own = lanes(at.z)
+        for b in range(8):
+            sums[b] = self.blocks[b, :, own]
+        for side in range(2):
+            for hop in range(1, 4):
+                i = 3 - hop
+
+                @pl.when(self.hop(side) == hop)
+                def _(side=side, i=i):
+                    wait_bytes(self.passing.at[side, i], self.recv_sem.at[side, i])
+                    for b in range(8):
+                        sums[b] = (
+                            sums[b].astype(F32) + self.passing[side, i, b].astype(F32)
+                        ).astype(BF16)
+
+        def one(step, carry):
+            other = (at.b + 1 + step) % 8
+            send_or_copy(
+                sums.at[other],
+                final.at[:, lanes(at.b)],
+                send_out,
+                recv_out,
+                (other, at.z),
+                step == 7,
+            )
+            return carry
+
+        lax.fori_loop(0, 8, one, 0)
+
+    def end(self):
+        for side in range(2):
+            for i in range(3):
+
+                @pl.when(self.hop(side) < 3 - i)
+                def _(side=side, i=i):
+                    wait_bytes(self.passing.at[side, i], self.send_sem.at[side, i])
 
 
 def head_mask(h):
@@ -582,102 +672,116 @@
     return pl.ds(pl.multiple_of(index * 1024, 1024), 1024)
 
 
-INPUTS = ("x", "wq", "wk", "wv", "wout", "small", "win", "wback", "cot")
-
-RESULTS = (
-    ("out", (128, 1024), BF16),
-    ("gtok", (128, 1024), BF16),
-    ("w_in", (2, 2, 128, 384), BF16),
-    ("o_in", (4, 128, 256), BF16),
-    ("fin_in", (128, 1024), BF16),
-    ("fin_back", (128, 1024), BF16),
-    ("notes_in", (32, 16, 128), F32),
-)
-
-SCRATCH = (
-    ("xs", (1024, 1024), BF16),
-    ("wqkv", (1024, 384), BF16),
-    ("queries", (1024, 128), BF16),
-    ("keys_all", (2048, 128), BF16),
-    ("values_all", (2048, 128), BF16),
-    ("mixed", (1024, 128), F32),
-    ("log_sums", (1024, 128), F32),
-    ("att", (128, 1024), BF16),
-    ("wo", (1024, 1024), BF16),
-    ("par", (8, 1024), F32),
-    ("bins", (1, 512), F32),
-    ("wi", (1024, 512), BF16),
-    ("wb", (1024, 512), BF16),
-    ("smalls", (32, 16, 128), BF16),
-    ("proj", (256, 384), F32),
-    ("scores", (256, 2048), F32),
-    ("d_buf", (256, 2048), F32),
-    ("p_buf", (256, 2048), BF16),
-    ("att_send", (1024, 128), BF16),
-    ("n1", (128, 1024), F32),
-    ("unit1", (128, 1024), F32),
-    ("scale1", (128, 128), F32),
-    ("d2", (128, 1024), F32),
-    ("d1", (128, 1024), F32),
-    ("db", (128, 1024), BF16),
-    ("norm_slots", (4, 256, 1024), BF16),
-    ("grad_slots", (4, 256, 1024), BF16),
-    ("hid", (4, 256, 512), BF16),
-    ("slope", (4, 256, 512), F32),
-    ("pre", (256, 512), F32),
-    ("terms", (4, 256, 1024), F32),
-    ("sib_out", (2, 4, 128, 1024), BF16),
-    ("sib_in", (2, 4, 128, 1024), BF16),
-    ("peer_out", (2, 4, 128, 1024), BF16),
-    ("peer_in", (2, 4, 128, 1024), BF16),
-    ("g_back", (8, 128, 512), BF16),
-    ("g_in", (8, 128, 512), BF16),
-    ("zg_back", (4, 8, 128, 128), BF16),
-    ("zg_in", (4, 8, 128, 128), BF16),
-    ("gs_back", (8, 128, 128), BF16),
-    ("gs_in", (8, 128, 128), BF16),
-    ("da_send", (128, 1024), BF16),
-    ("da", (1024, 128), BF16),
-    ("q_turned", (128, 1024), BF16),
-    ("da_turned", (128, 1024), BF16),
-    ("dq", (1024, 128), F32),
-    ("dk_turned", (128, 2048), F32),
-    ("dv_turned", (128, 2048), F32),
-    ("out_k", (1024, 128), F32),
-    ("out_v", (1024, 128), F32),
-    ("sib_k", (1024, 128), F32),
-    ("sib_v", (1024, 128), F32),
-    ("dqkv", (1024, 384), BF16),
-    ("x_in", (4, 256, 1024), BF16),
-    ("x_sum", (256, 1024), F32),
-    ("x_own", (64, 1024), F32),
-    ("z_out", (4, 64, 1024), BF16),
-    ("z_in", (4, 64, 1024), BF16),
-    ("w_sib_out", (4, 128, 384), F32),
-    ("w_sib_in", (4, 128, 384), F32),
-    ("w_out", (4, 128, 384), BF16),
-    ("o_out", (128, 1024), BF16),
-    ("vec", (8, 1024), F32),
-    ("gbin", (1, 512), F32),
-    ("notes", (32, 16, 128), F32),
-)
-
-SEMAPHORES = (
-    ("z", (4,)),
-    ("p", (4, 4)),
-    ("w", (2,)),
-    ("o", (8,)),
-    ("kv", (2, 4)),
-    ("misc", (12,)),
-    ("col", (4, 3)),
-    ("ex", (5, 4)),
-    ("ex_sib", (5, 4)),
-    ("zg", (2, 4)),
-    ("kv2", (2,)),
-    ("dx", (4, 4)),
-    ("dz", (4,)),
-    ("ws", (4,)),
-)
+class Inputs:
+    x = wq = wk = wv = wout = small = win = wback = cot = None
+
+
+def entries(table):
+    return [(n, e) for n, e in vars(table).items() if n[0] != "_"]
+
+
+class Results:
+    out = ((128, 1024), BF16)
+    gtok = ((128, 1024), BF16)
+    w_in = ((2, 2, 128, 384), BF16)
+    o_in = ((4, 128, 256), BF16)
+    fin_in = ((128, 1024), BF16)
+    fin_back = ((128, 1024), BF16)
+    notes_in = ((4, 16, 128), F32)
+
+
+class Scratch:
+    xs = ((1024, 1024), BF16)
+    wqkv = ((1024, 384), BF16)
+    w_near = ((3, 128, 256), BF16)
+    queries = ((1024, 128), BF16)
+    keys_all = ((2048, 128), BF16)
+    values_all = ((2048, 128), BF16)
+    mixed = ((1024, 128), F32)
+    log_sums = ((1024, 128), F32)
+    att = ((128, 1024), BF16)
+    wo = ((1024, 1024), BF16)
+    par = ((8, 1024), F32)
+    bins = ((1, 512), F32)
+    wi = ((1024, 512), BF16)
+    wb = ((1024, 512), BF16)
+    smalls = ((8, 16, 128), BF16)
+    smalls_z = ((4, 16, 128), BF16)
+    smalls_sum = ((16, 128), BF16)
+    proj = ((256, 384), F32)
+    scores = ((256, 2048), F32)
+    d_buf = ((256, 2048), F32)
+    p_buf = ((256, 2048), BF16)
+    att_send = ((1024, 128), BF16)
+    n1 = ((128, 1024), F32)
+    unit1 = ((128, 1024), F32)
+    scale1 = ((128, 128), F32)
+    d2 = ((128, 1024), F32)
+    d1 = ((128, 1024), F32)
+    db = ((128, 1024), BF16)
+    norm_slots = ((4, 256, 1024), BF16)
+    grad_slots = ((4, 256, 1024), BF16)
+    hid = ((4, 256, 512), BF16)
+    slope = ((4, 256, 512), F32)
+    low = ((4, 256, 512), BF16)
+    pre = ((128, 512), F32)
+    terms = ((4, 256, 1024), F32)
+    sib_out = ((2, 4, 128, 1024), BF16)
+    sib_in = ((2, 4, 128, 1024), BF16)
+    peer_out = ((2, 4, 128, 1024), BF16)
+    peer_in = ((2, 4, 128, 1024), BF16)
+    g_back = ((8, 128, 512), BF16)
+    g_in = ((8, 128, 512), BF16)
+    pass_back = ((2, 3, 8, 128, 128), BF16)
+    pass_in = ((2, 3, 8, 128, 128), BF16)
+    gs_back = ((8, 128, 128), BF16)
+    gs_in = ((8, 128, 128), BF16)
+    da_send = ((128, 1024), BF16)
+    da = ((1024, 128), BF16)
+    q_turned = ((128, 1024), BF16)
+    da_turned = ((128, 1024), BF16)
+    dq = ((1024, 128), F32)
+    dk_turned = ((128, 2048), F32)
+    dv_turned = ((128, 2048), F32)
+    out_k = ((1024, 128), F32)
+    out_v = ((1024, 128), F32)
+    sib_k = ((1024, 128), F32)
+    sib_v = ((1024, 128), F32)
+    dqkv = ((1024, 384), BF16)
+    x_sum = ((256, 1024), F32)
+    x_own = ((64, 1024), F32)
+    z_out = ((4, 64, 1024), BF16)
+    z_in = ((4, 64, 1024), BF16)
+    w_sib_out = ((4, 128, 384), F32)
+    w_sib_in = ((4, 128, 384), F32)
+    w_out = ((4, 128, 384), BF16)
+    o_out = ((128, 1024), BF16)
+    vec = ((8, 1024), F32)
+    gbin = ((1, 512), F32)
+    notes = ((8, 16, 128), F32)
+    notes_p = ((8, 16, 128), F32)
+    notes_sum = ((16, 128), F32)
+
+
+class Semaphores:
+    z = (4,)
+    p = (4, 3, 2)
+    wo = (3, 2)
+    w = (3,)
+    o = (5,)
+    kv = (2, 4)
+    misc = (12,)
+    col = (4, 3)
+    ga = (4, 3, 2)
+    ga_sib = (4, 4)
+    ex = (5, 4)
+    ex_sib = (5, 4)
+    zg = (2, 2, 3)
+    kv2 = (2,)
+    dx = (4, 3, 2)
+    da = (4,)
+    dz = (4,)
+    ws = (4,)
 
 
 class Refs:
@@ -686,8 +790,8 @@
 
 def layer_kernel(*refs):
     v = Refs()
-    names = list(INPUTS) + [n for n, _, _ in RESULTS] + [n for n, _, _ in SCRATCH]
-    for n, _ in SEMAPHORES:
+    names = [n for table in (Inputs, Results, Scratch) for n, _ in entries(table)]
+    for n, _ in entries(Semaphores):
         names += ["s_" + n, "r_" + n]
     for name, ref in zip(names, refs):
         setattr(v, name, ref)
@@ -698,79 +802,133 @@
     at.pair = 4 * (at.z // 2) + at.q
     col_in = Column(at, v.wi, [s.at[0] for s in (v.s_col, v.r_col)] + [s.at[1] for s in (v.s_col, v.r_col)])
     col_back = Column(at, v.wb, [s.at[2] for s in (v.s_col, v.r_col)] + [s.at[3] for s in (v.s_col, v.r_col)])
-    exchanges = [
-        Exchange(at, v.s_ex.at[i], v.r_ex.at[i], v.s_ex_sib.at[i], v.r_ex_sib.at[i])
-        for i in range(5)
+    gathers = [
+        [
+            Gather(at, slots, h, *[t.at[2 * i + h] for t in (v.s_ga, v.r_ga, v.s_ga_sib, v.r_ga_sib)])
+            for h in range(2)
+        ]
+        for i, slots in enumerate((v.norm_slots, v.grad_slots))
     ]
+
+    def exchange(i, side, rows):
+        buffers = [t.at[side] for t in (v.sib_out, v.sib_in, v.peer_out, v.peer_in)]
+        sems = [t.at[i] for t in (v.s_ex, v.r_ex, v.s_ex_sib, v.r_ex_sib)]
+        return Exchange(at, buffers, rows, *sems)
+
+    scatters = [
+        [exchange(2 * i + h, i, pl.ds(64 * h, 64)) for h in range(2)] for i in range(2)
+    ]
+    out_scatter = exchange(4, 0, pl.ds(0, 128))
+    upper = at.z // 2
+    at.planes = (at.z, at.z + 1 - 2 * at.parity, 2 - upper, 3 - 3 * upper)
+    rows_spread = [
+        Spread(
+            at,
+            lambda r, plane=plane: v.xs.at[slot_rows(at.chip(r) * 4 + plane)],
+            lambda block, k: block.at[pl.ds(k * 32, 32)],
+            v.s_p.at[i],
+            v.r_p.at[i],
+        )
+        for i, plane in enumerate(at.planes)
+    ]
+    wo_spread = Spread(
+        at,
+        lambda r: v.wo.at[:, lanes(2 * at.chip(r) + at.c)],
+        lambda block, k: block.at[pl.ds(k * 512, 512)],
+        v.s_wo,
+        v.r_wo,
+    )
+    sum_in = ColumnSum(at, v.g_in, v.pass_in, v.s_zg.at[0], v.r_zg.at[0])
+    sum_back = ColumnSum(at, v.g_back, v.pass_back, v.s_zg.at[1], v.r_zg.at[1])
     greet_all(at)
-    attend_phase(at, v, col_in, col_back)
-    ffn_phase(at, v, col_in, col_back, exchanges)
-    grads_phase(at, v, exchanges[0], exchanges[4])
-    end_phase(at, v, col_in, col_back, exchanges)
-
-
-def attend_phase(at, v, col_in, col_back):
+    attend_phase(at, v, col_in, col_back, rows_spread, wo_spread)
+    ffn_phase(at, v, col_in, col_back, gathers, scatters, sum_back, sum_in)
+    grads_phase(at, v, gathers[0], scatters, out_scatter, sum_in, sum_back)
+    ends = rows_spread + [wo_spread, sum_in, sum_back] + scatters[1] + [out_scatter]
+    end_phase(at, v, col_in, col_back, ends)
+
+
+def attend_phase(at, v, col_in, col_back, rows_spread, wo_spread):
     xs, wqkv, wo = v.xs, v.wqkv, v.wo
     parity, pair = at.parity, at.pair
 
-    for dz in (1, 3, 2):
-        plane = (at.z + dz) % 4
+    pltpu.make_async_copy(v.small, v.smalls_z.at[at.z], v.r_misc.at[1]).start()
+    for dz in range(1, 4):
+        remote(
+            v.small,
+            v.smalls_z.at[at.z],
+            v.s_misc.at[1],
+            v.r_misc.at[1],
+            (at.b, (at.z + dz) % 4),
+        ).start()
+
+    pltpu.make_async_copy(
+        v.x.at[slot_rows(parity)], xs.at[slot_rows(at.place)], v.r_z.at[at.z]
+    ).start()
+    weights = (v.wq, v.wk, v.wv)
+    for i in (1, 2, 3):
+        plane = at.planes[i]
         remote(
             v.x.at[slot_rows(plane % 2)],
             xs.at[slot_rows(at.place)],
-            v.s_z.at[dz],
-            v.r_z.at[dz],
+            v.s_z.at[i],
+            v.r_z.at[at.z],
             (at.b, plane),
         ).start()
-    pltpu.make_async_copy(
-        v.x.at[slot_rows(parity)], xs.at[slot_rows(at.place)], v.r_z.at[0]
-    ).start()
-    plane_weights(at, v.win, v.wi, v.s_misc.at[0], v.r_misc.at[0])
-
-    for dx in range(2):
-        for dz in range(2):
+        if i == 1:
+            for k, w in enumerate(weights):
+                remote(
+                    w, v.w_near.at[k], v.s_w.at[2], v.r_w.at[2], (at.b, at.planes[1])
+                ).start()
+
+    part = wo.at[pl.ds(pl.multiple_of(at.z * 256, 256), 256), lanes(at.b)]
+    pltpu.make_async_copy(v.wout, part, v.r_o.at[4]).start()
+    for i in (1, 2, 3):
+        remote(v.wout, part, v.s_o.at[4], v.r_o.at[4], (at.b, at.planes[i])).start()
+
+    def to_pairs(sources, group):
+        for dx in range(2):
             column = (at.x + dx) % 2
-            plane = 2 * (at.z // 2) + (at.z + dz) % 2
-            target = 2 * (parity * 2 + column) + at.c
-            mine = jnp.logical_and(
-                parity == at.y, jnp.logical_and(column == at.x, plane == at.z)
-            )
-            for k, w in enumerate((v.wq, v.wk, v.wv)):
+            for k, w in enumerate(sources):
                 send_or_copy(
                     w.at[:, lanes(column)],
                     wqkv.at[lanes(at.b), pl.ds(k * 128, 128)],
                     v.s_w.at[0],
                     v.r_w.at[0],
-                    (target, plane),
-                    mine if dx == 0 and dz == 0 else None,
+                    (2 * (group * 2 + column) + at.c, at.z),
+                    None if dx else group == at.y,
                 )
 
-    pltpu.make_async_copy(v.small, v.smalls.at[at.flat], v.r_misc.at[1]).start()
-
-    def spread(step, carry):
-        other = (at.flat + step) % 32
-        remote(
-            v.small,
-            v.smalls.at[at.flat],
-            v.s_misc.at[1],
-            v.r_misc.at[1],
-            (other // 4, other % 4),
-        ).start()
-        return carry
-
-    lax.fori_loop(1, 32, spread, 0)
-
-    part = wo.at[pl.ds(pl.multiple_of(at.z * 256, 256), 256), lanes(at.b)]
-    pltpu.make_async_copy(v.wout, part, v.r_o.at[0]).start()
-    for dz in range(1, 4):
-        remote(v.wout, part, v.s_o.at[0], v.r_o.at[0], (at.b, (at.z + dz) % 4)).start()
-
-    for dz in (0, 1, 3, 2):
-        block = xs.at[slot_rows(at.q * 4 + (at.z - dz + 4) % 4)]
-        wait_bytes(block, v.r_z.at[dz])
-        for r in (1, 2, 3):
-            remote(block, block, v.s_p.at[r, dz], v.r_p.at[r, dz], at.peer(r)).start()
-
+    for i in range(4):
+        wait_bytes(rows_spread[i].block(0), v.r_z.at[at.planes[i]])
+        rows_spread[i].start()
+        if i == 0:
+            to_pairs(weights, parity)
+            wait_bytes(v.smalls_z, v.r_misc.at[1])
+            total = v.smalls_z[0].astype(F32)
+            for z in range(1, 4):
+                total += v.smalls_z[z].astype(F32)
+            v.smalls_sum[...] = total.astype(BF16)
+            mine = v.smalls.at[at.b]
+            pltpu.make_async_copy(v.smalls_sum, mine, v.r_misc.at[10]).start()
+
+            def spread(step, carry):
+                remote(
+                    v.smalls_sum,
+                    mine,
+                    v.s_misc.at[10],
+                    v.r_misc.at[10],
+                    ((at.b + step) % 8, at.z),
+                ).start()
+                return carry
+
+            lax.fori_loop(1, 8, spread, 0)
+        if i == 1:
+            plane_weights(at, v.win, v.wi, v.s_misc.at[0], v.r_misc.at[0])
+            wait_bytes(v.w_near, v.r_w.at[2])
+            to_pairs([v.w_near.at[k] for k in range(3)], 1 - parity)
+        if i:
+            rows_spread[i - 1].relay()
     wait_bytes(v.wi.at[:, pl.ds(0, 128)], v.r_misc.at[0])
     col_in.send(0)
 
@@ -778,24 +936,31 @@
     for r in range(4):
         part = wqkv.at[lanes(2 * at.chip(r) + at.c)]
         remote(part, part, v.s_w.at[1], v.r_w.at[1], at.sibling()).start()
-
-    wait_bytes(v.smalls, v.r_misc.at[1])
+    rows_spread[3].relay()
+
+    wait_bytes(v.smalls, v.r_misc.at[10])
     for b in range(8):
-        total = v.smalls[4 * b].astype(F32)
-        for z in range(1, 4):
-            total += v.smalls[4 * b + z].astype(F32)
-        v.par[:, 128 * b : 128 * b + 128] = total[0:8]
+        v.par[:, 128 * b : 128 * b + 128] = v.smalls[b].astype(F32)[0:8]
+    row = lax.broadcasted_iota(jnp.int32, (8, 128), 0)
     for h in range(4):
-        v.bins[0:1, 128 * h : 128 * h + 128] = v.smalls[8 * h + at.b].astype(F32)[8:9]
+        rows = v.smalls[2 * h + at.b // 4].astype(F32)[8:16]
+        rows = jnp.where(row == at.b % 4, rows, 0.0)
+        v.bins[0:1, 128 * h : 128 * h + 128] = jnp.sum(rows, axis=0, keepdims=True)
     bias_q = v.par[0:1, lanes(pair)]
     bias_v = v.par[1:2, lanes(pair)]
     wait_bytes(wqkv.at[pl.ds(0, 512)], v.r_w.at[1])
 
+    whole = wo_spread.block(0)
+    wait_bytes(whole, v.r_o.at[4])
+    wo_spread.start()
+    remote(whole, whole, v.s_o.at[0], v.r_o.at[0], at.sibling()).start()
+    plane_weights(at, v.wback, v.wb, v.s_misc.at[2], v.r_misc.at[2])
+
     for r in range(4):
         chip = at.chip(r)
         if r:
-            for dz in (0, 1, 3, 2):
-                wait_bytes(xs.at[slot_rows(0)], v.r_p.at[r, dz])
+            for i in range(4):
+                rows_spread[i].rest(r)
         rows = chip_rows(chip)
         v.proj[...] = dot_nn(xs[rows], wqkv[...])
         v.queries[rows] = (v.proj[:, 0:128] + bias_q).astype(BF16)
@@ -805,25 +970,13 @@
         for k, ref in enumerate((v.keys_all, v.values_all)):
             view = ref.at[own_rows]
             remote(view, view, v.s_kv.at[k, r], v.r_kv.at[k, r], at.sibling()).start()
-        if r == 1:
-            col_in.arrive(0)
-            col_in.send(1)
-            plane_weights(at, v.wback, v.wb, v.s_misc.at[2], v.r_misc.at[2])
-
-    whole = wo.at[:, lanes(at.b)]
-    wait_bytes(whole, v.r_o.at[0])
-    for r in (1, 2, 3):
-        remote(whole, whole, v.s_o.at[r], v.r_o.at[r], at.peer(r)).start()
-    remote(whole, whole, v.s_o.at[4], v.r_o.at[4], at.sibling()).start()
-    col_in.arrive(1)
-    col_in.send(2)
-    wait_bytes(v.wb.at[:, pl.ds(0, 128)], v.r_misc.at[2])
-    col_back.send(0)
 
     for r in range(4):
         for k, ref in enumerate((v.keys_all, v.values_all)):
             wait_bytes(ref.at[pl.ds(0, 256)], v.r_kv.at[k, r])
 
+    col_in.arrive(0)
+    col_in.send(1)
     scores = v.scores
 
     def attend(step, carry):
@@ -854,196 +1007,243 @@
                 (2 * chip + at.c, plane),
                 step == 3 if k == 3 else None,
             )
+
+        @pl.when(step == 0)
+        def _():
+            wo_spread.relay()
+
+        @pl.when(step == 2)
+        def _():
+            col_in.arrive(1)
+            col_in.send(2)
+
         return carry
 
     lax.fori_loop(0, 4, attend, 0)
 
+    wait_bytes(v.wb.at[:, pl.ds(0, 128)], v.r_misc.at[2])
+    col_back.send(0)
+    for r in (1, 2, 3):
+        wo_spread.rest(r)
+        part = wo_spread.block(r)
+        remote(part, part, v.s_o.at[r], v.r_o.at[r], at.sibling()).start()
+    for r in range(4):
+        wait_bytes(whole, v.r_o.at[r])
+    wait_bytes(v.att, v.r_misc.at[3])
+
+
+def ffn_phase(at, v, col_in, col_back, gathers, scatters, sum_back, sum_in):
+    n1, terms, peer_in = v.n1, v.terms, v.peer_in
+
+    def param(i):
+        return v.par[i : i + 1, :]
+
+    def local(h, i):
+        return pl.ds(64 * h + 32 * i, 32)
+
+    def chip_part(h, i):
+        return pl.ds(pl.multiple_of(h * 128 + at.c * 64 + 32 * i, 32), 32)
+
+    n1[...] = dot_nn(v.att[...], v.wo[...])
+    for h in range(2):
+        for i in range(2):
+            rows = local(h, i)
+            unit, scale = norm_rows(v.x[rows].astype(F32) + n1[rows] + param(2))
+            v.unit1[rows] = unit
+            v.scale1[rows] = jnp.broadcast_to(scale, (32, 128))
+            normed = unit * param(3) + param(4)
+            n1[rows] = normed
+            v.norm_slots[at.q, chip_part(h, i)] = normed.astype(BF16)
+        gathers[0][h].start()
+
+    for h in range(2):
+        gathers[0][h].relay()
     col_back.arrive(0)
     col_back.send(1)
-    for r in (1, 2, 3):
-        part = wo.at[:, lanes(2 * at.chip(r) + at.c)]
-        wait_bytes(part, v.r_o.at[r])
-        remote(part, part, v.s_o.at[4 + r], v.r_o.at[4 + r], at.sibling()).start()
-    for r in range(4):
-        wait_bytes(whole, v.r_o.at[4 + r])
-    wait_bytes(v.att, v.r_misc.at[3])
-
-
-def ffn_phase(at, v, col_in, col_back, exchanges):
-    n1, terms = v.n1, v.terms
-    sib_out, sib_in, peer_out, peer_in = v.sib_out, v.sib_in, v.peer_out, v.peer_in
-    gather, scatter, gather2, scatter2 = exchanges[:4]
-
-    def param(i):
-        return v.par[i : i + 1, :]
-
-    n1[...] = dot_nn(v.att[...], v.wo[...])
-
-    def first_norm(rows):
-        unit, scale = norm_rows(v.x[rows].astype(F32) + n1[rows] + param(2))
-        v.unit1[rows] = unit
-        v.scale1[rows] = jnp.broadcast_to(scale, (32, 128))
-        n1[rows] = unit * param(3) + param(4)
-
-    by_rows(128, 32, first_norm)
-    v.norm_slots[at.q, half(at.c)] = n1[...].astype(BF16)
-    gather.gather_start(v.norm_slots)
-
     col_in.arrive(2)
-    col_back.arrive(1)
-    col_back.send(2)
-    col_back.arrive(2)
-
-    for r in range(4):
-        chip = gather.gather_step(v.norm_slots, r)
-        v.pre[...] = dot_nn(v.norm_slots[chip], v.wi[...])
-
-        def activate(rows, r=r):
+
+    for n, (h, r) in enumerate(((0, 0), (1, 0), (0, 1), (0, 2), (0, 3), (1, 1), (1, 2), (1, 3))):
+        chip = gathers[0][h].step(r)
+        v.pre[...] = dot_nn(v.norm_slots[chip, pl.ds(128 * h, 128)], v.wi[...])
+
+        def activate(i, carry, r=r, h=h):
+            rows = pl.ds(pl.multiple_of(i * 32, 32), 32)
+            into = pl.ds(pl.multiple_of(128 * h + i * 32, 32), 32)
             u = v.pre[rows] + v.bins[...]
             cdf = 0.5 * (1.0 + lax.erf(u * math.sqrt(0.5)))
             bell = jnp.exp(-0.5 * u * u) * (1.0 / math.sqrt(2.0 * math.pi))
-            v.hid[r, rows] = (u * cdf).astype(BF16)
-            v.slope[r, rows] = cdf + u * bell
-
-        by_rows(256, 32, activate)
-        terms[r] = contract_cols(v.hid[r], v.wb[...])
-        scatter.scatter_put(terms, sib_out.at[0], sib_in.at[0], r)
-        if r:
-            scatter.scatter_pass(terms, sib_in.at[0], peer_out.at[0], peer_in.at[0], r - 1)
-    scatter.scatter_pass(terms, sib_in.at[0], peer_out.at[0], peer_in.at[0], 3)
-    scatter.scatter_arrive(peer_in.at[0])
-
-    base = pl.multiple_of(at.c * 128, 128)
-
-    def second_norm(rows):
-        own = pl.ds(pl.multiple_of(base + rows.start, 32), 32)
-        total = (
-            terms[0, own]
-            + peer_in[0, 1, rows].astype(F32)
-            + peer_in[0, 2, rows].astype(F32)
-            + peer_in[0, 3, rows].astype(F32)
+            v.hid[r, into] = (u * cdf).astype(BF16)
+            v.slope[r, into] = cdf + u * bell
+            return carry
+
+        lax.fori_loop(0, 4, activate, 0)
+        if n == 4:
+            col_back.arrive(1)
+            col_back.send(2)
+    col_back.arrive(2)
+
+    def to_plane(scatter, done, h, r, product):
+        terms[r, pl.ds(128 * h, 128)] = product
+        scatter[h].put(r, terms[r, part_rows(h, 1 - at.c)])
+        done.append((h, r))
+        if len(done) > 3:
+            pass_on(scatter, *done[-4])
+
+    def pass_on(scatter, h, r):
+        total = scatter[h].add(r, terms[r, part_rows(h, at.c)])
+        if r == 0:
+            terms[0, part_rows(h, at.c)] = total
+
+    done = []
+    for h in range(2):
+        for r in (3, 1, 2, 0):
+            product = contract_cols(v.hid[r, pl.ds(128 * h, 128)], v.wb[...])
+            to_plane(scatters[0], done, h, r, product)
+    for one in done[-3:]:
+        pass_on(scatters[0], *one)
+
+    def peers(side, rows):
+        return (
+            peer_in[side, 1, rows].astype(F32)
+            + peer_in[side, 2, rows].astype(F32)
+            + peer_in[side, 3, rows].astype(F32)
         )
-        unit, scale = norm_rows(n1[rows] + total + param(5))
-        v.out[rows] = (unit * param(6) + param(7)).astype(BF16)
-        g = v.cot[rows].astype(F32)
-        d = norm_back(g * param(6), unit, scale)
-        v.d2[rows] = d
-        low = d.astype(BF16)
-        v.grad_slots[at.q, own] = low
-        return g * unit, g, low.astype(F32)
-
-    second_norm.count = 3
-    sums = row_sums(128, 32, 1024, second_norm)
-    v.vec[6:7, :] = sums[0]
-    v.vec[7:8, :] = sums[1]
-    v.vec[5:6, :] = sums[2]
-
-    gather2.gather_start(v.grad_slots)
-    gbin = jnp.zeros((1, 512), F32)
-    for r in range(4):
-        chip = gather2.gather_step(v.grad_slots, r)
-        v.pre[...] = dot_nn(v.grad_slots[chip], v.wb[...])
-
-        def deactivate(rows, r=r):
-            low = (v.pre[rows] * v.slope[r, rows]).astype(BF16)
-            v.pre[rows] = low.astype(F32)
-            return (low.astype(F32),)
-
-        deactivate.count = 1
-        gbin = gbin + row_sums(256, 32, 512, deactivate)[0]
-        v.slope[r] = v.pre[...]
-        terms[r] = contract_cols(v.pre[...].astype(BF16), v.wi[...])
-        if r == 0:
-            scatter.scatter_end(sib_out.at[0], peer_out.at[0])
-        scatter2.scatter_put(terms, sib_out.at[1], sib_in.at[1], r)
-        if r:
-            scatter2.scatter_pass(terms, sib_in.at[1], peer_out.at[1], peer_in.at[1], r - 1)
-    scatter2.scatter_pass(terms, sib_in.at[1], peer_out.at[1], peer_in.at[1], 3)
-    v.gbin[...] = gbin
+
+    def column_sums(parts, sums):
+        return tuple(
+            kept + jnp.sum(part.reshape(4, 8, 1024), axis=0) for kept, part in zip(sums, parts)
+        )
+
+    gbin = [jnp.zeros((8, 512), F32)]
+    done = []
+
+    def hidden_grad(h, r):
+        chip = gathers[1][h].step(r)
+        v.pre[...] = dot_nn(v.grad_slots[chip, pl.ds(128 * h, 128)], v.wb[...])
+
+        def deactivate(i, carry):
+            rows = pl.ds(pl.multiple_of(i * 32, 32), 32)
+            into = pl.ds(pl.multiple_of(128 * h + i * 32, 32), 32)
+            low = (v.pre[rows] * v.slope[r, into]).astype(BF16)
+            v.low[r, into] = low
+            return carry + jnp.sum(low.astype(F32).reshape(4, 8, 512), axis=0)
+
+        gbin[0] = lax.fori_loop(0, 4, deactivate, gbin[0])
+        product = contract_cols(v.low[r, pl.ds(128 * h, 128)], v.wi[...])
+        to_plane(scatters[1], done, h, r, product)
+
+    sums = tuple(jnp.zeros((8, 1024), F32) for _ in range(3))
+    for h in range(2):
+        scatters[0][h].arrive()
+        for i in range(2):
+            rows = local(h, i)
+            total = terms[0, chip_part(h, i)] + peers(0, rows)
+            unit, scale = norm_rows(n1[rows] + total + param(5))
+            v.out[rows] = (unit * param(6) + param(7)).astype(BF16)
+            g = v.cot[rows].astype(F32)
+            d = norm_back(g * param(6), unit, scale)
+            v.d2[rows] = d
+            low = d.astype(BF16)
+            v.grad_slots[at.q, chip_part(h, i)] = low
+            sums = column_sums((g * unit, g, low.astype(F32)), sums)
+        gathers[1][h].start()
+        if h == 0:
+            hidden_grad(0, 0)
+            gathers[1][0].relay()
+    for row, total in zip((6, 7, 5), sums):
+        v.vec[row : row + 1, :] = jnp.sum(total, axis=0, keepdims=True)
+
+    hidden_grad(0, 1)
+    hidden_grad(0, 2)
+    gathers[1][1].relay()
+    for h, r in ((0, 3), (1, 0), (1, 1), (1, 2), (1, 3)):
+        hidden_grad(h, r)
+    for one in done[-3:]:
+        pass_on(scatters[1], *one)
+    v.gbin[...] = jnp.sum(gbin[0], axis=0, keepdims=True)
 
     def weight_grad(slots, right, into):
         def one(step, carry):
-            other = (at.b + step) % 8
-            total = jnp.zeros((128, 512), F32)
+            other = (at.q + step) % 4
+            total = jnp.zeros((256, 512), F32)
             for r in range(4):
-                total += contract_rows(slots[at.chip(r), :, lanes(other)], right(r))
-            into[other] = total.astype(BF16)
+                total += contract_rows(slots[at.chip(r), :, chip_rows(other)], right(r))
+            into[2 * other] = total[0:128].astype(BF16)
+            into[2 * other + 1] = total[128:256].astype(BF16)
             return carry
 
-        lax.fori_loop(0, 8, one, 0)
-
-    weight_grad(v.grad_slots, lambda r: v.hid[r], v.g_back)
-    column_grads(at, v.g_back, v.zg_back, v.s_zg.at[0], v.r_zg.at[0])
-    weight_grad(v.norm_slots, lambda r: v.slope[r].astype(BF16), v.g_in)
-
-    scatter2.scatter_arrive(peer_in.at[1])
-
-    def first_back(rows):
-        own = pl.ds(pl.multiple_of(base + rows.start, 32), 32)
-        total = (
-            v.d2[rows]
-            + terms[0, own]
-            + peer_in[1, 1, rows].astype(F32)
-            + peer_in[1, 2, rows].astype(F32)
-            + peer_in[1, 3, rows].astype(F32)
-        )
-        unit = v.unit1[rows]
-        d = norm_back(total * param(3), unit, v.scale1[rows][:, :1])
-        v.d1[rows] = d
-        low = d.astype(BF16)
-        v.db[rows] = low
-        return total * unit, total, low.astype(F32)
-
-    first_back.count = 3
-    sums = row_sums(128, 32, 1024, first_back)
-    v.vec[3:4, :] = sums[0]
-    v.vec[4:5, :] = sums[1]
-    v.vec[2:3, :] = sums[2]
+        lax.fori_loop(0, 4, one, 0)
+
+    sums = tuple(jnp.zeros((8, 1024), F32) for _ in range(3))
+    for h in range(2):
+        if h == 0:
+            weight_grad(v.grad_slots, lambda r: v.hid[r], v.g_back)
+            for gather in gathers[1]:
+                gather.end()
+            sum_back.begin((0,))
+        else:
+            weight_grad(v.norm_slots, lambda r: v.low[r], v.g_in)
+        scatters[1][h].arrive()
+        for i in range(2):
+            rows = local(h, i)
+            total = v.d2[rows] + terms[0, chip_part(h, i)] + peers(1, rows)
+            unit = v.unit1[rows]
+            d = norm_back(total * param(3), unit, v.scale1[rows][:, :1])
+            v.d1[rows] = d
+            low = d.astype(BF16)
+            v.db[rows] = low
+            sums = column_sums((total * unit, total, low.astype(F32)), sums)
+        rows = pl.ds(64 * h, 64)
+        v.da_send[rows] = contract_cols(v.db[rows], v.wo[...]).astype(BF16)
+        for r in range(4):
+            chip = at.chip(r)
+            for plane in (h, h + 2):
+                pair = 2 * (plane - h) + chip
+                send_or_copy(
+                    v.da_send.at[rows, lanes(pair)],
+                    v.da.at[slot_rows(at.place)],
+                    v.s_misc.at[4],
+                    v.r_da.at[r],
+                    (2 * chip + at.c, plane),
+                    None if r else at.z == plane,
+                )
+
+    for row, total in zip((3, 4, 2), sums):
+        v.vec[row : row + 1, :] = jnp.sum(total, axis=0, keepdims=True)
     v.vec[0:2, :] = jnp.zeros((2, 1024), F32)
-
-    v.da_send[...] = contract_cols(v.db[...], v.wo[...]).astype(BF16)
-
-    def give(step, carry):
-        for k in range(4):
-            chip = (at.q + 1 + step) % 4
-            plane = (at.z + 1 + k) % 4
-            pair = 4 * (plane // 2) + chip
-            send_or_copy(
-                v.da_send.at[slot_rows(plane % 2), lanes(pair)],
-                v.da.at[slot_rows(at.place)],
-                v.s_misc.at[4],
-                v.r_misc.at[4],
-                (2 * chip + at.c, plane),
-                step == 3 if k == 3 else None,
-            )
-        return carry
-
-    lax.fori_loop(0, 4, give, 0)
-
-
-def grads_phase(at, v, gather, out_scatter):
+    sum_back.begin((1, 2))
+    sum_in.begin((0, 1, 2))
+
+
+def grads_phase(at, v, gathers, scatters, out_scatter, sum_in, sum_back):
     xs, wqkv, terms = v.xs, v.wqkv, v.terms
     parity, pair = at.parity, at.pair
-    sib_out, sib_in = v.sib_out.at[0], v.sib_in.at[0]
-    peer_out, peer_in = v.peer_out.at[0], v.peer_in.at[0]
-
+
+    for h in range(2):
+        scatters[0][h].end()
     for r in range(4):
-        terms[r] = contract_rows(v.db[:, chip_rows(at.chip(r))], v.att[...])
-        out_scatter.scatter_put(terms, sib_out, sib_in, r)
-        if r:
-            out_scatter.scatter_pass(terms, sib_in, peer_out, peer_in, r - 1)
-    out_scatter.scatter_pass(terms, sib_in, peer_out, peer_in, 3)
+        for core in (1 - at.c, at.c):
+            part = contract_rows(v.db[:, lanes(2 * at.chip(r) + core)], v.att[...])
+            if core is at.c:
+                terms[r, 0:128] = part
+            else:
+                out_scatter.put(r, part)
 
     v.q_turned[...] = v.queries[...].astype(F32).T.astype(BF16)
     v.dk_turned[...] = jnp.zeros_like(v.dk_turned)
     v.dv_turned[...] = jnp.zeros_like(v.dv_turned)
-    wait_bytes(v.da, v.r_misc.at[4])
-    column_grads(at, v.g_in, v.zg_in, v.s_zg.at[1], v.r_zg.at[1])
-    v.da_turned[...] = v.da[...].astype(F32).T.astype(BF16)
+    wait_bytes(v.da.at[chip_rows(at.q)], v.r_da.at[0])
     s_buf, d_buf, p_buf = v.scores, v.d_buf, v.p_buf
 
     def attend(step, carry):
-        rows = chip_rows(step)
+        chip = ((at.y + step // 2) % 2) * 2 + (at.x + step % 2) % 2
+        rows = chip_rows(chip)
+
+        @pl.when(step > 0)
+        def _():
+            wait_bytes(v.da.at[rows], v.r_da.at[step])
+
+        v.da_turned[:, rows] = v.da[rows].astype(F32).T.astype(BF16)
         parts = []
         for h in range(2):
             mask = head_mask(h)
@@ -1061,6 +1261,22 @@
             v.dk_turned[band] += dot_nn(v.q_turned[band, rows], low)
             parts.append(dot_nn(low, v.keys_all[...]))
         v.dq[rows] = jnp.where(head_mask(0) > 0.5, parts[0], parts[1]) * HEAD_DIM**-0.5
+
+        @pl.when(step == 0)
+        def _():
+            for r in (3, 1, 2):
+                out_scatter.add(r, terms[r, 0:128])
+            terms[0, 0:128] = out_scatter.add(0, terms[0, 0:128])
+            sum_back.relay(1, 0)
+
+        @pl.when(step == 1)
+        def _():
+            sum_back.relay(1, 1)
+
+        @pl.when(step == 3)
+        def _():
+            sum_back.relay(2, 0)
+
         return carry
 
     lax.fori_loop(0, 4, attend, 0)
@@ -1084,45 +1300,93 @@
     dqkv[:, 256:384] = low
     v.vec[1:2, lanes(pair)] = jnp.sum(low.astype(F32), axis=0, keepdims=True)
 
-    gather.gather_end(v.norm_slots)
-    x_out, x_in = v.norm_slots, v.x_in
+    notes = v.notes
+    for b in range(8):
+        notes[b, 0:8] = v.vec[:, 128 * b : 128 * b + 128]
+        notes[b, 8:16] = jnp.zeros((8, 128), F32)
+    row = lax.broadcasted_iota(jnp.int32, (8, 128), 0)
+    for h in range(4):
+        notes[2 * h + at.b // 4, 8:16] = jnp.where(
+            row == at.b % 4, v.gbin[0:1, 128 * h : 128 * h + 128], 0.0
+        )
+    pltpu.make_async_copy(notes.at[at.b], v.notes_p.at[at.b], v.r_misc.at[5]).start()
+
+    def spread(step, carry):
+        to = (at.b + step) % 8
+        remote(
+            notes.at[to], v.notes_p.at[at.b], v.s_misc.at[5], v.r_misc.at[5], (to, at.z)
+        ).start()
+        return carry
+
+    lax.fori_loop(1, 8, spread, 0)
+
+    for gather in gathers:
+        gather.end()
+    x_out, x_in, x_via = v.norm_slots, v.grad_slots.at[0:2], v.grad_slots.at[2:4]
     for r in (3, 1, 2, 0):
         part = contract_cols(dqkv[chip_rows(at.chip(r))], wqkv[...])
         if r:
             x_out[r] = part.astype(BF16)
         else:
             v.x_sum[...] = part
-    for dz in (2, 1, 3, 0):
-        rows = slot_rows((at.z + dz) % 4)
-        for r in (3, 1, 2):
+    def piece(dz, k):
+        return pl.ds(pl.multiple_of(((at.z + dz) % 4) * 64 + 32 * k, 32), 32)
+
+    order = (2, 1, 3, 0)
+
+    def send_dx(dz, via):
+        for r, k in ((1, 0), (2, 1)):
+            rows = piece(dz, k)
+            remote(
+                x_out.at[3 if via else r, rows],
+                x_via.at[r - 1, rows] if via else x_in.at[r - 1, rows],
+                v.s_dx.at[dz, 0 if via else r, k],
+                v.r_dx.at[dz, 0 if via else r, k],
+                at.peer(r),
+            ).start()
+
+    for dz in order:
+        send_dx(dz, True)
+
+    def relay_dx(dz):
+        for r, k in ((2, 0), (1, 1)):
+            rows = piece(dz, k)
+            wait_bytes(x_via.at[k, rows], v.r_dx.at[dz, 0, k])
+            x_out[r, rows] = (
+                x_out[r, rows].astype(F32) + x_via[k, rows].astype(F32)
+            ).astype(BF16)
             remote(
                 x_out.at[r, rows],
-                x_in.at[r, rows],
-                v.s_dx.at[r, dz],
-                v.r_dx.at[r, dz],
+                x_in.at[r - 1, rows],
+                v.s_dx.at[dz, r, k],
+                v.r_dx.at[dz, r, k],
                 at.peer(r),
             ).start()
 
-    notes = v.notes
-    for d in range(32):
-        notes[d, 0:8] = v.vec[:, 128 * (d // 4) : 128 * (d // 4) + 128]
-        notes[d, 8:16] = jnp.zeros((8, 128), F32)
-    for h in range(4):
-        notes[8 * h + at.b, 8:9] = v.gbin[0:1, 128 * h : 128 * h + 128]
-    pltpu.make_async_copy(notes.at[at.flat], v.notes_in.at[at.flat], v.r_misc.at[5]).start()
-
-    def spread(step, carry):
-        to = (at.flat + step) % 32
+    out_scatter.arrive()
+    peer_in = v.peer_in.at[0]
+
+    def out_rows(rows):
+        total = (
+            terms[0, rows]
+            + peer_in[1, rows].astype(F32)
+            + peer_in[2, rows].astype(F32)
+            + peer_in[3, rows].astype(F32)
+        )
+        v.o_out[rows] = total.astype(BF16)
+
+    by_rows(128, 32, out_rows)
+    wide = pl.ds(pl.multiple_of(at.z * 256, 256), 256)
+    pltpu.make_async_copy(v.o_out.at[:, wide], v.o_in.at[0], v.r_misc.at[8]).start()
+    for dz in range(1, 4):
+        plane = (at.z + dz) % 4
         remote(
-            notes.at[to],
-            v.notes_in.at[at.flat],
-            v.s_misc.at[5],
-            v.r_misc.at[5],
-            (to // 4, to % 4),
+            v.o_out.at[:, pl.ds(pl.multiple_of(plane * 256, 256), 256)],
+            v.o_in.at[dz],
+            v.s_misc.at[8],
+            v.r_misc.at[8],
+            (at.b, plane),
         ).start()
-        return carry
-
-    lax.fori_loop(1, 32, spread, 0)
 
     def features(b):
         return contract_rows(xs[:, lanes(b)], dqkv[...])
@@ -1132,6 +1396,11 @@
         remote(
             v.w_sib_out.at[r], v.w_sib_in.at[r], v.s_ws.at[r], v.r_ws.at[r], at.sibling()
         ).start()
+    for dz in order:
+        send_dx(dz, False)
+        relay_dx(dz)
+    sum_in.relay(1, 0)
+    sum_back.finish(v.gs_back, v.fin_back, v.s_misc.at[7], v.r_misc.at[7])
     plane_w = 2 * (at.z // 2) + at.y
     for r in range(4):
         total = features(2 * at.chip(r) + at.c)
@@ -1146,46 +1415,27 @@
             plane_w == at.z if r == 0 else None,
         )
 
-    plane_grads(
-        at, v.g_back, v.zg_back, v.gs_back, v.fin_back, v.r_zg.at[0], v.s_misc.at[7], v.r_misc.at[7]
-    )
-    out_scatter.scatter_arrive(peer_in)
-
-    def out_rows(rows):
-        own = pl.ds(pl.multiple_of(at.c * 128 + rows.start, 32), 32)
-        total = (
-            terms[0, own]
-            + peer_in[1, rows].astype(F32)
-            + peer_in[2, rows].astype(F32)
-            + peer_in[3, rows].astype(F32)
-        )
-        v.o_out[rows] = total.astype(BF16)
-
-    by_rows(128, 32, out_rows)
-    wide = pl.ds(pl.multiple_of(at.z * 256, 256), 256)
-    pltpu.make_async_copy(v.o_out.at[:, wide], v.o_in.at[0], v.r_misc.at[8]).start()
+    sum_in.relay(1, 1)
+    wait_bytes(v.notes_p, v.r_misc.at[5])
+    total = v.notes_p[0]
+    for b in range(1, 8):
+        total += v.notes_p[b]
+    v.notes_sum[...] = total
+    mine = v.notes_in.at[at.z]
+    pltpu.make_async_copy(v.notes_sum, mine, v.r_misc.at[11]).start()
     for dz in range(1, 4):
-        plane = (at.z + dz) % 4
         remote(
-            v.o_out.at[:, pl.ds(pl.multiple_of(plane * 256, 256), 256)],
-            v.o_in.at[dz],
-            v.s_misc.at[8],
-            v.r_misc.at[8],
-            (at.b, plane),
+            v.notes_sum, mine, v.s_misc.at[11], v.r_misc.at[11], (at.b, (at.z + dz) % 4)
         ).start()
 
     z_out, z_in = v.z_out, v.z_in
-    for dz in (2, 1, 3, 0):
+    for dz in order:
         plane = (at.z + dz) % 4
         rows = slot_rows(plane)
-        for r in (3, 1, 2):
-            wait_bytes(x_in.at[r, rows], v.r_dx.at[r, dz])
-        total = (
-            v.x_sum[rows]
-            + x_in[1, rows].astype(F32)
-            + x_in[2, rows].astype(F32)
-            + x_in[3, rows].astype(F32)
-        )
+        for r in (1, 2):
+            for k in range(2):
+                wait_bytes(x_in.at[r - 1, piece(dz, k)], v.r_dx.at[dz, r, k])
+        total = v.x_sum[rows] + x_in[0, rows].astype(F32) + x_in[1, rows].astype(F32)
         if dz:
             z_out[dz] = total.astype(BF16)
             remote(
@@ -1193,9 +1443,9 @@
             ).start()
         else:
             v.x_own[...] = total
-    plane_grads(
-        at, v.g_in, v.zg_in, v.gs_in, v.fin_in, v.r_zg.at[1], v.s_misc.at[9], v.r_misc.at[9]
-    )
+        if dz == 1:
+            sum_in.relay(2, 0)
+    sum_in.finish(v.gs_in, v.fin_in, v.s_misc.at[9], v.r_misc.at[9])
     for dz in (1, 2, 3):
         wait_bytes(z_in.at[dz], v.r_dz.at[dz])
     same = slot_rows(parity)
@@ -1205,37 +1455,31 @@
 
     wait_bytes(v.o_in, v.r_misc.at[8])
     wait_bytes(v.w_in, v.r_misc.at[6])
-    wait_bytes(v.notes_in, v.r_misc.at[5])
+    wait_bytes(v.notes_in, v.r_misc.at[11])
     wait_bytes(v.fin_back, v.r_misc.at[7])
     wait_bytes(v.fin_in, v.r_misc.at[9])
 
 
-def end_phase(at, v, col_in, col_back, exchanges):
-    gather, scatter, gather2, scatter2, out_scatter = exchanges
+def end_phase(at, v, col_in, col_back, ends):
+    for one in ends:
+        one.end()
     slot = v.xs.at[slot_rows(0)]
     for dz in range(1, 4):
         wait_bytes(slot, v.s_z.at[dz])
-    for r in (1, 2, 3):
-        for dz in range(4):
-            wait_bytes(slot, v.s_p.at[r, dz])
-            wait_bytes(slot, v.s_dx.at[r, dz])
-    near = at.parity == at.y
-
-    @pl.when(jnp.logical_not(near))
-    def _():
-        wait_bytes(v.wqkv.at[pl.ds(0, 512)], v.s_w.at[0])
-
-    @pl.when(near)
-    def _():
-        wait_bytes(v.wqkv.at[pl.ds(0, 384)], v.s_w.at[0])
-
+    for dz in range(4):
+        for r in range(3):
+            for k in range(2):
+                wait_bytes(v.grad_slots.at[0, pl.ds(0, 32)], v.s_dx.at[dz, r, k])
+    wait_bytes(v.wqkv.at[pl.ds(0, 384)], v.s_w.at[0])
     wait_bytes(v.wqkv.at[pl.ds(0, 512)], v.s_w.at[1])
+    wait_bytes(v.w_near, v.s_w.at[2])
     seven = v.wi.at[pl.ds(0, 896), pl.ds(0, 128)]
     for i in (0, 2, 7, 9):
         wait_bytes(seven, v.s_misc.at[i])
-    wait_bytes(v.smalls.at[pl.ds(0, 31)], v.s_misc.at[1])
-    wait_bytes(v.wo.at[pl.ds(0, 768), pl.ds(0, 128)], v.s_o.at[0])
-    for r in range(1, 8):
+    wait_bytes(v.smalls.at[pl.ds(0, 3)], v.s_misc.at[1])
+    wait_bytes(v.smalls.at[pl.ds(0, 7)], v.s_misc.at[10])
+    wait_bytes(v.wo.at[pl.ds(0, 768), pl.ds(0, 128)], v.s_o.at[4])
+    for r in range(4):
         wait_bytes(v.wo.at[:, pl.ds(0, 128)], v.s_o.at[r])
     for r in range(4):
         for k in range(2):
@@ -1245,12 +1489,11 @@
     col_in.end()
     col_back.end()
     for dz in (1, 2, 3):
-        for k in range(2):
-            wait_bytes(v.zg_in.at[dz], v.s_zg.at[k, dz])
         wait_bytes(v.z_out.at[dz], v.s_dz.at[dz])
     for k in range(2):
         wait_bytes(v.sib_k, v.s_kv2.at[k])
-    wait_bytes(v.notes.at[pl.ds(0, 31)], v.s_misc.at[5])
+    wait_bytes(v.notes.at[pl.ds(0, 7)], v.s_misc.at[5])
+    wait_bytes(v.notes.at[pl.ds(0, 3)], v.s_misc.at[11])
     for r in range(4):
         wait_bytes(v.w_sib_out.at[r], v.s_ws.at[r])
     plane_w = 2 * (at.z // 2) + at.y
@@ -1264,9 +1507,6 @@
         wait_bytes(v.w_out, v.s_misc.at[6])
 
     wait_bytes(v.o_in.at[pl.ds(0, 3)], v.s_misc.at[8])
-    gather2.gather_end(v.grad_slots)
-    scatter2.scatter_end(v.sib_out.at[1], v.peer_out.at[1])
-    out_scatter.scatter_end(v.sib_out.at[0], v.peer_out.at[0])
 
 
 def finish_kernel(
@@ -1300,15 +1540,15 @@
     ).T
     gwin_ref[...] = fin_in[...].astype(F32)
     gwback_ref[...] = fin_back[...].astype(F32)
-    total = notes_in[0]
-    for d in range(1, 32):
-        total += notes_in[d]
+    total = notes_in[0] + notes_in[1] + notes_in[2] + notes_in[3]
     z = place_ref[0]
     part = jnp.zeros((8, 32), F32)
+    units = jnp.zeros((1, 128), F32)
     for k in range(4):
         part += jnp.where(z == k, total[0:8, 32 * k : 32 * k + 32], 0.0)
+        units += jnp.where(z == k, total[8 + k : 9 + k], 0.0)
     small_ref[...] = part
-    bin_ref[...] = total[8:9, :]
+    bin_ref[...] = units
 
 
 def vmem():
@@ -1316,14 +1556,15 @@
 
 
 def run_layer(*args):
-    scratch = [pltpu.VMEM(s, t) for _, s, t in SCRATCH]
-    for _, shape in SEMAPHORES:
+    results = [e for _, e in entries(Results)]
+    scratch = [pltpu.VMEM(s, t) for _, (s, t) in entries(Scratch)]
+    for _, shape in entries(Semaphores):
         scratch += [DMA(shape), DMA(shape)]
     return pl.pallas_call(
         layer_kernel,
-        out_shape=[jax.ShapeDtypeStruct(s, t) for _, s, t in RESULTS],
+        out_shape=[jax.ShapeDtypeStruct(s, t) for s, t in results],
         in_specs=[vmem()] * len(args),
-        out_specs=[vmem()] * len(RESULTS),
+        out_specs=[vmem()] * len(results),
         scratch_shapes=scratch,
         compiler_params=pltpu.CompilerParams(
             collective_id=1, has_side_effects=True, vmem_limit_bytes=VMEM_LIMIT
@@ -1349,7 +1590,7 @@
         out_shape=[jax.ShapeDtypeStruct(s, t) for s, t in shapes],
         in_specs=[pl.BlockSpec(memory_space=pltpu.SMEM)] + [vmem()] * (len(args) - 1),
         out_specs=[vmem()] * len(shapes),
-        compiler_params=pltpu.CompilerParams(vmem_limit_bytes=32 * 2**20),
+        compiler_params=pltpu.CompilerParams(vmem_limit_bytes=VMEM_LIMIT),
     )(*args)
 
 
@@ -1387,7 +1628,10 @@
         jnp.tile(vectors, (1, 4)),
         jnp.zeros((), BF16),
     )
-    small = jnp.concatenate((spread, b_in[None], jnp.zeros((7, 128), BF16)), axis=0)
+    units = jnp.where(
+        lax.broadcasted_iota(jnp.int32, (8, 1), 0) == head_id, b_in[None], jnp.zeros((), BF16)
+    )
+    small = jnp.concatenate((spread, units), axis=0)
     results = run_layer(
         x, w_query, w_key, w_value, w_out, small, w_in, w_back, cotangent.reshape(-1, model_dim)
     )

time: 218 us -> 184 us (0.84)
  Pallas kernels: 208 us -> 180 us
  local copies, waits for them, and re-layouts: 8.7 us -> 2.58 us
    pallas_call x1, Pallas kernels: 206 us -> 177 us  [run_layer(): pl.pallas_call(layer_kernel, out_shape=[jax.ShapeDtypeStruct(s, t) for s,...]
    unnamed x32 -> x20, local copies, waits for them, and re-layouts: 7.94 us -> 1.91 us
where the time goes in v4:
time: 184 us
  Pallas kernels  180 us (98%)
  local copies, waits for them, and re-layouts  2.58 us (1%)
    pallas_call x1, Pallas kernels, run_layer(): pl.pallas_call(layer_kernel, out_shape=[jax.ShapeDtypeStruct(s, t) for s,...  177 us

profile of v4, /device:TPU:0, one launch (start us, length us, event | category | flops | bytes accessed | tf_op | source)
XLA Modules:
  0.0 184.0 jit_solution(2111260202954784989)
XLA Ops:
  0.7 0.0 copy-start.8
  0.7 0.0 copy-start.4
  0.7 0.0 copy-start.5
  0.7 0.0 copy-start.6
  0.7 0.0 copy-start.7
  0.7 0.0 copy-start.1
  0.7 0.0 copy-start.2
  0.7 0.0 copy-start.3
  0.8 0.5 copy-done.8
  1.3 0.0 copy-done.4
  1.3 0.0 copy-done.5
  1.3 0.0 copy-done.6
  1.4 0.0 copy-done.7
  1.4 0.0 copy-done.1
  1.4 0.0 copy-done.2
  1.4 0.0 copy-done.3
  1.5 0.0 copy-start.9
  1.5 0.1 tile.10
  1.6 0.6 copy-done.9
  2.1 0.1 broadcast_select_fusion
  2.2 0.6 pad_maximum_fusion.refs_5_
  2.8 177.2 %shard_map.296 = (bf16[128,1024]{1,0:T(8,128)(2,1)}, bf16[128,1024]{1,0:T(8,128)(2,1)}, bf16[2,2,128,384]{3,2,1,0:T(8,128)(2,1)}, bf16[4,128,256]{2,1,0:T(8,128)...) custom-call(bf16[128,1024]{1,0:T(8,128)(2,1)} %bitcast.30, ...), custom_call_target="tpu_custom_call" | custom-call | tf_op jit(solution)/shard_map/pallas_call | solution.py:1563
  180.0 2.8 %shard_map.297 = (bf16[128,1024]{1,0:T(8,128)(2,1)}, bf16[128,1024]{1,0:T(8,128)(2,1)}, f32[128,256]{1,0:T(8,128)}, f32[128,256]{1,0:T(8,128)}, f32[128,256]{1,0...) custom-call(s32[1]{0:T(128)} %bitcast.place_ref, ...), custom_call_target="tpu_custom_call" | custom-call | tf_op jit(solution)/shard_map/pallas_call | solution.py:1588
  182.8 0.0 copy-start
  182.8 0.7 copy-done
  183.5 0.5 slice_bitcast_fusion
  (4 shorter events, 0.1 us)
Async XLA Ops:
  0.7 0.7 copy-start.8
  0.7 0.7 copy-start.4
  0.7 0.7 copy-start.5
  0.7 0.7 copy-start.6
  0.7 0.7 copy-start.7
  0.7 0.7 copy-start.1
  0.7 0.7 copy-start.2
  0.7 0.7 copy-start.3
  1.5 0.7 copy-start.9
  182.8 0.7 copy-start

commit v5 on v4

--- a/solution.py
+++ b/solution.py
@@ -376,34 +376,28 @@
         for i in (0, 1):
             for r, k in ((1, i), (2, 1 - i)):
                 piece = self.part(mine, k)
-                remote(piece, piece, self.send.at[r, k], self.recv.at[r, k], self.at.peer(r)).start()
+                remote(piece, piece, self.send, self.recv.at[r, k], self.at.peer(r)).start()
 
     def relay(self):
         for r, k in ((1, 0), (2, 1)):
             piece = self.part(self.block(r), k)
             wait_bytes(piece, self.recv.at[r, k])
-            remote(piece, piece, self.send.at[0, k], self.recv.at[0, k], self.at.peer(3 - r)).start()
+            remote(piece, piece, self.send, self.recv.at[0, k], self.at.peer(3 - r)).start()
 
     def rest(self, r):
         block = self.block(r)
         for row, k in {1: ((1, 1),), 2: ((2, 0),), 3: ((0, 0), (0, 1))}[r]:
             wait_bytes(self.part(block, k), self.recv.at[row, k])
 
-    def end(self):
-        mine = self.block(0)
-        for row in range(3):
-            for k in range(2):
-                wait_bytes(self.part(mine, k), self.send.at[row, k])
-
 
 def part_rows(h, core):
     return pl.ds(pl.multiple_of(h * 128 + core * 64, 64), 64)
 
 
 class Gather:
-    def __init__(self, at, slots, h, send, recv, send_sib, recv_sib):
+    def __init__(self, at, slots, h, send, recv, recv_sib):
         self.at, self.slots, self.h = at, slots, h
-        self.send_sib, self.recv_sib = send_sib, recv_sib
+        self.send, self.recv_sib = send, recv_sib
 
         def part(block, k):
             return block.at[pl.ds(k * 32, 32)]
@@ -414,9 +408,7 @@
 
     def to_sibling(self, r):
         block = self.spread.block(r)
-        remote(
-            block, block, self.send_sib.at[r], self.recv_sib.at[r], self.at.sibling()
-        ).start()
+        remote(block, block, self.send, self.recv_sib.at[r], self.at.sibling()).start()
 
     def start(self):
         self.spread.start()
@@ -425,24 +417,19 @@
     def relay(self):
         self.spread.relay()
 
-    def step(self, r):
+    def forward(self, r):
+        self.spread.rest(r)
+        self.to_sibling(r)
+
+    def ready(self, r):
         at = self.at
-        if r:
-            self.spread.rest(r)
-            self.to_sibling(r)
         wait_bytes(self.slots.at[at.chip(r), part_rows(self.h, 1 - at.c)], self.recv_sib.at[r])
         return at.chip(r)
 
-    def end(self):
-        self.spread.end()
-        for r in range(4):
-            wait_bytes(self.spread.block(r), self.send_sib.at[r])
-
 
 class Exchange:
-    def __init__(self, at, buffers, rows, send, recv, send_sib, recv_sib):
-        self.at, self.send, self.recv = at, send, recv
-        self.send_sib, self.recv_sib = send_sib, recv_sib
+    def __init__(self, at, buffers, rows, send, recv, recv_sib):
+        self.at, self.send, self.recv, self.recv_sib = at, send, recv, recv_sib
         self.sib_out, self.sib_in, self.out, self.into = buffers
         self.rows = rows
 
@@ -452,7 +439,7 @@
         remote(
             mine,
             self.sib_in.at[r, self.rows],
-            self.send_sib.at[r],
+            self.send,
             self.recv_sib.at[r],
             self.at.sibling(),
         ).start()
@@ -465,18 +452,12 @@
         held = self.out.at[r, self.rows]
         held[...] = total.astype(BF16)
         remote(
-            held, self.into.at[r, self.rows], self.send.at[r], self.recv.at[r], self.at.peer(r)
+            held, self.into.at[r, self.rows], self.send, self.recv.at[r], self.at.peer(r)
         ).start()
 
     def arrive(self):
         for r in (1, 2, 3):
             wait_bytes(self.into.at[r, self.rows], self.recv.at[r])
-
-    def end(self):
-        for r in range(4):
-            wait_bytes(self.sib_out.at[r, self.rows], self.send_sib.at[r])
-            if r:
-                wait_bytes(self.out.at[r, self.rows], self.send.at[r])
 
 
 def norm_rows(values):
@@ -673,7 +654,7 @@
 
 
 class Inputs:
-    x = wq = wk = wv = wout = small = win = wback = cot = None
+    small = x_hbm = cot_hbm = wq = wk = wv = wout = win = wback = None
 
 
 def entries(table):
@@ -691,6 +672,10 @@
 
 
 class Scratch:
+    out_here = ((128, 1024), BF16)
+    gtok_here = ((128, 1024), BF16)
+    x = ((128, 1024), BF16)
+    cot = ((128, 1024), BF16)
     xs = ((1024, 1024), BF16)
     wqkv = ((1024, 384), BF16)
     w_near = ((3, 128, 256), BF16)
@@ -763,13 +748,13 @@
     notes_sum = ((16, 128), F32)
 
 
-class Semaphores:
+class Arrivals:
     z = (4,)
     p = (4, 3, 2)
     wo = (3, 2)
     w = (3,)
     o = (5,)
-    kv = (2, 4)
+    kv = (1,)
     misc = (12,)
     col = (4, 3)
     ga = (4, 3, 2)
@@ -779,9 +764,28 @@
     zg = (2, 2, 3)
     kv2 = (2,)
     dx = (4, 3, 2)
-    da = (4,)
     dz = (4,)
     ws = (4,)
+    da = (4,)
+    own = (4,)
+
+
+class Departures:
+    z = (1,)
+    p = (1,)
+    wo = (1,)
+    w = (3,)
+    o = (1,)
+    kv = (1,)
+    misc = (12,)
+    col = (4, 3)
+    ga = (2,)
+    ex = (3,)
+    zg = (2, 2, 3)
+    kv2 = (1,)
+    dx = (1,)
+    dz = (1,)
+    ws = (1,)
 
 
 class Refs:
@@ -791,8 +795,7 @@
 def layer_kernel(*refs):
     v = Refs()
     names = [n for table in (Inputs, Results, Scratch) for n, _ in entries(table)]
-    for n, _ in entries(Semaphores):
-        names += ["s_" + n, "r_" + n]
+    names += ["r_" + n for n, _ in entries(Arrivals)] + ["s_" + n for n, _ in entries(Departures)]
     for name, ref in zip(names, refs):
         setattr(v, name, ref)
     at = Place()
@@ -804,7 +807,7 @@
     col_back = Column(at, v.wb, [s.at[2] for s in (v.s_col, v.r_col)] + [s.at[3] for s in (v.s_col, v.r_col)])
     gathers = [
         [
-            Gather(at, slots, h, *[t.at[2 * i + h] for t in (v.s_ga, v.r_ga, v.s_ga_sib, v.r_ga_sib)])
+            Gather(at, slots, h, v.s_ga.at[i], v.r_ga.at[2 * i + h], v.r_ga_sib.at[2 * i + h])
             for h in range(2)
         ]
         for i, slots in enumerate((v.norm_slots, v.grad_slots))
@@ -812,8 +815,7 @@
 
     def exchange(i, side, rows):
         buffers = [t.at[side] for t in (v.sib_out, v.sib_in, v.peer_out, v.peer_in)]
-        sems = [t.at[i] for t in (v.s_ex, v.r_ex, v.s_ex_sib, v.r_ex_sib)]
-        return Exchange(at, buffers, rows, *sems)
+        return Exchange(at, buffers, rows, v.s_ex.at[i // 2], v.r_ex.at[i], v.r_ex_sib.at[i])
 
     scatters = [
         [exchange(2 * i + h, i, pl.ds(64 * h, 64)) for h in range(2)] for i in range(2)
@@ -826,7 +828,7 @@
             at,
             lambda r, plane=plane: v.xs.at[slot_rows(at.chip(r) * 4 + plane)],
             lambda block, k: block.at[pl.ds(k * 32, 32)],
-            v.s_p.at[i],
+            v.s_p.at[0],
             v.r_p.at[i],
         )
         for i, plane in enumerate(at.planes)
@@ -835,17 +837,19 @@
         at,
         lambda r: v.wo.at[:, lanes(2 * at.chip(r) + at.c)],
         lambda block, k: block.at[pl.ds(k * 512, 512)],
-        v.s_wo,
+        v.s_wo.at[0],
         v.r_wo,
     )
     sum_in = ColumnSum(at, v.g_in, v.pass_in, v.s_zg.at[0], v.r_zg.at[0])
     sum_back = ColumnSum(at, v.g_back, v.pass_back, v.s_zg.at[1], v.r_zg.at[1])
+    pltpu.make_async_copy(v.x_hbm, v.x, v.r_own.at[0]).start()
+    pltpu.make_async_copy(v.cot_hbm, v.cot, v.r_own.at[1]).start()
     greet_all(at)
+    wait_bytes(v.x, v.r_own.at[0])
     attend_phase(at, v, col_in, col_back, rows_spread, wo_spread)
     ffn_phase(at, v, col_in, col_back, gathers, scatters, sum_back, sum_in)
-    grads_phase(at, v, gathers[0], scatters, out_scatter, sum_in, sum_back)
-    ends = rows_spread + [wo_spread, sum_in, sum_back] + scatters[1] + [out_scatter]
-    end_phase(at, v, col_in, col_back, ends)
+    grads_phase(at, v, out_scatter, sum_in, sum_back)
+    end_phase(at, v, (sum_in, sum_back, col_in, col_back))
 
 
 def attend_phase(at, v, col_in, col_back, rows_spread, wo_spread):
@@ -871,7 +875,7 @@
         remote(
             v.x.at[slot_rows(plane % 2)],
             xs.at[slot_rows(at.place)],
-            v.s_z.at[i],
+            v.s_z.at[0],
             v.r_z.at[at.z],
             (at.b, plane),
         ).start()
@@ -884,7 +888,7 @@
     part = wo.at[pl.ds(pl.multiple_of(at.z * 256, 256), 256), lanes(at.b)]
     pltpu.make_async_copy(v.wout, part, v.r_o.at[4]).start()
     for i in (1, 2, 3):
-        remote(v.wout, part, v.s_o.at[4], v.r_o.at[4], (at.b, at.planes[i])).start()
+        remote(v.wout, part, v.s_o.at[0], v.r_o.at[4], (at.b, at.planes[i])).start()
 
     def to_pairs(sources, group):
         for dx in range(2):
@@ -969,11 +973,9 @@
         v.values_all[own_rows] = (v.proj[:, 256:384] + bias_v).astype(BF16)
         for k, ref in enumerate((v.keys_all, v.values_all)):
             view = ref.at[own_rows]
-            remote(view, view, v.s_kv.at[k, r], v.r_kv.at[k, r], at.sibling()).start()
-
-    for r in range(4):
-        for k, ref in enumerate((v.keys_all, v.values_all)):
-            wait_bytes(ref.at[pl.ds(0, 256)], v.r_kv.at[k, r])
+            remote(view, view, v.s_kv.at[0], v.r_kv.at[0], at.sibling()).start()
+
+    wait_bytes(v.keys_all, v.r_kv.at[0])
 
     col_in.arrive(0)
     col_in.send(1)
@@ -1026,7 +1028,7 @@
     for r in (1, 2, 3):
         wo_spread.rest(r)
         part = wo_spread.block(r)
-        remote(part, part, v.s_o.at[r], v.r_o.at[r], at.sibling()).start()
+        remote(part, part, v.s_o.at[0], v.r_o.at[r], at.sibling()).start()
     for r in range(4):
         wait_bytes(whole, v.r_o.at[r])
     wait_bytes(v.att, v.r_misc.at[3])
@@ -1044,6 +1046,7 @@
     def chip_part(h, i):
         return pl.ds(pl.multiple_of(h * 128 + at.c * 64 + 32 * i, 32), 32)
 
+    wait_bytes(v.cot, v.r_own.at[1])
     n1[...] = dot_nn(v.att[...], v.wo[...])
     for h in range(2):
         for i in range(2):
@@ -1056,17 +1059,11 @@
             v.norm_slots[at.q, chip_part(h, i)] = normed.astype(BF16)
         gathers[0][h].start()
 
-    for h in range(2):
-        gathers[0][h].relay()
-    col_back.arrive(0)
-    col_back.send(1)
-    col_in.arrive(2)
-
-    for n, (h, r) in enumerate(((0, 0), (1, 0), (0, 1), (0, 2), (0, 3), (1, 1), (1, 2), (1, 3))):
-        chip = gathers[0][h].step(r)
+    def hidden(h, r):
+        chip = gathers[0][h].ready(r)
         v.pre[...] = dot_nn(v.norm_slots[chip, pl.ds(128 * h, 128)], v.wi[...])
 
-        def activate(i, carry, r=r, h=h):
+        def activate(i, carry):
             rows = pl.ds(pl.multiple_of(i * 32, 32), 32)
             into = pl.ds(pl.multiple_of(128 * h + i * 32, 32), 32)
             u = v.pre[rows] + v.bins[...]
@@ -1077,9 +1074,31 @@
             return carry
 
         lax.fori_loop(0, 4, activate, 0)
-        if n == 4:
-            col_back.arrive(1)
-            col_back.send(2)
+
+    def neighbours(gather):
+        gather.relay()
+        gather.forward(1)
+        gather.forward(2)
+
+    neighbours(gathers[0][0])
+    gathers[0][1].relay()
+    col_back.arrive(0)
+    col_back.send(1)
+    col_in.arrive(2)
+    hidden(0, 0)
+    gathers[0][1].forward(1)
+    gathers[0][1].forward(2)
+    hidden(1, 0)
+    hidden(0, 1)
+    hidden(0, 2)
+    gathers[0][0].forward(3)
+    hidden(1, 1)
+    gathers[0][1].forward(3)
+    col_back.arrive(1)
+    col_back.send(2)
+    hidden(1, 2)
+    hidden(0, 3)
+    hidden(1, 3)
     col_back.arrive(2)
 
     def to_plane(scatter, done, h, r, product):
@@ -1118,7 +1137,7 @@
     done = []
 
     def hidden_grad(h, r):
-        chip = gathers[1][h].step(r)
+        chip = gathers[1][h].ready(r)
         v.pre[...] = dot_nn(v.grad_slots[chip, pl.ds(128 * h, 128)], v.wb[...])
 
         def deactivate(i, carry):
@@ -1139,7 +1158,7 @@
             rows = local(h, i)
             total = terms[0, chip_part(h, i)] + peers(0, rows)
             unit, scale = norm_rows(n1[rows] + total + param(5))
-            v.out[rows] = (unit * param(6) + param(7)).astype(BF16)
+            v.out_here[rows] = (unit * param(6) + param(7)).astype(BF16)
             g = v.cot[rows].astype(F32)
             d = norm_back(g * param(6), unit, scale)
             v.d2[rows] = d
@@ -1149,40 +1168,45 @@
         gathers[1][h].start()
         if h == 0:
             hidden_grad(0, 0)
-            gathers[1][0].relay()
+    pltpu.make_async_copy(v.out_here, v.out, v.r_own.at[2]).start()
     for row, total in zip((6, 7, 5), sums):
         v.vec[row : row + 1, :] = jnp.sum(total, axis=0, keepdims=True)
-
-    hidden_grad(0, 1)
-    hidden_grad(0, 2)
-    gathers[1][1].relay()
-    for h, r in ((0, 3), (1, 0), (1, 1), (1, 2), (1, 3)):
-        hidden_grad(h, r)
-    for one in done[-3:]:
-        pass_on(scatters[1], *one)
-    v.gbin[...] = jnp.sum(gbin[0], axis=0, keepdims=True)
 
     def weight_grad(slots, right, into):
         def one(step, carry):
             other = (at.q + step) % 4
             total = jnp.zeros((256, 512), F32)
             for r in range(4):
-                total += contract_rows(slots[at.chip(r), :, chip_rows(other)], right(r))
+                total += contract_rows(slots[at.chip(r), :, chip_rows(other)], right[r])
             into[2 * other] = total[0:128].astype(BF16)
             into[2 * other + 1] = total[128:256].astype(BF16)
             return carry
 
         lax.fori_loop(0, 4, one, 0)
 
+    neighbours(gathers[1][0])
+    hidden_grad(1, 0)
+    hidden_grad(0, 1)
+    neighbours(gathers[1][1])
+    hidden_grad(0, 2)
+    gathers[1][0].forward(3)
+    hidden_grad(1, 1)
+    hidden_grad(0, 3)
+    gathers[1][1].forward(3)
+    hidden_grad(1, 2)
+    hidden_grad(1, 3)
+    for one in done[-3:]:
+        pass_on(scatters[1], *one)
+    v.gbin[...] = jnp.sum(gbin[0], axis=0, keepdims=True)
+
     sums = tuple(jnp.zeros((8, 1024), F32) for _ in range(3))
     for h in range(2):
         if h == 0:
-            weight_grad(v.grad_slots, lambda r: v.hid[r], v.g_back)
-            for gather in gathers[1]:
-                gather.end()
+            weight_grad(v.grad_slots, v.hid, v.g_back)
+            wait_bytes(v.xs.at[pl.ds(0, 896)], v.s_ga.at[1])
             sum_back.begin((0,))
         else:
-            weight_grad(v.norm_slots, lambda r: v.low[r], v.g_in)
+            weight_grad(v.norm_slots, v.low, v.g_in)
         scatters[1][h].arrive()
         for i in range(2):
             rows = local(h, i)
@@ -1211,17 +1235,18 @@
     for row, total in zip((3, 4, 2), sums):
         v.vec[row : row + 1, :] = jnp.sum(total, axis=0, keepdims=True)
     v.vec[0:2, :] = jnp.zeros((2, 1024), F32)
-    sum_back.begin((1, 2))
-    sum_in.begin((0, 1, 2))
-
-
-def grads_phase(at, v, gathers, scatters, out_scatter, sum_in, sum_back):
+    for i in range(3):
+        if i:
+            sum_back.begin((i,))
+        sum_in.begin((i,))
+
+
+def grads_phase(at, v, out_scatter, sum_in, sum_back):
     xs, wqkv, terms = v.xs, v.wqkv, v.terms
     parity, pair = at.parity, at.pair
 
-    for h in range(2):
-        scatters[0][h].end()
-    for r in range(4):
+    wait_bytes(xs.at[pl.ds(0, 896)], v.s_ex.at[0])
+    for r in (3, 1, 2, 0):
         for core in (1 - at.c, at.c):
             part = contract_rows(v.db[:, lanes(2 * at.chip(r) + core)], v.att[...])
             if core is at.c:
@@ -1232,6 +1257,9 @@
     v.q_turned[...] = v.queries[...].astype(F32).T.astype(BF16)
     v.dk_turned[...] = jnp.zeros_like(v.dk_turned)
     v.dv_turned[...] = jnp.zeros_like(v.dv_turned)
+    for r in (3, 1, 2):
+        out_scatter.add(r, terms[r, 0:128])
+    terms[0, 0:128] = out_scatter.add(0, terms[0, 0:128])
     wait_bytes(v.da.at[chip_rows(at.q)], v.r_da.at[0])
     s_buf, d_buf, p_buf = v.scores, v.d_buf, v.p_buf
 
@@ -1262,20 +1290,13 @@
             parts.append(dot_nn(low, v.keys_all[...]))
         v.dq[rows] = jnp.where(head_mask(0) > 0.5, parts[0], parts[1]) * HEAD_DIM**-0.5
 
-        @pl.when(step == 0)
-        def _():
-            for r in (3, 1, 2):
-                out_scatter.add(r, terms[r, 0:128])
-            terms[0, 0:128] = out_scatter.add(0, terms[0, 0:128])
-            sum_back.relay(1, 0)
-
         @pl.when(step == 1)
         def _():
-            sum_back.relay(1, 1)
-
-        @pl.when(step == 3)
+            sum_back.relay(1, 0)
+
+        @pl.when(step == 2)
         def _():
-            sum_back.relay(2, 0)
+            sum_in.relay(1, 0)
 
         return carry
 
@@ -1286,83 +1307,11 @@
     v.out_k[...] = v.dk_turned[:, other].T * HEAD_DIM**-0.5
     v.out_v[...] = v.dv_turned[:, other].T
     for k, (ref, into) in enumerate(((v.out_k, v.sib_k), (v.out_v, v.sib_v))):
-        remote(ref, into, v.s_kv2.at[k], v.r_kv2.at[k], at.sibling()).start()
+        remote(ref, into, v.s_kv2.at[0], v.r_kv2.at[k], at.sibling()).start()
     dqkv = v.dqkv
     low = v.dq[...].astype(BF16)
     dqkv[:, 0:128] = low
     v.vec[0:1, lanes(pair)] = jnp.sum(low.astype(F32), axis=0, keepdims=True)
-    own_k = v.dk_turned[:, mine].T * HEAD_DIM**-0.5
-    wait_bytes(v.sib_k, v.r_kv2.at[0])
-    dqkv[:, 128:256] = (own_k + v.sib_k[...]).astype(BF16)
-    own_v = v.dv_turned[:, mine].T
-    wait_bytes(v.sib_v, v.r_kv2.at[1])
-    low = (own_v + v.sib_v[...]).astype(BF16)
-    dqkv[:, 256:384] = low
-    v.vec[1:2, lanes(pair)] = jnp.sum(low.astype(F32), axis=0, keepdims=True)
-
-    notes = v.notes
-    for b in range(8):
-        notes[b, 0:8] = v.vec[:, 128 * b : 128 * b + 128]
-        notes[b, 8:16] = jnp.zeros((8, 128), F32)
-    row = lax.broadcasted_iota(jnp.int32, (8, 128), 0)
-    for h in range(4):
-        notes[2 * h + at.b // 4, 8:16] = jnp.where(
-            row == at.b % 4, v.gbin[0:1, 128 * h : 128 * h + 128], 0.0
-        )
-    pltpu.make_async_copy(notes.at[at.b], v.notes_p.at[at.b], v.r_misc.at[5]).start()
-
-    def spread(step, carry):
-        to = (at.b + step) % 8
-        remote(
-            notes.at[to], v.notes_p.at[at.b], v.s_misc.at[5], v.r_misc.at[5], (to, at.z)
-        ).start()
-        return carry
-
-    lax.fori_loop(1, 8, spread, 0)
-
-    for gather in gathers:
-        gather.end()
-    x_out, x_in, x_via = v.norm_slots, v.grad_slots.at[0:2], v.grad_slots.at[2:4]
-    for r in (3, 1, 2, 0):
-        part = contract_cols(dqkv[chip_rows(at.chip(r))], wqkv[...])
-        if r:
-            x_out[r] = part.astype(BF16)
-        else:
-            v.x_sum[...] = part
-    def piece(dz, k):
-        return pl.ds(pl.multiple_of(((at.z + dz) % 4) * 64 + 32 * k, 32), 32)
-
-    order = (2, 1, 3, 0)
-
-    def send_dx(dz, via):
-        for r, k in ((1, 0), (2, 1)):
-            rows = piece(dz, k)
-            remote(
-                x_out.at[3 if via else r, rows],
-                x_via.at[r - 1, rows] if via else x_in.at[r - 1, rows],
-                v.s_dx.at[dz, 0 if via else r, k],
-                v.r_dx.at[dz, 0 if via else r, k],
-                at.peer(r),
-            ).start()
-
-    for dz in order:
-        send_dx(dz, True)
-
-    def relay_dx(dz):
-        for r, k in ((2, 0), (1, 1)):
-            rows = piece(dz, k)
-            wait_bytes(x_via.at[k, rows], v.r_dx.at[dz, 0, k])
-            x_out[r, rows] = (
-                x_out[r, rows].astype(F32) + x_via[k, rows].astype(F32)
-            ).astype(BF16)
-            remote(
-                x_out.at[r, rows],
-                x_in.at[r - 1, rows],
-                v.s_dx.at[dz, r, k],
-                v.r_dx.at[dz, r, k],
-                at.peer(r),
-            ).start()
-
     out_scatter.arrive()
     peer_in = v.peer_in.at[0]
 
@@ -1388,19 +1337,116 @@
             (at.b, plane),
         ).start()
 
+    sum_back.relay(1, 1)
+    sum_back.relay(2, 0)
+    own_k = v.dk_turned[:, mine].T * HEAD_DIM**-0.5
+    wait_bytes(v.sib_k, v.r_kv2.at[0])
+    dqkv[:, 128:256] = (own_k + v.sib_k[...]).astype(BF16)
+    own_v = v.dv_turned[:, mine].T
+    wait_bytes(v.sib_v, v.r_kv2.at[1])
+    low = (own_v + v.sib_v[...]).astype(BF16)
+    dqkv[:, 256:384] = low
+    v.vec[1:2, lanes(pair)] = jnp.sum(low.astype(F32), axis=0, keepdims=True)
+
+    notes = v.notes
+    for b in range(8):
+        notes[b, 0:8] = v.vec[:, 128 * b : 128 * b + 128]
+        notes[b, 8:16] = jnp.zeros((8, 128), F32)
+    row = lax.broadcasted_iota(jnp.int32, (8, 128), 0)
+    for h in range(4):
+        notes[2 * h + at.b // 4, 8:16] = jnp.where(
+            row == at.b % 4, v.gbin[0:1, 128 * h : 128 * h + 128], 0.0
+        )
+    pltpu.make_async_copy(notes.at[at.b], v.notes_p.at[at.b], v.r_misc.at[5]).start()
+
+    def spread(step, carry):
+        to = (at.b + step) % 8
+        remote(
+            notes.at[to], v.notes_p.at[at.b], v.s_misc.at[5], v.r_misc.at[5], (to, at.z)
+        ).start()
+        return carry
+
+    lax.fori_loop(1, 8, spread, 0)
+
+    wait_bytes(xs.at[pl.ds(0, 896)], v.s_ga.at[0])
+    x_out, x_in, x_via = v.norm_slots, v.grad_slots.at[0:2], v.grad_slots.at[2:4]
+    for r in (3, 1, 2, 0):
+        part = contract_cols(dqkv[chip_rows(at.chip(r))], wqkv[...])
+        if r:
+            x_out[r] = part.astype(BF16)
+        else:
+            v.x_sum[...] = part
+    def piece(dz, k):
+        return pl.ds(pl.multiple_of(((at.z + dz) % 4) * 64 + 32 * k, 32), 32)
+
+    order = (2, 1, 3, 0)
+
+    def send_dx(dz, via):
+        for r, k in ((1, 0), (2, 1)):
+            rows = piece(dz, k)
+            remote(
+                x_out.at[3 if via else r, rows],
+                x_via.at[r - 1, rows] if via else x_in.at[r - 1, rows],
+                v.s_dx.at[0],
+                v.r_dx.at[dz, 0 if via else r, k],
+                at.peer(r),
+            ).start()
+
+    def relay_dx(dz):
+        for r, k in ((2, 0), (1, 1)):
+            rows = piece(dz, k)
+            wait_bytes(x_via.at[k, rows], v.r_dx.at[dz, 0, k])
+            x_out[r, rows] = (
+                x_out[r, rows].astype(F32) + x_via[k, rows].astype(F32)
+            ).astype(BF16)
+            remote(
+                x_out.at[r, rows],
+                x_in.at[r - 1, rows],
+                v.s_dx.at[0],
+                v.r_dx.at[dz, r, k],
+                at.peer(r),
+            ).start()
+
+    z_out, z_in = v.z_out, v.z_in
+    def column_dx(dz):
+        plane = (at.z + dz) % 4
+        rows = slot_rows(plane)
+        for r in (1, 2):
+            for k in range(2):
+                wait_bytes(x_in.at[r - 1, piece(dz, k)], v.r_dx.at[dz, r, k])
+        total = v.x_sum[rows] + x_in[0, rows].astype(F32) + x_in[1, rows].astype(F32)
+        if dz:
+            z_out[dz] = total.astype(BF16)
+            remote(
+                z_out.at[dz], z_in.at[dz], v.s_dz.at[0], v.r_dz.at[dz], (at.b, plane)
+            ).start()
+        else:
+            v.x_own[...] = total
+
+    def begin_dx(dz):
+        send_dx(dz, True)
+        send_dx(dz, False)
+
+    begin_dx(2)
+    begin_dx(1)
     def features(b):
         return contract_rows(xs[:, lanes(b)], dqkv[...])
 
     for r in range(4):
         v.w_sib_out[r] = features(2 * at.chip(r) + 1 - at.c)
         remote(
-            v.w_sib_out.at[r], v.w_sib_in.at[r], v.s_ws.at[r], v.r_ws.at[r], at.sibling()
+            v.w_sib_out.at[r], v.w_sib_in.at[r], v.s_ws.at[0], v.r_ws.at[r], at.sibling()
         ).start()
-    for dz in order:
-        send_dx(dz, False)
-        relay_dx(dz)
-    sum_in.relay(1, 0)
-    sum_back.finish(v.gs_back, v.fin_back, v.s_misc.at[7], v.r_misc.at[7])
+    relay_dx(2)
+    begin_dx(3)
+    sum_in.relay(1, 1)
+    sum_in.relay(2, 0)
+    relay_dx(1)
+    begin_dx(0)
+    column_dx(2)
+    relay_dx(3)
+    column_dx(1)
+    relay_dx(0)
     plane_w = 2 * (at.z // 2) + at.y
     for r in range(4):
         total = features(2 * at.chip(r) + at.c)
@@ -1415,7 +1461,9 @@
             plane_w == at.z if r == 0 else None,
         )
 
-    sum_in.relay(1, 1)
+    column_dx(3)
+    sum_back.finish(v.gs_back, v.fin_back, v.s_misc.at[7], v.r_misc.at[7])
+    sum_in.finish(v.gs_in, v.fin_in, v.s_misc.at[9], v.r_misc.at[9])
     wait_bytes(v.notes_p, v.r_misc.at[5])
     total = v.notes_p[0]
     for b in range(1, 8):
@@ -1428,31 +1476,15 @@
             v.notes_sum, mine, v.s_misc.at[11], v.r_misc.at[11], (at.b, (at.z + dz) % 4)
         ).start()
 
-    z_out, z_in = v.z_out, v.z_in
-    for dz in order:
-        plane = (at.z + dz) % 4
-        rows = slot_rows(plane)
-        for r in (1, 2):
-            for k in range(2):
-                wait_bytes(x_in.at[r - 1, piece(dz, k)], v.r_dx.at[dz, r, k])
-        total = v.x_sum[rows] + x_in[0, rows].astype(F32) + x_in[1, rows].astype(F32)
-        if dz:
-            z_out[dz] = total.astype(BF16)
-            remote(
-                z_out.at[dz], z_in.at[dz], v.s_dz.at[dz], v.r_dz.at[dz], (at.b, plane)
-            ).start()
-        else:
-            v.x_own[...] = total
-        if dz == 1:
-            sum_in.relay(2, 0)
-    sum_in.finish(v.gs_in, v.fin_in, v.s_misc.at[9], v.r_misc.at[9])
+    column_dx(0)
     for dz in (1, 2, 3):
         wait_bytes(z_in.at[dz], v.r_dz.at[dz])
     same = slot_rows(parity)
-    v.gtok[same] = (v.d1[same] + v.x_own[...] + z_in[2].astype(F32)).astype(BF16)
+    v.gtok_here[same] = (v.d1[same] + v.x_own[...] + z_in[2].astype(F32)).astype(BF16)
     cross = slot_rows(1 - parity)
-    v.gtok[cross] = (v.d1[cross] + z_in[1].astype(F32) + z_in[3].astype(F32)).astype(BF16)
-
+    v.gtok_here[cross] = (v.d1[cross] + z_in[1].astype(F32) + z_in[3].astype(F32)).astype(BF16)
+
+    pltpu.make_async_copy(v.gtok_here, v.gtok, v.r_own.at[3]).start()
     wait_bytes(v.o_in, v.r_misc.at[8])
     wait_bytes(v.w_in, v.r_misc.at[6])
     wait_bytes(v.notes_in, v.r_misc.at[11])
@@ -1460,16 +1492,25 @@
     wait_bytes(v.fin_in, v.r_misc.at[9])
 
 
-def end_phase(at, v, col_in, col_back, ends):
+def end_phase(at, v, ends):
+    wait_bytes(v.out_here, v.r_own.at[2])
     for one in ends:
         one.end()
-    slot = v.xs.at[slot_rows(0)]
-    for dz in range(1, 4):
-        wait_bytes(slot, v.s_z.at[dz])
-    for dz in range(4):
-        for r in range(3):
-            for k in range(2):
-                wait_bytes(v.grad_slots.at[0, pl.ds(0, 32)], v.s_dx.at[dz, r, k])
+
+    def rows(n):
+        return v.xs.at[pl.ds(0, n)]
+
+    wait_bytes(rows(192), v.s_z.at[0])
+    wait_bytes(rows(768), v.s_p.at[0])
+    wait_bytes(rows(384), v.s_wo.at[0])
+    wait_bytes(rows(608), v.s_o.at[0])
+    wait_bytes(rows(256), v.s_kv.at[0])
+    for i in (1, 2):
+        wait_bytes(rows(896), v.s_ex.at[i])
+    wait_bytes(rows(768), v.s_dx.at[0])
+    wait_bytes(rows(192), v.s_dz.at[0])
+    wait_bytes(v.w_sib_out, v.s_ws.at[0])
+    wait_bytes(rows(512), v.s_kv2.at[0])
     wait_bytes(v.wqkv.at[pl.ds(0, 384)], v.s_w.at[0])
     wait_bytes(v.wqkv.at[pl.ds(0, 512)], v.s_w.at[1])
     wait_bytes(v.w_near, v.s_w.at[2])
@@ -1478,24 +1519,10 @@
         wait_bytes(seven, v.s_misc.at[i])
     wait_bytes(v.smalls.at[pl.ds(0, 3)], v.s_misc.at[1])
     wait_bytes(v.smalls.at[pl.ds(0, 7)], v.s_misc.at[10])
-    wait_bytes(v.wo.at[pl.ds(0, 768), pl.ds(0, 128)], v.s_o.at[4])
-    for r in range(4):
-        wait_bytes(v.wo.at[:, pl.ds(0, 128)], v.s_o.at[r])
-    for r in range(4):
-        for k in range(2):
-            wait_bytes(v.keys_all.at[pl.ds(0, 256)], v.s_kv.at[k, r])
     for i in (3, 4):
         wait_bytes(v.att_send.at[pl.ds(0, 960)], v.s_misc.at[i])
-    col_in.end()
-    col_back.end()
-    for dz in (1, 2, 3):
-        wait_bytes(v.z_out.at[dz], v.s_dz.at[dz])
-    for k in range(2):
-        wait_bytes(v.sib_k, v.s_kv2.at[k])
     wait_bytes(v.notes.at[pl.ds(0, 7)], v.s_misc.at[5])
     wait_bytes(v.notes.at[pl.ds(0, 3)], v.s_misc.at[11])
-    for r in range(4):
-        wait_bytes(v.w_sib_out.at[r], v.s_ws.at[r])
     plane_w = 2 * (at.z // 2) + at.y
 
     @pl.when(plane_w == at.z)
@@ -1507,6 +1534,7 @@
         wait_bytes(v.w_out, v.s_misc.at[6])
 
     wait_bytes(v.o_in.at[pl.ds(0, 3)], v.s_misc.at[8])
+    wait_bytes(v.gtok_here, v.r_own.at[3])
 
 
 def finish_kernel(
@@ -1558,13 +1586,13 @@
 def run_layer(*args):
     results = [e for _, e in entries(Results)]
     scratch = [pltpu.VMEM(s, t) for _, (s, t) in entries(Scratch)]
-    for _, shape in entries(Semaphores):
-        scratch += [DMA(shape), DMA(shape)]
+    for _, shape in entries(Arrivals) + entries(Departures):
+        scratch.append(DMA(shape))
     return pl.pallas_call(
         layer_kernel,
         out_shape=[jax.ShapeDtypeStruct(s, t) for s, t in results],
-        in_specs=[vmem()] * len(args),
-        out_specs=[vmem()] * len(results),
+        in_specs=[vmem()] + [pl.BlockSpec(memory_space=pl.ANY)] * (len(args) - 1),
+        out_specs=[pl.BlockSpec(memory_space=pl.ANY)] * len(results),
         scratch_shapes=scratch,
         compiler_params=pltpu.CompilerParams(
             collective_id=1, has_side_effects=True, vmem_limit_bytes=VMEM_LIMIT
@@ -1633,7 +1661,7 @@
     )
     small = jnp.concatenate((spread, units), axis=0)
     results = run_layer(
-        x, w_query, w_key, w_value, w_out, small, w_in, w_back, cotangent.reshape(-1, model_dim)
+        small, x, cotangent.reshape(-1, model_dim), w_query, w_key, w_value, w_out, w_in, w_back
     )
     output, grad_tokens, gq, gk, gv, gout, gw_in, gw_back, own, gb_in = run_finish(
         head_id.astype(jnp.int32).reshape(1), *results

time: 184 us -> 175 us (0.951)
  Pallas kernels: 180 us -> 171 us
    pallas_call x1, Pallas kernels: 177 us -> 168 us  [run_layer(): pl.pallas_call(layer_kernel, out_shape=[jax.ShapeDtypeStruct(s, t) for s,...]
where the time goes in v5:
time: 175 us
  Pallas kernels  171 us (98%)
  local copies, waits for them, and re-layouts  2.58 us (1%)
    pallas_call x1, Pallas kernels, run_layer(): pl.pallas_call(layer_kernel, out_shape=[jax.ShapeDtypeStruct(s, t) for s,...  168 us

profile of v5, /device:TPU:0, one launch (start us, length us, event | category | flops | bytes accessed | tf_op | source)
XLA Modules:
  0.0 175.0 jit_solution(11028202065883941629)
XLA Ops:
  0.7 0.0 copy-start.8
  0.7 0.0 copy-start.4
  0.7 0.0 copy-start.5
  0.7 0.0 copy-start.6
  0.7 0.0 copy-start.7
  0.7 0.0 copy-start.1
  0.7 0.0 copy-start.2
  0.7 0.0 copy-start.3
  0.8 0.5 copy-done.8
  1.3 0.0 copy-done.4
  1.3 0.0 copy-done.5
  1.3 0.0 copy-done.6
  1.4 0.0 copy-done.7
  1.4 0.0 copy-done.1
  1.4 0.0 copy-done.2
  1.4 0.0 copy-done.3
  1.5 0.0 copy-start.9
  1.5 0.1 tile.10
  1.6 0.6 copy-done.9
  2.1 0.1 broadcast_select_fusion
  2.2 0.6 pad_maximum_fusion.refs_0_
  2.8 168.2 %shard_map.296 = (bf16[128,1024]{1,0:T(8,128)(2,1)}, bf16[128,1024]{1,0:T(8,128)(2,1)}, bf16[2,2,128,384]{3,2,1,0:T(8,128)(2,1)}, bf16[4,128,256]{2,1,0:T(8,128)...) custom-call(bf16[16,128]{1,0:T(8,128)(2,1)} %pad_maximum_fusion.refs_0_, ...), custom_call_target="tpu_custom_call" | custom-call | tf_op jit(solution)/shard_map/pallas_call | solution.py:1591
  171.0 2.8 %shard_map.297 = (bf16[128,1024]{1,0:T(8,128)(2,1)}, bf16[128,1024]{1,0:T(8,128)(2,1)}, f32[128,256]{1,0:T(8,128)}, f32[128,256]{1,0:T(8,128)}, f32[128,256]{1,0...) custom-call(s32[1]{0:T(128)} %bitcast.place_ref, ...), custom_call_target="tpu_custom_call" | custom-call | tf_op jit(solution)/shard_map/pallas_call | solution.py:1616
  173.8 0.0 copy-start
  173.8 0.7 copy-done
  174.5 0.5 slice_bitcast_fusion
  (4 shorter events, 0.1 us)
Async XLA Ops:
  0.7 0.7 copy-start.8
  0.7 0.7 copy-start.4
  0.7 0.7 copy-start.5
  0.7 0.7 copy-start.6
  0.7 0.7 copy-start.7
  0.7 0.7 copy-start.1
  0.7 0.7 copy-start.2
  0.7 0.7 copy-start.3
  1.5 0.7 copy-start.9
  173.8 0.7 copy-start

commit v6 on v5

--- a/solution.py
+++ b/solution.py
@@ -489,12 +489,12 @@
 
 
 class Column:
-    def __init__(self, at, ref, sems):
-        self.at, self.ref = at, ref
+    def __init__(self, at, ref, rows, sems):
+        self.at, self.ref, self.rows = at, ref, rows
         self.up_send, self.up_recv, self.down_send, self.down_recv = sems
 
     def block(self, plane):
-        return self.ref.at[:, lanes(plane)]
+        return self.ref.at[self.rows, lanes(plane)]
 
     def sides(self, hop, act, arriving):
         z = self.at.z
@@ -672,6 +672,7 @@
 
 
 class Scratch:
+    small_here = ((16, 128), BF16)
     out_here = ((128, 1024), BF16)
     gtok_here = ((128, 1024), BF16)
     x = ((128, 1024), BF16)
@@ -756,7 +757,7 @@
     o = (5,)
     kv = (1,)
     misc = (12,)
-    col = (4, 3)
+    col = (6, 3)
     ga = (4, 3, 2)
     ga_sib = (4, 4)
     ex = (5, 4)
@@ -778,7 +779,7 @@
     o = (1,)
     kv = (1,)
     misc = (12,)
-    col = (4, 3)
+    col = (6, 3)
     ga = (2,)
     ex = (3,)
     zg = (2, 2, 3)
@@ -803,8 +804,12 @@
     at.place = at.q * 4 + at.z
     at.parity = at.z % 2
     at.pair = 4 * (at.z // 2) + at.q
-    col_in = Column(at, v.wi, [s.at[0] for s in (v.s_col, v.r_col)] + [s.at[1] for s in (v.s_col, v.r_col)])
-    col_back = Column(at, v.wb, [s.at[2] for s in (v.s_col, v.r_col)] + [s.at[3] for s in (v.s_col, v.r_col)])
+    def column(ref, rows, i):
+        sems = [t.at[2 * i + k] for k in range(2) for t in (v.s_col, v.r_col)]
+        return Column(at, ref, rows, sems)
+
+    col_in = column(v.wi, pl.ds(0, 1024), 0)
+    col_back = [column(v.wb, pl.ds(512 * k, 512), 1 + k) for k in range(2)]
     gathers = [
         [
             Gather(at, slots, h, v.s_ga.at[i], v.r_ga.at[2 * i + h], v.r_ga_sib.at[2 * i + h])
@@ -842,6 +847,7 @@
     )
     sum_in = ColumnSum(at, v.g_in, v.pass_in, v.s_zg.at[0], v.r_zg.at[0])
     sum_back = ColumnSum(at, v.g_back, v.pass_back, v.s_zg.at[1], v.r_zg.at[1])
+    place_small(at, v)
     pltpu.make_async_copy(v.x_hbm, v.x, v.r_own.at[0]).start()
     pltpu.make_async_copy(v.cot_hbm, v.cot, v.r_own.at[1]).start()
     greet_all(at)
@@ -849,17 +855,32 @@
     attend_phase(at, v, col_in, col_back, rows_spread, wo_spread)
     ffn_phase(at, v, col_in, col_back, gathers, scatters, sum_back, sum_in)
     grads_phase(at, v, out_scatter, sum_in, sum_back)
-    end_phase(at, v, (sum_in, sum_back, col_in, col_back))
+    end_phase(at, v, (sum_in, sum_back, col_in, *col_back))
+
+
+def place_small(at, v):
+    def iota(shape, axis):
+        return lax.broadcasted_iota(jnp.int32, shape, axis)
+
+    spread = jnp.where(
+        iota((8, 256), 1) // 32 == iota((8, 256), 0), v.small[0:1, 0:256], 0.0
+    ).astype(BF16)
+    lane = iota((256, 128), 1)
+    source = iota((256, 128), 0) % 32 + 32 * at.z
+    picked = jnp.where(lane == source, 1.0, 0.0).astype(BF16)
+    top = dot_nn(spread, picked)
+    units = jnp.where(iota((8, 128), 0) == at.z, v.small[0:1, 256:384], 0.0)
+    v.small_here[...] = jnp.concatenate((top, units), axis=0).astype(BF16)
 
 
 def attend_phase(at, v, col_in, col_back, rows_spread, wo_spread):
     xs, wqkv, wo = v.xs, v.wqkv, v.wo
     parity, pair = at.parity, at.pair
 
-    pltpu.make_async_copy(v.small, v.smalls_z.at[at.z], v.r_misc.at[1]).start()
+    pltpu.make_async_copy(v.small_here, v.smalls_z.at[at.z], v.r_misc.at[1]).start()
     for dz in range(1, 4):
         remote(
-            v.small,
+            v.small_here,
             v.smalls_z.at[at.z],
             v.s_misc.at[1],
             v.r_misc.at[1],
@@ -940,8 +961,6 @@
     for r in range(4):
         part = wqkv.at[lanes(2 * at.chip(r) + at.c)]
         remote(part, part, v.s_w.at[1], v.r_w.at[1], at.sibling()).start()
-    rows_spread[3].relay()
-
     wait_bytes(v.smalls, v.r_misc.at[10])
     for b in range(8):
         v.par[:, 128 * b : 128 * b + 128] = v.smalls[b].astype(F32)[0:8]
@@ -954,13 +973,7 @@
     bias_v = v.par[1:2, lanes(pair)]
     wait_bytes(wqkv.at[pl.ds(0, 512)], v.r_w.at[1])
 
-    whole = wo_spread.block(0)
-    wait_bytes(whole, v.r_o.at[4])
-    wo_spread.start()
-    remote(whole, whole, v.s_o.at[0], v.r_o.at[0], at.sibling()).start()
-    plane_weights(at, v.wback, v.wb, v.s_misc.at[2], v.r_misc.at[2])
-
-    for r in range(4):
+    def project(r):
         chip = at.chip(r)
         if r:
             for i in range(4):
@@ -974,6 +987,18 @@
         for k, ref in enumerate((v.keys_all, v.values_all)):
             view = ref.at[own_rows]
             remote(view, view, v.s_kv.at[0], v.r_kv.at[0], at.sibling()).start()
+
+    project(0)
+    rows_spread[3].relay()
+
+    whole = wo_spread.block(0)
+    wait_bytes(whole, v.r_o.at[4])
+    wo_spread.start()
+    remote(whole, whole, v.s_o.at[0], v.r_o.at[0], at.sibling()).start()
+    plane_weights(at, v.wback, v.wb, v.s_misc.at[2], v.r_misc.at[2])
+
+    for r in (1, 2, 3):
+        project(r)
 
     wait_bytes(v.keys_all, v.r_kv.at[0])
 
@@ -1024,7 +1049,8 @@
     lax.fori_loop(0, 4, attend, 0)
 
     wait_bytes(v.wb.at[:, pl.ds(0, 128)], v.r_misc.at[2])
-    col_back.send(0)
+    for half_back in col_back:
+        half_back.send(0)
     for r in (1, 2, 3):
         wo_spread.rest(r)
         part = wo_spread.block(r)
@@ -1082,24 +1108,29 @@
 
     neighbours(gathers[0][0])
     gathers[0][1].relay()
-    col_back.arrive(0)
-    col_back.send(1)
+    col_back[0].arrive(0)
+    col_back[0].send(1)
     col_in.arrive(2)
     hidden(0, 0)
     gathers[0][1].forward(1)
     gathers[0][1].forward(2)
+    col_back[1].arrive(0)
+    col_back[1].send(1)
     hidden(1, 0)
     hidden(0, 1)
     hidden(0, 2)
     gathers[0][0].forward(3)
     hidden(1, 1)
     gathers[0][1].forward(3)
-    col_back.arrive(1)
-    col_back.send(2)
     hidden(1, 2)
+    col_back[0].arrive(1)
+    col_back[0].send(2)
     hidden(0, 3)
     hidden(1, 3)
-    col_back.arrive(2)
+    col_back[1].arrive(1)
+    col_back[1].send(2)
+    for half_back in col_back:
+        half_back.arrive(2)
 
     def to_plane(scatter, done, h, r, product):
         terms[r, pl.ds(128 * h, 128)] = product
@@ -1554,8 +1585,8 @@
     gout_ref,
     gwin_ref,
     gwback_ref,
-    small_ref,
     bin_ref,
+    *vector_refs,
 ):
     out_ref[...] = out_in[...]
     gtok_ref[...] = gtok_in[...]
@@ -1575,8 +1606,9 @@
     for k in range(4):
         part += jnp.where(z == k, total[0:8, 32 * k : 32 * k + 32], 0.0)
         units += jnp.where(z == k, total[8 + k : 9 + k], 0.0)
-    small_ref[...] = part
-    bin_ref[...] = units
+    for j, ref in enumerate(vector_refs):
+        ref[...] = part[j]
+    bin_ref[...] = units[0]
 
 
 def vmem():
@@ -1610,9 +1642,8 @@
         ((256, 128), F32),
         ((128, 1024), F32),
         ((128, 1024), F32),
-        ((8, 32), F32),
-        ((1, 128), F32),
-    )
+        ((128,), F32),
+    ) + (((32,), F32),) * 8
     return pl.pallas_call(
         finish_kernel,
         out_shape=[jax.ShapeDtypeStruct(s, t) for s, t in shapes],
@@ -1648,22 +1679,22 @@
     token_shape = tokens.shape
     model_dim = tokens.shape[2]
     x = tokens.reshape(-1, model_dim)
-    vectors = jnp.stack(
-        (b_query, b_value, b_out, norm1_gain, norm1_shift, b_back, norm2_gain, norm2_shift)
-    )
-    spread = jnp.where(
-        lax.broadcasted_iota(jnp.int32, (1, 128), 1) // 32 == head_id,
-        jnp.tile(vectors, (1, 4)),
-        jnp.zeros((), BF16),
-    )
-    units = jnp.where(
-        lax.broadcasted_iota(jnp.int32, (8, 1), 0) == head_id, b_in[None], jnp.zeros((), BF16)
-    )
-    small = jnp.concatenate((spread, units), axis=0)
+    vectors = (
+        b_query,
+        b_value,
+        b_out,
+        norm1_gain,
+        norm1_shift,
+        b_back,
+        norm2_gain,
+        norm2_shift,
+        b_in,
+    )
+    small = jnp.concatenate(vectors).astype(F32).reshape(1, -1)
     results = run_layer(
         small, x, cotangent.reshape(-1, model_dim), w_query, w_key, w_value, w_out, w_in, w_back
     )
-    output, grad_tokens, gq, gk, gv, gout, gw_in, gw_back, own, gb_in = run_finish(
+    output, grad_tokens, gq, gk, gv, gout, gw_in, gw_back, gb_in, *own = run_finish(
         head_id.astype(jnp.int32).reshape(1), *results
     )
     return (
@@ -1680,7 +1711,7 @@
         own[4],
         gw_in,
         gw_back,
-        gb_in.reshape(-1),
+        gb_in,
         own[5],
         own[6],
         own[7],

time: 175 us -> 175 us (level)
  local copies, waits for them, and re-layouts: 2.58 us -> 0.81 us
where the time goes in v6:
time: 175 us
  Pallas kernels  172 us (98%)
    pallas_call x1, Pallas kernels, run_layer(): pl.pallas_call(layer_kernel, out_shape=[jax.ShapeDtypeStruct(s, t) for s,...  170 us

profile of v6, /device:TPU:0, one launch (start us, length us, event | category | flops | bytes accessed | tf_op | source)
XLA Modules:
  0.0 174.7 jit_solution(11001292515325727975)
XLA Ops:
  0.7 0.0 copy-start.7
  0.7 0.0 copy-start.8
  0.7 0.0 copy-start.3
  0.7 0.0 copy-start.4
  0.7 0.0 copy-start.5
  0.7 0.0 copy-start.6
  0.7 0.0 copy-start
  0.7 0.0 copy-start.1
  0.7 0.0 copy-start.2
  0.8 0.6 copy-done.7
  1.3 0.0 copy-done.8
  1.3 0.0 copy-done.3
  1.4 0.0 copy-done.4
  1.4 0.0 copy-done.5
  1.4 0.0 copy-done.6
  1.4 0.0 copy-done
  1.4 0.0 copy-done.1
  1.4 0.0 copy-done.2
  1.4 0.1 concatenate.37
  1.5 0.6 convert_element_type.10.refs_0_
  2.1 169.6 %shard_map.296 = (bf16[128,1024]{1,0:T(8,128)(2,1)}, bf16[128,1024]{1,0:T(8,128)(2,1)}, bf16[2,2,128,384]{3,2,1,0:T(8,128)(2,1)}, bf16[4,128,256]{2,1,0:T(8,128)...) custom-call(f32[1,384]{1,0:T(1,128)} %convert_element_type.10.refs_0_, ...), custom_call_target="tpu_custom_call" | custom-call | tf_op jit(solution)/shard_map/pallas_call | solution.py:1623
  171.8 2.8 %shard_map.297 = (bf16[128,1024]{1,0:T(8,128)(2,1)}, bf16[128,1024]{1,0:T(8,128)(2,1)}, f32[128,256]{1,0:T(8,128)}, f32[128,256]{1,0:T(8,128)}, f32[128,256]{1,0...) custom-call(s32[1]{0:T(128)} %bitcast.place_ref, ...), custom_call_target="tpu_custom_call" | custom-call | tf_op jit(solution)/shard_map/pallas_call | solution.py:1647
Async XLA Ops:
  0.7 0.7 copy-start.7
  0.7 0.7 copy-start.8
  0.7 0.7 copy-start.3
  0.7 0.7 copy-start.4
  0.7 0.7 copy-start.5
  0.7 0.7 copy-start.6
  0.7 0.7 copy-start
  0.7 0.7 copy-start.1
  0.7 0.7 copy-start.2

commit v7 on v6

--- a/solution.py
+++ b/solution.py
@@ -449,14 +449,34 @@
         total = mine + self.sib_in[r, self.rows].astype(F32)
         if r == 0:
             return total
-        held = self.out.at[r, self.rows]
-        held[...] = total.astype(BF16)
+        self.out[r, self.rows] = total.astype(BF16)
+        if r == 3:
+            for k in range(2):
+                self.pass_half(3, k, 3, self.recv.at[3 * k], k + 1)
+        else:
+            self.pass_half(r, r - 1, r, self.recv.at[r], r)
+
+    def half(self, k):
+        size = self.rows.size // 2
+        return pl.ds(self.rows.start + size * k, size)
+
+    def pass_half(self, r, k, slot, recv, peer):
+        rows = self.half(k)
         remote(
-            held, self.into.at[r, self.rows], self.send, self.recv.at[r], self.at.peer(r)
+            self.out.at[r, rows], self.into.at[slot, rows], self.send, recv, self.at.peer(peer)
         ).start()
 
+    def relay(self):
+        for k in range(2):
+            rows, r = self.half(k), 2 - k
+            wait_bytes(self.into.at[3, rows], self.recv.at[3 * k])
+            self.out[r, rows] = (
+                self.out[r, rows].astype(F32) + self.into[3, rows].astype(F32)
+            ).astype(BF16)
+            self.pass_half(r, k, r, self.recv.at[r], r)
+
     def arrive(self):
-        for r in (1, 2, 3):
+        for r in (1, 2):
             wait_bytes(self.into.at[r, self.rows], self.recv.at[r])
 
 
@@ -1151,13 +1171,11 @@
             to_plane(scatters[0], done, h, r, product)
     for one in done[-3:]:
         pass_on(scatters[0], *one)
+    for h in range(2):
+        scatters[0][h].relay()
 
     def peers(side, rows):
-        return (
-            peer_in[side, 1, rows].astype(F32)
-            + peer_in[side, 2, rows].astype(F32)
-            + peer_in[side, 3, rows].astype(F32)
-        )
+        return peer_in[side, 1, rows].astype(F32) + peer_in[side, 2, rows].astype(F32)
 
     def column_sums(parts, sums):
         return tuple(
@@ -1231,13 +1249,13 @@
     v.gbin[...] = jnp.sum(gbin[0], axis=0, keepdims=True)
 
     sums = tuple(jnp.zeros((8, 1024), F32) for _ in range(3))
+    weight_grad(v.grad_slots, v.hid, v.g_back)
+    wait_bytes(v.xs.at[pl.ds(0, 896)], v.s_ga.at[1])
+    sum_back.begin((0,))
+    scatters[1][0].relay()
+    weight_grad(v.norm_slots, v.low, v.g_in)
+    scatters[1][1].relay()
     for h in range(2):
-        if h == 0:
-            weight_grad(v.grad_slots, v.hid, v.g_back)
-            wait_bytes(v.xs.at[pl.ds(0, 896)], v.s_ga.at[1])
-            sum_back.begin((0,))
-        else:
-            weight_grad(v.norm_slots, v.low, v.g_in)
         scatters[1][h].arrive()
         for i in range(2):
             rows = local(h, i)
@@ -1323,6 +1341,7 @@
 
         @pl.when(step == 1)
         def _():
+            out_scatter.relay()
             sum_back.relay(1, 0)
 
         @pl.when(step == 2)
@@ -1347,12 +1366,7 @@
     peer_in = v.peer_in.at[0]
 
     def out_rows(rows):
-        total = (
-            terms[0, rows]
-            + peer_in[1, rows].astype(F32)
-            + peer_in[2, rows].astype(F32)
-            + peer_in[3, rows].astype(F32)
-        )
+        total = terms[0, rows] + peer_in[1, rows].astype(F32) + peer_in[2, rows].astype(F32)
         v.o_out[rows] = total.astype(BF16)
 
     by_rows(128, 32, out_rows)

time: 175 us -> 171 us (0.977)
  Pallas kernels: 172 us -> 168 us
    pallas_call x1, Pallas kernels: 170 us -> 165 us  [run_layer(): pl.pallas_call(layer_kernel, out_shape=[jax.ShapeDtypeStruct(s, t) for s,...]
where the time goes in v7:
time: 171 us; the launch traced here: 170 us
  Pallas kernels  168 us (98%)
    pallas_call x1, Pallas kernels, run_layer(): pl.pallas_call(layer_kernel, out_shape=[jax.ShapeDtypeStruct(s, t) for s,...  165 us

profile of v7, /device:TPU:0, one launch (start us, length us, event | category | flops | bytes accessed | tf_op | source)
XLA Modules:
  0.0 170.3 jit_solution(732327320982984324)
XLA Ops:
  0.7 0.0 copy-start.7
  0.7 0.0 copy-start.8
  0.7 0.0 copy-start.3
  0.7 0.0 copy-start.4
  0.7 0.0 copy-start.5
  0.7 0.0 copy-start.6
  0.7 0.0 copy-start
  0.7 0.0 copy-start.1
  0.7 0.0 copy-start.2
  0.8 0.6 copy-done.7
  1.3 0.0 copy-done.8
  1.3 0.0 copy-done.3
  1.4 0.0 copy-done.4
  1.4 0.0 copy-done.5
  1.4 0.0 copy-done.6
  1.4 0.0 copy-done
  1.4 0.0 copy-done.1
  1.4 0.0 copy-done.2
  1.4 0.1 concatenate.37
  1.5 0.6 convert_element_type.10.refs_0_
  2.1 165.2 %shard_map.296 = (bf16[128,1024]{1,0:T(8,128)(2,1)}, bf16[128,1024]{1,0:T(8,128)(2,1)}, bf16[2,2,128,384]{3,2,1,0:T(8,128)(2,1)}, bf16[4,128,256]{2,1,0:T(8,128)...) custom-call(f32[1,384]{1,0:T(1,128)} %convert_element_type.10.refs_0_, ...), custom_call_target="tpu_custom_call" | custom-call | tf_op jit(solution)/shard_map/pallas_call | solution.py:1637
  167.4 2.8 %shard_map.297 = (bf16[128,1024]{1,0:T(8,128)(2,1)}, bf16[128,1024]{1,0:T(8,128)(2,1)}, f32[128,256]{1,0:T(8,128)}, f32[128,256]{1,0:T(8,128)}, f32[128,256]{1,0...) custom-call(s32[1]{0:T(128)} %bitcast.place_ref, ...), custom_call_target="tpu_custom_call" | custom-call | tf_op jit(solution)/shard_map/pallas_call | solution.py:1661
Async XLA Ops:
  0.7 0.7 copy-start.7
  0.7 0.7 copy-start.8
  0.7 0.7 copy-start.3
  0.7 0.7 copy-start.4
  0.7 0.7 copy-start.5
  0.7 0.7 copy-start.6
  0.7 0.7 copy-start
  0.7 0.7 copy-start.1
  0.7 0.7 copy-start.2

commit v8 on v7

--- a/solution.py
+++ b/solution.py
@@ -972,10 +972,11 @@
             plane_weights(at, v.win, v.wi, v.s_misc.at[0], v.r_misc.at[0])
             wait_bytes(v.w_near, v.r_w.at[2])
             to_pairs([v.w_near.at[k] for k in range(3)], 1 - parity)
+        if i == 3:
+            wait_bytes(v.wi.at[:, pl.ds(0, 128)], v.r_misc.at[0])
+            col_in.send(0)
         if i:
             rows_spread[i - 1].relay()
-    wait_bytes(v.wi.at[:, pl.ds(0, 128)], v.r_misc.at[0])
-    col_in.send(0)
 
     wait_bytes(wqkv.at[pl.ds(0, 512)], v.r_w.at[0])
     for r in range(4):
@@ -1017,13 +1018,13 @@
     remote(whole, whole, v.s_o.at[0], v.r_o.at[0], at.sibling()).start()
     plane_weights(at, v.wback, v.wb, v.s_misc.at[2], v.r_misc.at[2])
 
+    col_in.arrive(0)
+    col_in.send(1)
     for r in (1, 2, 3):
         project(r)
 
     wait_bytes(v.keys_all, v.r_kv.at[0])
 
-    col_in.arrive(0)
-    col_in.send(1)
     scores = v.scores
 
     def attend(step, carry):
@@ -1058,9 +1059,6 @@
         @pl.when(step == 0)
         def _():
             wo_spread.relay()
-
-        @pl.when(step == 2)
-        def _():
             col_in.arrive(1)
             col_in.send(2)
 
@@ -1127,28 +1125,27 @@
         gather.forward(2)
 
     neighbours(gathers[0][0])
+    for half_back in col_back:
+        half_back.arrive(0)
+        half_back.send(1)
     gathers[0][1].relay()
-    col_back[0].arrive(0)
-    col_back[0].send(1)
     col_in.arrive(2)
     hidden(0, 0)
     gathers[0][1].forward(1)
     gathers[0][1].forward(2)
-    col_back[1].arrive(0)
-    col_back[1].send(1)
     hidden(1, 0)
     hidden(0, 1)
     hidden(0, 2)
+    col_back[0].arrive(1)
+    col_back[0].send(2)
     gathers[0][0].forward(3)
     hidden(1, 1)
     gathers[0][1].forward(3)
+    col_back[1].arrive(1)
+    col_back[1].send(2)
     hidden(1, 2)
-    col_back[0].arrive(1)
-    col_back[0].send(2)
     hidden(0, 3)
     hidden(1, 3)
-    col_back[1].arrive(1)
-    col_back[1].send(2)
     for half_back in col_back:
         half_back.arrive(2)
 
@@ -1309,6 +1306,7 @@
     for r in (3, 1, 2):
         out_scatter.add(r, terms[r, 0:128])
     terms[0, 0:128] = out_scatter.add(0, terms[0, 0:128])
+    sum_back.relay(1, 0)
     wait_bytes(v.da.at[chip_rows(at.q)], v.r_da.at[0])
     s_buf, d_buf, p_buf = v.scores, v.d_buf, v.p_buf
 
@@ -1342,11 +1340,12 @@
         @pl.when(step == 1)
         def _():
             out_scatter.relay()
-            sum_back.relay(1, 0)
-
-        @pl.when(step == 2)
+            sum_back.relay(2, 0)
+            sum_in.relay(1, 0)
+
+        @pl.when(step == 3)
         def _():
-            sum_in.relay(1, 0)
+            sum_back.relay(1, 1)
 
         return carry
 
@@ -1382,8 +1381,6 @@
             (at.b, plane),
         ).start()
 
-    sum_back.relay(1, 1)
-    sum_back.relay(2, 0)
     own_k = v.dk_turned[:, mine].T * HEAD_DIM**-0.5
     wait_bytes(v.sib_k, v.r_kv2.at[0])
     dqkv[:, 128:256] = (own_k + v.sib_k[...]).astype(BF16)
@@ -1492,6 +1489,7 @@
     relay_dx(3)
     column_dx(1)
     relay_dx(0)
+    column_dx(3)
     plane_w = 2 * (at.z // 2) + at.y
     for r in range(4):
         total = features(2 * at.chip(r) + at.c)
@@ -1506,7 +1504,6 @@
             plane_w == at.z if r == 0 else None,
         )
 
-    column_dx(3)
     sum_back.finish(v.gs_back, v.fin_back, v.s_misc.at[7], v.r_misc.at[7])
     sum_in.finish(v.gs_in, v.fin_in, v.s_misc.at[9], v.r_misc.at[9])
     wait_bytes(v.notes_p, v.r_misc.at[5])

time: 171 us -> 166 us (0.971)
  Pallas kernels: 168 us -> 163 us
    pallas_call x1, Pallas kernels: 165 us -> 160 us  [run_layer(): pl.pallas_call(layer_kernel, out_shape=[jax.ShapeDtypeStruct(s, t) for s,...]
where the time goes in v8:
time: 166 us; the launch traced here: 165 us
  Pallas kernels  163 us (98%)
    pallas_call x1, Pallas kernels, run_layer(): pl.pallas_call(layer_kernel, out_shape=[jax.ShapeDtypeStruct(s, t) for s,...  160 us

profile of v8, /device:TPU:0, one launch (start us, length us, event | category | flops | bytes accessed | tf_op | source)
XLA Modules:
  0.0 165.4 jit_solution(11990490450665163776)
XLA Ops:
  0.7 0.0 copy-start.7
  0.7 0.0 copy-start.8
  0.7 0.0 copy-start.3
  0.7 0.0 copy-start.4
  0.7 0.0 copy-start.5
  0.7 0.0 copy-start.6
  0.7 0.0 copy-start
  0.7 0.0 copy-start.1
  0.7 0.0 copy-start.2
  0.8 0.6 copy-done.7
  1.3 0.0 copy-done.8
  1.3 0.0 copy-done.3
  1.4 0.0 copy-done.4
  1.4 0.0 copy-done.5
  1.4 0.0 copy-done.6
  1.4 0.0 copy-done
  1.4 0.0 copy-done.1
  1.4 0.0 copy-done.2
  1.4 0.1 concatenate.37
  1.5 0.6 convert_element_type.10.refs_0_
  2.1 160.3 %shard_map.296 = (bf16[128,1024]{1,0:T(8,128)(2,1)}, bf16[128,1024]{1,0:T(8,128)(2,1)}, bf16[2,2,128,384]{3,2,1,0:T(8,128)(2,1)}, bf16[4,128,256]{2,1,0:T(8,128)...) custom-call(f32[1,384]{1,0:T(1,128)} %convert_element_type.10.refs_0_, ...), custom_call_target="tpu_custom_call" | custom-call | tf_op jit(solution)/shard_map/pallas_call | solution.py:1634
  162.4 2.8 %shard_map.297 = (bf16[128,1024]{1,0:T(8,128)(2,1)}, bf16[128,1024]{1,0:T(8,128)(2,1)}, f32[128,256]{1,0:T(8,128)}, f32[128,256]{1,0:T(8,128)}, f32[128,256]{1,0...) custom-call(s32[1]{0:T(128)} %bitcast.place_ref, ...), custom_call_target="tpu_custom_call" | custom-call | tf_op jit(solution)/shard_map/pallas_call | solution.py:1658
Async XLA Ops:
  0.7 0.7 copy-start.7
  0.7 0.7 copy-start.8
  0.7 0.7 copy-start.3
  0.7 0.7 copy-start.4
  0.7 0.7 copy-start.5
  0.7 0.7 copy-start.6
  0.7 0.7 copy-start
  0.7 0.7 copy-start.1
  0.7 0.7 copy-start.2

commit v9 on v8

--- a/solution.py
+++ b/solution.py
@@ -1486,10 +1486,6 @@
     relay_dx(1)
     begin_dx(0)
     column_dx(2)
-    relay_dx(3)
-    column_dx(1)
-    relay_dx(0)
-    column_dx(3)
     plane_w = 2 * (at.z // 2) + at.y
     for r in range(4):
         total = features(2 * at.chip(r) + at.c)
@@ -1504,8 +1500,12 @@
             plane_w == at.z if r == 0 else None,
         )
 
+    relay_dx(3)
     sum_back.finish(v.gs_back, v.fin_back, v.s_misc.at[7], v.r_misc.at[7])
+    column_dx(1)
+    relay_dx(0)
     sum_in.finish(v.gs_in, v.fin_in, v.s_misc.at[9], v.r_misc.at[9])
+    column_dx(3)
     wait_bytes(v.notes_p, v.r_misc.at[5])
     total = v.notes_p[0]
     for b in range(1, 8):

time: 166 us -> 165 us (level)
  no operation moved by 1% of the time
where the time goes in v9:
time: 165 us
  Pallas kernels  163 us (99%)
    pallas_call x1, Pallas kernels, run_layer(): pl.pallas_call(layer_kernel, out_shape=[jax.ShapeDtypeStruct(s, t) for s,...  160 us

profile of v9, /device:TPU:0, one launch (start us, length us, event | category | flops | bytes accessed | tf_op | source)
XLA Modules:
  0.0 165.3 jit_solution(15544485477233939837)
XLA Ops:
  0.7 0.0 copy-start.7
  0.7 0.0 copy-start.8
  0.7 0.0 copy-start.3
  0.7 0.0 copy-start.4
  0.7 0.0 copy-start.5
  0.7 0.0 copy-start.6
  0.7 0.0 copy-start
  0.7 0.0 copy-start.1
  0.7 0.0 copy-start.2
  0.8 0.6 copy-done.7
  1.3 0.0 copy-done.8
  1.3 0.0 copy-done.3
  1.4 0.0 copy-done.4
  1.4 0.0 copy-done.5
  1.4 0.0 copy-done.6
  1.4 0.0 copy-done
  1.4 0.0 copy-done.1
  1.4 0.0 copy-done.2
  1.4 0.1 concatenate.37
  1.5 0.6 convert_element_type.10.refs_0_
  2.1 160.2 %shard_map.296 = (bf16[128,1024]{1,0:T(8,128)(2,1)}, bf16[128,1024]{1,0:T(8,128)(2,1)}, bf16[2,2,128,384]{3,2,1,0:T(8,128)(2,1)}, bf16[4,128,256]{2,1,0:T(8,128)...) custom-call(f32[1,384]{1,0:T(1,128)} %convert_element_type.10.refs_0_, ...), custom_call_target="tpu_custom_call" | custom-call | tf_op jit(solution)/shard_map/pallas_call | solution.py:1634
  162.3 2.8 %shard_map.297 = (bf16[128,1024]{1,0:T(8,128)(2,1)}, bf16[128,1024]{1,0:T(8,128)(2,1)}, f32[128,256]{1,0:T(8,128)}, f32[128,256]{1,0:T(8,128)}, f32[128,256]{1,0...) custom-call(s32[1]{0:T(128)} %bitcast.place_ref, ...), custom_call_target="tpu_custom_call" | custom-call | tf_op jit(solution)/shard_map/pallas_call | solution.py:1658
Async XLA Ops:
  0.7 0.7 copy-start.7
  0.7 0.7 copy-start.8
  0.7 0.7 copy-start.3
  0.7 0.7 copy-start.4
  0.7 0.7 copy-start.5
  0.7 0.7 copy-start.6
  0.7 0.7 copy-start
  0.7 0.7 copy-start.1
  0.7 0.7 copy-start.2
